TPU v7x, 32 devices: a whole 2x2x4 slice. The times are simulated.
32 devices in a mesh: groups: 2 (over y), ctx: 8 (over z, x), tp: 2 (over core).
Axes of the slice: x: 2, y: 2, z: 4, core: 2. Of those that a mesh axis runs over, the one named last changes fastest.
Arguments:
- queries: bfloat16 [256, 64, 192], P(('groups', 'ctx'), 'tp'), parts along dimension 0, may hold values from -30 to 30
- latent_cache: bfloat16 [4096, 576], P(('groups', 'ctx')), parts along dimension 0, may hold values from -6 to 6
- kv_weight: bfloat16 [512, 64, 256], P('ctx', 'tp'), may hold values from -0.25 to 0.25
- block_order: int32 [16], P('groups'), parts along dimension 0, may hold values from 0 to 7, as said below
- span_start: int32 [2], P('groups'), parts along dimension 0, may hold values from 1024 to 1920
Outputs:
- attended: bfloat16 [256, 64, 128], P(('groups', 'ctx'), 'tp'), parts along dimension 0
There are 2 independent parts, one for each index of `groups`. A program takes and returns all parts, laid end to end along the dimension named above; an argument that names none is the same for every part. Nothing has to cross between parts.
Inputs may be any that keep to these rules, and one draw needn't show every extreme that they name: `block_order`: A permutation: every block of the prompt is stored by exactly one shard.
All inputs are finite; a program needn't handle non-finite values.
Results may differ from a plain program's by a relative error of at most 0.015.
Values may be sent and summed in bfloat16 or wider, within the bound.
No kernel may reach another device: no remote copies, remote signals or barrier semaphores. Data moves between devices by JAX's collectives and lax.ppermute only.
A program may use at most 64 MiB of HBM per device.

v0:
```python
import math

import jax
import jax.numpy as jnp
from jax import lax
from jax.sharding import PartitionSpec as P

LAT = 512
ROPE = 64
NOPE = 128
VD = 128


def tile_update(running, tile_rows, tile_positions, gathered_queries, weight_matrix, query_last):
    row_max, row_total, accum = running
    softmax_scale = 1.0 / math.sqrt(NOPE + ROPE)
    head_count = gathered_queries.shape[1]
    latent = tile_rows[:, :LAT]
    rope_part = tile_rows[:, LAT:]
    key_value = jnp.dot(latent, weight_matrix, preferred_element_type=jnp.float32).astype(
        jnp.bfloat16
    )
    key_value = key_value.reshape(tile_rows.shape[0], head_count, NOPE + VD)
    scores = jnp.einsum(
        "qhc,khc->hqk",
        gathered_queries[:, :, :NOPE],
        key_value[:, :, :NOPE],
        preferred_element_type=jnp.float32,
    )
    scores = scores + jnp.einsum(
        "qhr,kr->hqk", gathered_queries[:, :, NOPE:], rope_part, preferred_element_type=jnp.float32
    )
    scores = scores * softmax_scale
    visible = (tile_positions[None, :] <= query_last[:, None])[None]
    scores = jnp.where(visible, scores, jnp.float32(-1e30))
    new_max = jnp.maximum(row_max, jnp.max(scores, axis=2))
    weights = jnp.where(visible, jnp.exp(scores - new_max[:, :, None]), jnp.float32(0.0))
    row_total = jnp.sum(weights, axis=2)
    accum = jnp.einsum(
        "hqk,khv->hqv",
        weights.astype(jnp.bfloat16),
        key_value[:, :, NOPE:],
        preferred_element_type=jnp.float32,
    )
    return (new_max, row_total, accum)


def local(queries, latent_cache, kv_weight, block_order, span_start):
    shard_index = lax.axis_index("ctx")
    gathered_queries = lax.all_gather(queries, "ctx", axis=0, tiled=True)
    full_weight = lax.all_gather(kv_weight, "ctx", axis=0, tiled=True)
    head_count = full_weight.shape[1]
    weight_matrix = full_weight.reshape(LAT, head_count * (NOPE + VD))
    row_count = latent_cache.shape[0]
    own_block = lax.dynamic_index_in_dim(block_order, shard_index, 0, keepdims=False)
    key_positions = own_block * row_count + jnp.arange(row_count, dtype=jnp.int32)
    query_count = gathered_queries.shape[0]
    query_last = span_start[0] + jnp.arange(query_count, dtype=jnp.int32)
    final_position = span_start[0] + query_count - 1
    running = (
        jnp.full((head_count, query_count), -1e30, jnp.float32),
        jnp.zeros((head_count, query_count), jnp.float32),
        jnp.zeros((head_count, query_count, VD), jnp.float32),
    )
    running = lax.cond(
        key_positions[0] <= final_position,
        lambda current, rows_now=latent_cache, places=key_positions: tile_update(
            current, rows_now, places, gathered_queries, weight_matrix, query_last
        ),
        lambda current: current,
        running,
    )
    row_max, row_total, accum = running
    parts_accum, parts_max, parts_total = (
        lax.all_to_all(
            accum[:, :, None, :].astype(jnp.bfloat16),
            "ctx",
            split_axis=1,
            concat_axis=2,
            tiled=True,
        ).astype(jnp.float32),
        lax.all_to_all(
            row_max[:, :, None].astype(jnp.bfloat16), "ctx", split_axis=1, concat_axis=2, tiled=True
        ).astype(jnp.float32),
        lax.all_to_all(
            row_total[:, :, None].astype(jnp.bfloat16),
            "ctx",
            split_axis=1,
            concat_axis=2,
            tiled=True,
        ).astype(jnp.float32),
    )
    overall = jnp.max(parts_max, axis=2, keepdims=True)
    factor = jnp.exp(parts_max - overall)
    denominator = jnp.sum(factor * parts_total, axis=2)
    numerator = jnp.sum(factor[:, :, :, None] * parts_accum, axis=2)
    result = (numerator / denominator[:, :, None]).astype(jnp.bfloat16)
    return jnp.transpose(result, (1, 0, 2))


def solution(mesh):
    return jax.shard_map(
        local,
        mesh=mesh,
        in_specs=(
            P(("groups", "ctx"), "tp", None),
            P(("groups", "ctx"), None),
            P("ctx", "tp", None),
            P("groups"),
            P("groups"),
        ),
        out_specs=P(("groups", "ctx"), "tp", None),
        check_vma=False,
    )
```

profile of v0, /device:TPU:0, one launch (start us, length us, event | category | flops | bytes accessed | tf_op | source)
XLA Modules:
  0.0 287.6 jit_solution(9518662600967891308)
XLA Ops:
  6.5 0.0 all-gather.5.cloned.1.call-start
  6.5 1.8 copy.48
  8.3 0.0 all-gather.5.cloned.1.call-update
  8.4 0.0 all-gather.3.cloned.1.call-start
  8.4 0.7 all-gather.3.cloned.1.call-update
  9.1 1.2 dynamic_slice.4
  11.0 0.5 slice.21
  12.8 50.4 %all-gather.5.cloned.1.call-done = bf16[128,32,192]{2,0,1:T(8,128)(2,1)} async-done(((bf16[16,32,192]{2,0,1:T(8,128)(2,1)}), bf16[128,32,192]{2,0,1:T(8,128)(2,1)}) %all-gather.5.cloned.1.call-update) | async-done | bytes 1572880 | tf_op jit(solution)/shard_map/all_gather | solution.py:50
  63.2 125.3 %all-gather.3.cloned.1.call-done = bf16[512,32,256]{2,1,0:T(8,128)(2,1)} async-done(((bf16[64,32,256]{2,1,0:T(8,128)(2,1)}), bf16[512,32,256]{2,1,0:T(8,128)(2,1)}) %all-gather.3.cloned.1.call-update) | async-done | bytes 8388624 | tf_op jit(solution)/shard_map/all_gather | solution.py:51
  188.5 39.2 %conditional.1 = (f32[32,128]{1,0:T(8,128)}, bf16[32,128]{1,0:T(8,128)(2,1)S(1)}, bf16[32,128,128]{2,1,0:T(8,128)(2,1)S(1)}) conditional(s32[]{:T(128)} %convert_element_type.64, () %tuple.13, (s32[256]{0:T(256)S(1)}, s32[]{:T(128)}, bf16[256,576]{0,1:T(8,128)(2,1)}, bf16[512,32,256]{2,1,0:T(8,128)(2,1)}, bf16[128,32,192]{2,0,1:T(8,128)(2,1)}, ...), branch_computations={%region_0.1_spmd, %region_1.4_spmd} | conditional | flops 2831183872 | bytes 93448816 | solution.py:65
  188.5 16.5 %copy.61 = bf16[64,8,32,256]{3,1,2,0:T(8,128)(2,1)} copy(bf16[64,8,32,256]{3,2,1,0:T(8,128)(2,1)} %bitcast.70) | data formatting | bytes 16777216 | tf_op jit(solution)/shard_map/cond
  205.0 0.0 copy-done.2
  205.0 6.0 %convolution_convert_fusion = bf16[256,8192]{1,0:T(8,128)(2,1)S(1)} fusion(bf16[512,8192]{1,0:T(8,128)(2,1)} %bitcast.67, bf16[256,576]{0,1:T(8,128)(2,1)S(1)} %copy-done.2), kind=kOutput, calls=%fused_computation | convolution fusion | flops 2149580800 | bytes 12845056 | tf_op jit(solution)/shard_map/cond/branch_1_fun/dot_general | solution.py:20
  210.9 1.4 copy.62
  212.3 2.1 fusion.27
  214.5 3.9 %copy.45 = bf16[128,32,192]{0,2,1:T(8,128)(2,1)} copy(bf16[128,32,192]{2,0,1:T(8,128)(2,1)} %get-tuple-element.19) | data formatting | bytes 3145728 | tf_op jit(solution)/shard_map
  218.4 1.9 fusion.12
  220.3 0.7 broadcast_add_fusion
  221.0 0.1 broadcast_compare_fusion
  221.1 0.0 copy-done
  221.1 0.0 copy-start.1
  221.1 1.7 fusion.28
  222.8 0.6 broadcast_maximum_fusion
  223.4 2.5 fusion.4
  225.9 1.5 fusion.3
  227.7 0.7 convert_bitcast_fusion.2
  228.4 0.1 copy.49
  228.5 0.6 broadcast.29
  229.1 0.9 reduce.2
  230.0 0.7 reshape.63
  230.7 3.3 %all-to-all-start = ((bf16[8,2,256]{2,1,0:T(2,128)(2,1)}), bf16[8,2,256]{2,1,0:T(2,128)(2,1)S(1)}, u32[]{:S(2)}, u32[]{:S(2)}) async-start(bf16[8,2,256]{2,1,0:T(2,128)(2,1)} %reshape.63), calls=%async_computation | async-start | bytes 16384 | tf_op jit(solution)/shard_map/all_to_all | solution.py:82
  234.0 0.1 copy.53
  234.1 0.9 reduce.3
  235.0 0.7 reshape.65
  235.7 4.8 %all-to-all-done = bf16[8,2,256]{2,1,0:T(2,128)(2,1)S(1)} async-done(((bf16[8,2,256]{2,1,0:T(2,128)(2,1)}), bf16[8,2,256]{2,1,0:T(2,128)(2,1)S(1)}, u32[]{:S(2)}, u32[]{:S(2)}) %all-to-all-start) | async-done | bytes 8224 | tf_op jit(solution)/shard_map/all_to_all | solution.py:82
  240.5 3.3 %all-to-all-start.2 = ((bf16[8,2,256]{2,1,0:T(2,128)(2,1)}), bf16[8,2,256]{2,1,0:T(2,128)(2,1)S(1)}, u32[]{:S(2)}, u32[]{:S(2)}) async-start(bf16[8,2,256]{2,1,0:T(2,128)(2,1)} %reshape.65), calls=%async_computation.2 | async-start | bytes 16384 | tf_op jit(solution)/shard_map/all_to_all | solution.py:85
  243.8 1.7 copy.74
  245.5 4.8 %all-to-all-done.2 = bf16[8,2,256]{2,1,0:T(2,128)(2,1)S(1)} async-done(((bf16[8,2,256]{2,1,0:T(2,128)(2,1)}), bf16[8,2,256]{2,1,0:T(2,128)(2,1)S(1)}, u32[]{:S(2)}, u32[]{:S(2)}) %all-to-all-start.2) | async-done | bytes 8224 | tf_op jit(solution)/shard_map/all_to_all | solution.py:85
  250.3 3.6 %all-to-all-start.1 = ((bf16[32,128,1,128]{3,0,2,1:T(8,128)(2,1)}), bf16[32,128,1,128]{3,0,2,1:T(8,128)(2,1)S(1)}, u32[]{:S(2)}, u32[]{:S(2)}) async-start(bf16[32,128,1,128]{3,0,2,1:T(8,128)(2,1)} %bitcast.65), calls=%async_computation.1 | async-start | bytes 2097152 | tf_op jit(solution)/shard_map/all_to_all | solution.py:75
  253.8 0.1 reshape.64
  254.0 0.1 reshape.66
  254.1 0.1 copy.55
  254.2 0.1 copy.50
  254.3 22.9 %all-to-all-done.1 = bf16[32,128,1,128]{3,0,2,1:T(8,128)(2,1)S(1)} async-done(((bf16[32,128,1,128]{3,0,2,1:T(8,128)(2,1)}), bf16[32,128,1,128]{3,0,2,1:T(8,128)(2,1)S(1)}, u32[]{:S(2)}, u32[]{:S(2)}) %all-to-all-start.1) | async-done | bytes 1048608 | tf_op jit(solution)/shard_map/all_to_all | solution.py:75
  277.3 0.3 convert.13
  277.5 2.4 fusion.18
  279.9 0.1 fusion.20
  280.1 0.7 copy.56
  (11 shorter events, 0.1 us)
Async XLA Ops:
  6.5 56.7 %all-gather.5.cloned.1.call-start = ((), (), s32[]{:S(2)}) async-start(), calls=%async_computation.4 | async-start | bytes 2359296 | tf_op jit(solution)/shard_map/all_gather | solution.py:50
  8.4 180.1 %all-gather.3.cloned.1.call-start = ((), (), s32[]{:S(2)}) async-start(), calls=%async_computation.3 | async-start | bytes 9437184 | tf_op jit(solution)/shard_map/all_gather | solution.py:51
  188.5 16.5 %copy-start.2 = (bf16[256,576]{0,1:T(8,128)(2,1)S(1)}, bf16[256,576]{0,1:T(8,128)(2,1)}, u32[]{:S(2)}) copy-start(bf16[256,576]{0,1:T(8,128)(2,1)} %get-tuple-element.31) | copy-start | bytes 884740 | tf_op jit(solution)/shard_map/cond
  218.4 2.7 copy-start
  221.1 2.3 copy-start.1
  230.7 9.8 %all-to-all-start = ((bf16[8,2,256]{2,1,0:T(2,128)(2,1)}), bf16[8,2,256]{2,1,0:T(2,128)(2,1)S(1)}, u32[]{:S(2)}, u32[]{:S(2)}) async-start(bf16[8,2,256]{2,1,0:T(2,128)(2,1)} %reshape.63), calls=%async_computation | async-start | bytes 16384 | tf_op jit(solution)/shard_map/all_to_all | solution.py:82
  240.5 9.8 %all-to-all-start.2 = ((bf16[8,2,256]{2,1,0:T(2,128)(2,1)}), bf16[8,2,256]{2,1,0:T(2,128)(2,1)S(1)}, u32[]{:S(2)}, u32[]{:S(2)}) async-start(bf16[8,2,256]{2,1,0:T(2,128)(2,1)} %reshape.65), calls=%async_computation.2 | async-start | bytes 16384 | tf_op jit(solution)/shard_map/all_to_all | solution.py:85
  250.3 27.0 %all-to-all-start.1 = ((bf16[32,128,1,128]{3,0,2,1:T(8,128)(2,1)}), bf16[32,128,1,128]{3,0,2,1:T(8,128)(2,1)S(1)}, u32[]{:S(2)}, u32[]{:S(2)}) async-start(bf16[32,128,1,128]{3,0,2,1:T(8,128)(2,1)} %bitcast.65), calls=%async_computation.1 | async-start | bytes 2097152 | tf_op jit(solution)/shard_map/all_to_all | solution.py:75
Sparse Core Ops, SparseCore 0:
  9.4 53.7 all-gather.4
  65.3 123.1 all-gather.2
where the time goes:
time: 288 us
  waiting for transfers between devices  209 us (73%)
  local copies, waits for them, and re-layouts  32.5 us (11%)
  between operations  15.5 us (5%)
  matrix products  12.1 us (4%)
  starting transfers between devices  10.3 us (4%)
  other arithmetic  8.19 us (3%)
    all_gather x1, waiting for transfers between devices, local(): full_weight = lax.all_gather(kv_weight, 'ctx', axis=0, tiled=True)  125 us
    all_gather x1, waiting for transfers between devices, local(): gathered_queries = lax.all_gather(queries, 'ctx', axis=0, tiled=True)  50.4 us
    all_to_all x1, waiting for transfers between devices, local(): lax.all_to_all(accum[:, :, None, :].astype(jnp.bfloat16), 'ctx', split_ax...  22.9 us
    cond x8, local copies, waits for them, and re-layouts  17.9 us
    dot_general x1, matrix products, tile_update(): jnp.dot(latent, weight_matrix, preferred_element_type=jnp.float32)  5.96 us
  transfers between devices with their start and end apart: 5, of which 5 were waited for; matrix products, arithmetic and copies ran while one was open for 2% of the time, Pallas kernels for 0%

commit v1 on v0

--- a/solution.py
+++ b/solution.py
@@ -1,14 +1,138 @@
+import functools
 import math
 
 import jax
 import jax.numpy as jnp
 from jax import lax
+from jax.experimental import pallas as pl
+from jax.experimental.pallas import tpu as pltpu
 from jax.sharding import PartitionSpec as P
 
 LAT = 512
 ROPE = 64
 NOPE = 128
 VD = 128
+HIDDEN = -1e30
+
+
+def attend_kernel(
+    slots, rows, halves, heads,
+    order_ref, start_ref, weight_ref, query_ref, *refs,
+):
+    piece_refs = refs[: 1 + 2 * (slots - 1)]
+    out_ref, latent, keys, sems = refs[1 + 2 * (slots - 1):]
+    half = rows // halves
+    me = lax.axis_index("ctx")
+    core = lax.axis_index("tp")
+    copies = [pltpu.make_async_copy(piece_refs[0], latent.at[pl.ds(0, rows)], sems.at[0])]
+    for slot in range(1, slots):
+        for which in range(2):
+            at = core if which == 0 else 1 - core
+            place = pl.multiple_of(slot * rows + at * half, half)
+            index = 2 * slot - 1 + which
+            copies.append(
+                pltpu.make_async_copy(
+                    piece_refs[index], latent.at[pl.ds(place, half)], sems.at[index]
+                )
+            )
+    for copy in copies:
+        copy.start()
+    for copy in copies:
+        copy.wait()
+    total_rows = slots * rows
+    query_count = query_ref.shape[0] * query_ref.shape[1]
+    scale = math.log2(math.e) / math.sqrt(NOPE + ROPE)
+    rope = latent[:, LAT:]
+    tail = jnp.concatenate([rope, jnp.zeros_like(rope)], axis=1)
+    for buffer in range(2):
+        keys[buffer, :, NOPE:] = tail
+    ahead = lax.broadcasted_iota(jnp.int32, (query_count, rows), 1) - lax.broadcasted_iota(
+        jnp.int32, (query_count, rows), 0
+    )
+    limits = [start_ref[0] - order_ref[me ^ slot] * rows for slot in range(slots)]
+    for head in range(heads):
+        buffer = head % 2
+        weight = weight_ref[:, :, head * (NOPE + VD):(head + 1) * (NOPE + VD)]
+        weight = weight.reshape(LAT, NOPE + VD)
+        key_value = jnp.dot(latent[:, :LAT], weight, preferred_element_type=jnp.float32)
+        key_value = key_value.astype(jnp.bfloat16)
+        keys[buffer, :, :NOPE] = key_value[:, :NOPE]
+        values = key_value[:, NOPE:]
+        query = query_ref[:, :, head * 256:(head + 1) * 256].reshape(query_count, 256)
+        scores = lax.dot_general(
+            query, keys[buffer], (((1,), (1,)), ((), ())), preferred_element_type=jnp.float32
+        )
+        scores = jnp.concatenate(
+            [
+                jnp.where(
+                    ahead <= limits[slot], scores[:, slot * rows:(slot + 1) * rows], HIDDEN
+                )
+                for slot in range(slots)
+            ],
+            axis=1,
+        )
+        top = jnp.max(scores, axis=1, keepdims=True)
+        probs = jnp.exp2((scores - top) * scale)
+        totals = jnp.sum(probs, axis=1, keepdims=True)
+        result = jnp.dot(probs.astype(jnp.bfloat16), values, preferred_element_type=jnp.float32)
+        out_ref[:, head * VD:(head + 1) * VD] = (result / totals).astype(jnp.bfloat16)
+
+
+def split_by_heads(contexts, cores, queries, latent_cache, kv_weight, block_order, span_start):
+    query_rows, head_count, query_width = queries.shape
+    heads = head_count // contexts
+    rows = latent_cache.shape[0]
+    half = rows // cores
+    weight_rows = kv_weight.shape[0]
+
+    def swap(array, bit):
+        return lax.ppermute(array, "ctx", [(i, i ^ bit) for i in range(contexts)])
+
+    weight = kv_weight.reshape(weight_rows, contexts, heads * (NOPE + VD)).transpose(1, 0, 2)
+    padded = jnp.pad(queries, ((0, 0), (0, 0), (0, 256 - query_width)))
+    query = padded.reshape(query_rows, contexts, heads * 256).transpose(1, 0, 2)
+    packed = jnp.concatenate([weight, query], axis=1)
+    packed = lax.all_to_all(packed, "ctx", 0, 0, tiled=True)
+    weight = packed[:, :weight_rows]
+    query = packed[:, weight_rows:]
+
+    core = lax.axis_index("tp")
+    held = {0: lax.dynamic_slice_in_dim(latent_cache, core * half, half, 0)}
+    bits = []
+    bit = contexts // 2
+    while bit >= 1:
+        bits.append(bit)
+        bit //= 2
+    for bit in bits:
+        for slot in list(held):
+            held[slot | bit] = swap(held[slot], bit)
+    pieces = [latent_cache]
+    for slot in range(1, contexts):
+        pieces.append(held[slot])
+        pieces.append(lax.ppermute(held[slot], "tp", [(0, 1), (1, 0)]))
+
+    total_rows = contexts * rows
+    query_count = contexts * query_rows
+    anywhere = pl.BlockSpec(memory_space=pl.ANY)
+    on_chip = pl.BlockSpec(memory_space=pltpu.VMEM)
+    scalars = pl.BlockSpec(memory_space=pltpu.SMEM)
+    attended = pl.pallas_call(
+        functools.partial(attend_kernel, contexts, rows, cores, heads),
+        out_shape=jax.ShapeDtypeStruct((query_count, heads * VD), jnp.bfloat16),
+        in_specs=[scalars, scalars, on_chip, on_chip] + [anywhere] * len(pieces),
+        out_specs=on_chip,
+        scratch_shapes=[
+            pltpu.VMEM((total_rows, LAT + ROPE), jnp.bfloat16),
+            pltpu.VMEM((2, total_rows, 256), jnp.bfloat16),
+            pltpu.SemaphoreType.DMA((len(pieces),)),
+        ],
+        compiler_params=pltpu.CompilerParams(vmem_limit_bytes=48 * 2**20),
+        name="attend",
+    )(block_order, span_start, weight, query, *pieces)
+    attended = attended.reshape(contexts, query_rows, heads * VD)
+    attended = lax.all_to_all(attended, "ctx", 0, 0, tiled=True)
+    attended = attended.reshape(contexts, query_rows, heads, VD).transpose(1, 0, 2, 3)
+    return attended.reshape(query_rows, head_count, VD)
 
 
 def tile_update(running, tile_rows, tile_positions, gathered_queries, weight_matrix, query_last):
@@ -45,7 +169,7 @@
     return (new_max, row_total, accum)
 
 
-def local(queries, latent_cache, kv_weight, block_order, span_start):
+def split_by_context(queries, latent_cache, kv_weight, block_order, span_start):
     shard_index = lax.axis_index("ctx")
     gathered_queries = lax.all_gather(queries, "ctx", axis=0, tiled=True)
     full_weight = lax.all_gather(kv_weight, "ctx", axis=0, tiled=True)
@@ -99,6 +223,16 @@
 
 
 def solution(mesh):
+    contexts = mesh.shape["ctx"]
+    cores = mesh.shape["tp"]
+
+    def local(queries, latent_cache, kv_weight, block_order, span_start):
+        arrays = (queries, latent_cache, kv_weight, block_order, span_start)
+        whole_heads = queries.shape[1] % contexts == 0 and contexts & (contexts - 1) == 0
+        if whole_heads and cores == 2:
+            return split_by_heads(contexts, cores, *arrays)
+        return split_by_context(*arrays)
+
     return jax.shard_map(
         local,
         mesh=mesh,

time: 288 us -> 91 us (0.32)
  waiting for transfers between devices: 209 us -> 41.5 us
  local copies, waits for them, and re-layouts: 32.5 us -> 5.89 us
  between operations: 15.5 us -> 0.83 us
  matrix products: 12.1 us -> 0 us
  Pallas kernels: 0 us -> 11.8 us
  blocking collectives: 0 us -> 11.7 us
  starting transfers between devices: 10.3 us -> 17.8 us
  other arithmetic: 8.19 us -> 1.19 us
    all_gather x2 -> x0, waiting for transfers between devices: 176 us -> none  [the longest x1 125 us: local(): full_weight = lax.all_gather(kv_weight, 'ctx', axis=0, tiled=True)]
    ppermute x0 -> x14, waiting for transfers between devices: none -> 41.5 us  [the longest x7 41.5 us: swap(): return lax.ppermute(array, 'ctx', [(i, i ^ bit) for i in range(contexts)])]
    all_to_all x3 -> x1, waiting for transfers between devices: 32.5 us -> 0.01 us  [split_by_heads(): packed = lax.all_to_all(packed, 'ctx', 0, 0, tiled=True)]
    cond x9 -> x0, local copies, waits for them, and re-layouts: 19.5 us -> none
    dot_general x4 -> x0, matrix products: 12.1 us -> none  [the longest x1 5.96 us: tile_update(): jnp.dot(latent, weight_matrix, preferred_element_type=jnp.float32)]
    pallas_call x0 -> x1, Pallas kernels: none -> 11.8 us  [split_by_heads(): pl.pallas_call(functools.partial(attend_kernel, contexts, rows, cores, he...]
    all_to_all x0 -> x1, blocking collectives: none -> 11.7 us  [split_by_heads(): attended = lax.all_to_all(attended, 'ctx', 0, 0, tiled=True)]
    ppermute x0 -> x14, starting transfers between devices: none -> 10.4 us  [the longest x7 9.36 us: swap(): return lax.ppermute(array, 'ctx', [(i, i ^ bit) for i in range(contexts)])]
  transfers between devices with their start and end apart: 5 -> 15, of which waited for: 5 -> 5; matrix products, arithmetic and copies ran while one was open for 2% -> 3% of each run, Pallas kernels for 0% -> 0%
where the time goes in v1:
time: 91 us; the launch traced here: 90.7 us
  waiting for transfers between devices  41.5 us (46%)
  starting transfers between devices  17.8 us (20%)
  Pallas kernels  11.8 us (13%)
  blocking collectives  11.7 us (13%)
  local copies, waits for them, and re-layouts  5.89 us (6%)
  other arithmetic  1.19 us (1%)
    ppermute x7, waiting for transfers between devices, swap(): return lax.ppermute(array, 'ctx', [(i, i ^ bit) for i in range(contexts)])  41.5 us
    pallas_call x1, Pallas kernels, split_by_heads(): pl.pallas_call(functools.partial(attend_kernel, contexts, rows, cores, he...  11.8 us
    all_to_all x1, blocking collectives, split_by_heads(): attended = lax.all_to_all(attended, 'ctx', 0, 0, tiled=True)  11.7 us
    ppermute x7, starting transfers between devices, swap(): return lax.ppermute(array, 'ctx', [(i, i ^ bit) for i in range(contexts)])  9.36 us
    all_to_all x1, starting transfers between devices, split_by_heads(): packed = lax.all_to_all(packed, 'ctx', 0, 0, tiled=True)  7.38 us
  transfers between devices with their start and end apart: 15, of which 5 were waited for; matrix products, arithmetic and copies ran while one was open for 3% of the time, Pallas kernels for 0%

profile of v1, /device:TPU:0, one launch (start us, length us, event | category | flops | bytes accessed | tf_op | source)
XLA Modules:
  0.0 90.7 jit_solution(750629969823086535)
XLA Ops:
  0.0 0.0 copy-start.1
  0.0 1.1 %pad.4 = bf16[16,32,256]{2,1,0:T(8,128)(2,1)S(1)} pad(bf16[16,32,192]{2,1,0:T(8,128)(2,1)} %param.5, bf16[]{:T(256)} %constant.2.clone.1), padding=0_0x0_0x0_64 | pad | bytes 458754 | tf_op jit(solution)/shard_map/jit(_pad)/pad | solution.py:92
  1.1 0.2 reshape.16
  1.3 0.2 copy.17
  1.4 0.0 copy-done.1
  1.4 0.7 reshape.15
  2.1 0.6 copy.16
  2.7 1.2 %pad_maximum_fusion = bf16[8,80,1024]{2,1,0:T(8,128)(2,1)} fusion(bf16[8,16,1024]{2,1,0:T(8,128)(2,1)S(1)} %bitcast.12, bf16[8,64,1024]{2,1,0:T(8,128)(2,1)S(1)} %bitcast.11), kind=kLoop, calls=%fused_computation | loop fusion | flops 2621440 | bytes 2621440 | tf_op jit(solution)/shard_map/concatenate | solution.py:94
  3.9 0.0 copy-start.2
  3.9 7.4 %all-to-all-start = ((bf16[8,80,1024]{2,1,0:T(8,128)(2,1)}), bf16[8,80,1024]{2,1,0:T(8,128)(2,1)}, u32[]{:S(2)}, u32[]{:S(2)}) async-start(bf16[8,80,1024]{2,1,0:T(8,128)(2,1)} %pad_maximum_fusion), calls=%async_computation | async-start | bytes 2621440 | tf_op jit(solution)/shard_map/all_to_all | solution.py:95
  11.3 0.0 copy-done.2
  11.3 0.2 copy.12.refs_0_
  11.5 3.0 %collective-permute-start.6 = (bf16[128,576]{1,0:T(8,128)(2,1)S(1)}, bf16[128,576]{1,0:T(8,128)(2,1)S(1)}, u32[]{:S(2)}, u32[]{:S(2)}) collective-permute-start(bf16[128,576]{1,0:T(8,128)(2,1)S(1)} %constant_dynamic-slice_fusion), channel_id=1, source_target_pairs={{0,8},{2,10},{4,12},{6,14},{8,0},{10,2},{12,4},{14,6},{1,9},{3,11}... | collective-permute-start | bytes 442376 | tf_op jit(solution)/shard_map/ppermute | solution.py:89
  14.5 1.5 %collective-permute-start = (bf16[128,576]{1,0:T(8,128)(2,1)S(1)}, bf16[128,576]{1,0:T(8,128)(2,1)S(1)}, u32[]{:S(2)}, u32[]{:S(2)}) collective-permute-start(bf16[128,576]{1,0:T(8,128)(2,1)S(1)} %constant_dynamic-slice_fusion), channel_id=1, source_target_pairs={{0,2},{2,0},{4,6},{6,4},{8,10},{10,8},{12,14},{14,12},{1,3},{3,1},... | collective-permute-start | bytes 442376 | tf_op jit(solution)/shard_map/ppermute | solution.py:89
  16.0 1.5 %collective-permute-start.2 = (bf16[128,576]{1,0:T(8,128)(2,1)S(1)}, bf16[128,576]{1,0:T(8,128)(2,1)S(1)}, u32[]{:S(2)}, u32[]{:S(2)}) collective-permute-start(bf16[128,576]{1,0:T(8,128)(2,1)S(1)} %constant_dynamic-slice_fusion), channel_id=1, source_target_pairs={{0,4},{2,6},{4,0},{6,2},{8,12},{10,14},{12,8},{14,10},{1,5},{3,7},... | collective-permute-start | bytes 442376 | tf_op jit(solution)/shard_map/ppermute | solution.py:89
  17.4 32.3 %collective-permute-done.6.refs_7_ = bf16[128,576]{1,0:T(8,128)(2,1)S(1)} collective-permute-done((bf16[128,576]{1,0:T(8,128)(2,1)S(1)}, bf16[128,576]{1,0:T(8,128)(2,1)S(1)}, u32[]{:S(2)}, u32[]{:S(2)}) %collective-permute-start.6) | collective-permute-done | bytes 147488 | tf_op jit(solution)/shard_map/ppermute | solution.py:89
  49.7 0.0 collective-permute-start.10
  49.7 0.0 collective-permute-done.refs_1_
  49.7 0.0 collective-permute-start.1
  49.7 0.0 collective-permute-done.2.refs_3_
  49.7 0.5 collective-permute-start.3
  50.2 1.4 %collective-permute-start.4 = (bf16[128,576]{1,0:T(8,128)(2,1)S(1)}, bf16[128,576]{1,0:T(8,128)(2,1)S(1)}, u32[]{:S(2)}, u32[]{:S(2)}) collective-permute-start(bf16[128,576]{1,0:T(8,128)(2,1)S(1)} %collective-permute-done.2.refs_3_), channel_id=1, source_target_pairs={{0,2},{2,0},{4,6},{6,4},{8,10},{10,8},{12,14},{14,12},{1,3},{3,1},... | collective-permute-start | bytes 442376 | tf_op jit(solution)/shard_map/ppermute | solution.py:89
  51.6 0.6 collective-permute-start.8
  52.2 2.8 %collective-permute-done.10.refs_11_ = bf16[128,576]{1,0:T(8,128)(2,1)S(1)} collective-permute-done((bf16[128,576]{1,0:T(8,128)(2,1)S(1)}, bf16[128,576]{1,0:T(8,128)(2,1)S(1)}, u32[]{:S(2)}, u32[]{:S(2)}) %collective-permute-start.10) | collective-permute-done | bytes 147488 | tf_op jit(solution)/shard_map/ppermute | solution.py:89
  55.0 1.4 %collective-permute-start.12 = (bf16[128,576]{1,0:T(8,128)(2,1)S(1)}, bf16[128,576]{1,0:T(8,128)(2,1)S(1)}, u32[]{:S(2)}, u32[]{:S(2)}) collective-permute-start(bf16[128,576]{1,0:T(8,128)(2,1)S(1)} %collective-permute-done.10.refs_11_), channel_id=1, source_target_pairs={{0,2},{2,0},{4,6},{6,4},{8,10},{10,8},{12,14},{14,12},{1,3},{3,1},... | collective-permute-start | bytes 442376 | tf_op jit(solution)/shard_map/ppermute | solution.py:89
  56.4 0.0 collective-permute-done.1.refs_2_
  56.4 0.0 collective-permute-start.7
  56.4 0.0 collective-permute-done.3.refs_4_
  56.4 0.5 collective-permute-start.11
  56.9 0.3 collective-permute-done.4.refs_5_
  57.3 0.0 collective-permute-start.5
  57.3 3.5 %collective-permute-done.8.refs_9_ = bf16[128,576]{1,0:T(8,128)(2,1)S(1)} collective-permute-done((bf16[128,576]{1,0:T(8,128)(2,1)S(1)}, bf16[128,576]{1,0:T(8,128)(2,1)S(1)}, u32[]{:S(2)}, u32[]{:S(2)}) %collective-permute-start.8) | collective-permute-done | bytes 147488 | tf_op jit(solution)/shard_map/ppermute | solution.py:89
  60.8 0.0 collective-permute-start.9
  60.8 2.6 %collective-permute-done.12.refs_13_ = bf16[128,576]{1,0:T(8,128)(2,1)S(1)} collective-permute-done((bf16[128,576]{1,0:T(8,128)(2,1)S(1)}, bf16[128,576]{1,0:T(8,128)(2,1)S(1)}, u32[]{:S(2)}, u32[]{:S(2)}) %collective-permute-start.12) | collective-permute-done | bytes 147488 | tf_op jit(solution)/shard_map/ppermute | solution.py:89
  63.4 0.0 collective-permute-start.13
  64.1 0.0 copy-start
  64.1 0.0 all-to-all-done
  64.1 1.3 %slice.8.weight_ref = bf16[8,64,1024]{2,1,0:T(8,128)(2,1)S(1)} slice(bf16[8,80,1024]{2,1,0:T(8,128)(2,1)} %all-to-all-done), slice={[0:8], [0:64], [0:1024]} | slice | bytes 2097152 | tf_op jit(solution)/shard_map/slice | solution.py:96
  65.4 1.0 %slice.9.query_ref = bf16[8,16,1024]{2,1,0:T(8,128)(2,1)S(1)} slice(bf16[8,80,1024]{2,1,0:T(8,128)(2,1)} %all-to-all-done), slice={[0:8], [64:80], [0:1024]} | slice | bytes 524288 | tf_op jit(solution)/shard_map/slice | solution.py:97
  66.4 0.0 collective-permute-done.7.refs_8_
  66.4 0.0 collective-permute-done.5.refs_6_
  66.4 0.0 collective-permute-done.9.refs_10_
  66.4 0.0 collective-permute-done.11.refs_12_
  66.4 0.0 collective-permute-done.13.refs_14_
  66.4 0.0 copy-done
  66.4 11.8 %attend.1 = bf16[128,512]{1,0:T(8,128)(2,1)S(1)} custom-call(s32[8]{0:T(128)S(1)} %copy-done, s32[1]{0:T(128)S(6)} %copy.18.start_ref, bf16[8,64,1024]{2,1,0:T(8,128)(2,1)S(1)} %slice.8.weight_ref, bf16[8,16,1024]{2,1,0:T(8,128)(2,1)S(1)} %slice.9.query_ref, bf16[256,576]{1,0:T(8,128)(2,1)S(1)} %copy.12.refs_0_, ...), custom_call_target="tpu_custom_call" | custom-call | tf_op jit(solution)/shard_map/attend/pallas_call | solution.py:119
  78.3 11.7 %all_to_all.10 = bf16[8,16,512]{2,1,0:T(8,128)(2,1)S(1)} all-to-all(bf16[8,16,512]{2,1,0:T(8,128)(2,1)S(1)} %bitcast.10), channel_id=1, replica_groups=mesh['groups'=2,'ctx'=8,'tp'=2] {'ctx'}, dimensions={0} | all-to-all | bytes 262144 | tf_op jit(solution)/shard_map/all_to_all | solution.py:133
  90.0 0.7 copy.13
  (2 shorter events, 0.1 us)
Async XLA Ops:
  0.0 1.4 %copy-start.1 = (bf16[64,32,256]{2,1,0:T(8,128)(2,1)S(1)}, bf16[64,32,256]{2,1,0:T(8,128)(2,1)}, u32[]{:S(2)}) copy-start(bf16[64,32,256]{2,1,0:T(8,128)(2,1)} %param.7) | copy-start | bytes 3145732
  3.9 7.4 %copy-start.2 = (bf16[256,576]{0,1:T(8,128)(2,1)S(1)}, bf16[256,576]{0,1:T(8,128)(2,1)}, u32[]{:S(2)}) copy-start(bf16[256,576]{0,1:T(8,128)(2,1)} %param.6) | copy-start | bytes 884740
  3.9 60.2 %all-to-all-start = ((bf16[8,80,1024]{2,1,0:T(8,128)(2,1)}), bf16[8,80,1024]{2,1,0:T(8,128)(2,1)}, u32[]{:S(2)}, u32[]{:S(2)}) async-start(bf16[8,80,1024]{2,1,0:T(8,128)(2,1)} %pad_maximum_fusion), calls=%async_computation | async-start | bytes 2621440 | tf_op jit(solution)/shard_map/all_to_all | solution.py:95
  11.5 38.2 %collective-permute-start.6 = (bf16[128,576]{1,0:T(8,128)(2,1)S(1)}, bf16[128,576]{1,0:T(8,128)(2,1)S(1)}, u32[]{:S(2)}, u32[]{:S(2)}) collective-permute-start(bf16[128,576]{1,0:T(8,128)(2,1)S(1)} %constant_dynamic-slice_fusion), channel_id=1, source_target_pairs={{0,8},{2,10},{4,12},{6,14},{8,0},{10,2},{12,4},{14,6},{1,9},{3,11}... | collective-permute-start | bytes 442376 | tf_op jit(solution)/shard_map/ppermute | solution.py:89
  14.5 35.2 %collective-permute-start = (bf16[128,576]{1,0:T(8,128)(2,1)S(1)}, bf16[128,576]{1,0:T(8,128)(2,1)S(1)}, u32[]{:S(2)}, u32[]{:S(2)}) collective-permute-start(bf16[128,576]{1,0:T(8,128)(2,1)S(1)} %constant_dynamic-slice_fusion), channel_id=1, source_target_pairs={{0,2},{2,0},{4,6},{6,4},{8,10},{10,8},{12,14},{14,12},{1,3},{3,1},... | collective-permute-start | bytes 442376 | tf_op jit(solution)/shard_map/ppermute | solution.py:89
  16.0 33.7 %collective-permute-start.2 = (bf16[128,576]{1,0:T(8,128)(2,1)S(1)}, bf16[128,576]{1,0:T(8,128)(2,1)S(1)}, u32[]{:S(2)}, u32[]{:S(2)}) collective-permute-start(bf16[128,576]{1,0:T(8,128)(2,1)S(1)} %constant_dynamic-slice_fusion), channel_id=1, source_target_pairs={{0,4},{2,6},{4,0},{6,2},{8,12},{10,14},{12,8},{14,10},{1,5},{3,7},... | collective-permute-start | bytes 442376 | tf_op jit(solution)/shard_map/ppermute | solution.py:89
  49.7 5.3 %collective-permute-start.10 = (bf16[128,576]{1,0:T(8,128)(2,1)S(1)}, bf16[128,576]{1,0:T(8,128)(2,1)S(1)}, u32[]{:S(2)}, u32[]{:S(2)}) collective-permute-start(bf16[128,576]{1,0:T(8,128)(2,1)S(1)} %collective-permute-done.6.refs_7_), channel_id=1, source_target_pairs={{0,4},{2,6},{4,0},{6,2},{8,12},{10,14},{12,8},{14,10},{1,5},{3,7},... | collective-permute-start | bytes 442376 | tf_op jit(solution)/shard_map/ppermute | solution.py:89
  49.7 6.7 %collective-permute-start.1 = (bf16[128,576]{1,0:T(8,128)(2,1)S(1)}, bf16[128,576]{1,0:T(8,128)(2,1)S(1)}, u32[]{:S(2)}, u32[]{:S(2)}) collective-permute-start(bf16[128,576]{1,0:T(8,128)(2,1)S(1)} %collective-permute-done.refs_1_), channel_id=1, source_target_pairs={{0,1},{1,0},{2,3},{3,2},{4,5},{5,4},{6,7},{7,6},{8,9},{9,8},{10,11... | collective-permute-start | bytes 442376 | tf_op jit(solution)/shard_map/ppermute | solution.py:112
  49.7 6.7 %collective-permute-start.3 = (bf16[128,576]{1,0:T(8,128)(2,1)S(1)}, bf16[128,576]{1,0:T(8,128)(2,1)S(1)}, u32[]{:S(2)}, u32[]{:S(2)}) collective-permute-start(bf16[128,576]{1,0:T(8,128)(2,1)S(1)} %collective-permute-done.2.refs_3_), channel_id=1, source_target_pairs={{0,1},{1,0},{2,3},{3,2},{4,5},{5,4},{6,7},{7,6},{8,9},{9,8},{10,11... | collective-permute-start | bytes 442376 | tf_op jit(solution)/shard_map/ppermute | solution.py:112
  50.2 7.1 %collective-permute-start.4 = (bf16[128,576]{1,0:T(8,128)(2,1)S(1)}, bf16[128,576]{1,0:T(8,128)(2,1)S(1)}, u32[]{:S(2)}, u32[]{:S(2)}) collective-permute-start(bf16[128,576]{1,0:T(8,128)(2,1)S(1)} %collective-permute-done.2.refs_3_), channel_id=1, source_target_pairs={{0,2},{2,0},{4,6},{6,4},{8,10},{10,8},{12,14},{14,12},{1,3},{3,1},... | collective-permute-start | bytes 442376 | tf_op jit(solution)/shard_map/ppermute | solution.py:89
  51.6 9.1 %collective-permute-start.8 = (bf16[128,576]{1,0:T(8,128)(2,1)S(1)}, bf16[128,576]{1,0:T(8,128)(2,1)S(1)}, u32[]{:S(2)}, u32[]{:S(2)}) collective-permute-start(bf16[128,576]{1,0:T(8,128)(2,1)S(1)} %collective-permute-done.6.refs_7_), channel_id=1, source_target_pairs={{0,2},{2,0},{4,6},{6,4},{8,10},{10,8},{12,14},{14,12},{1,3},{3,1},... | collective-permute-start | bytes 442376 | tf_op jit(solution)/shard_map/ppermute | solution.py:89
  55.0 8.4 %collective-permute-start.12 = (bf16[128,576]{1,0:T(8,128)(2,1)S(1)}, bf16[128,576]{1,0:T(8,128)(2,1)S(1)}, u32[]{:S(2)}, u32[]{:S(2)}) collective-permute-start(bf16[128,576]{1,0:T(8,128)(2,1)S(1)} %collective-permute-done.10.refs_11_), channel_id=1, source_target_pairs={{0,2},{2,0},{4,6},{6,4},{8,10},{10,8},{12,14},{14,12},{1,3},{3,1},... | collective-permute-start | bytes 442376 | tf_op jit(solution)/shard_map/ppermute | solution.py:89
  56.4 9.9 %collective-permute-start.7 = (bf16[128,576]{1,0:T(8,128)(2,1)S(1)}, bf16[128,576]{1,0:T(8,128)(2,1)S(1)}, u32[]{:S(2)}, u32[]{:S(2)}) collective-permute-start(bf16[128,576]{1,0:T(8,128)(2,1)S(1)} %collective-permute-done.6.refs_7_), channel_id=1, source_target_pairs={{0,1},{1,0},{2,3},{3,2},{4,5},{5,4},{6,7},{7,6},{8,9},{9,8},{10,11... | collective-permute-start | bytes 442376 | tf_op jit(solution)/shard_map/ppermute | solution.py:112
  56.4 10.0 %collective-permute-start.11 = (bf16[128,576]{1,0:T(8,128)(2,1)S(1)}, bf16[128,576]{1,0:T(8,128)(2,1)S(1)}, u32[]{:S(2)}, u32[]{:S(2)}) collective-permute-start(bf16[128,576]{1,0:T(8,128)(2,1)S(1)} %collective-permute-done.10.refs_11_), channel_id=1, source_target_pairs={{0,1},{1,0},{2,3},{3,2},{4,5},{5,4},{6,7},{7,6},{8,9},{9,8},{10,11... | collective-permute-start | bytes 442376 | tf_op jit(solution)/shard_map/ppermute | solution.py:112
  57.3 9.1 %collective-permute-start.5 = (bf16[128,576]{1,0:T(8,128)(2,1)S(1)}, bf16[128,576]{1,0:T(8,128)(2,1)S(1)}, u32[]{:S(2)}, u32[]{:S(2)}) collective-permute-start(bf16[128,576]{1,0:T(8,128)(2,1)S(1)} %collective-permute-done.4.refs_5_), channel_id=1, source_target_pairs={{0,1},{1,0},{2,3},{3,2},{4,5},{5,4},{6,7},{7,6},{8,9},{9,8},{10,11... | collective-permute-start | bytes 442376 | tf_op jit(solution)/shard_map/ppermute | solution.py:112
  60.8 5.6 %collective-permute-start.9 = (bf16[128,576]{1,0:T(8,128)(2,1)S(1)}, bf16[128,576]{1,0:T(8,128)(2,1)S(1)}, u32[]{:S(2)}, u32[]{:S(2)}) collective-permute-start(bf16[128,576]{1,0:T(8,128)(2,1)S(1)} %collective-permute-done.8.refs_9_), channel_id=1, source_target_pairs={{0,1},{1,0},{2,3},{3,2},{4,5},{5,4},{6,7},{7,6},{8,9},{9,8},{10,11... | collective-permute-start | bytes 442376 | tf_op jit(solution)/shard_map/ppermute | solution.py:112
  63.4 3.0 %collective-permute-start.13 = (bf16[128,576]{1,0:T(8,128)(2,1)S(1)}, bf16[128,576]{1,0:T(8,128)(2,1)S(1)}, u32[]{:S(2)}, u32[]{:S(2)}) collective-permute-start(bf16[128,576]{1,0:T(8,128)(2,1)S(1)} %collective-permute-done.12.refs_13_), channel_id=1, source_target_pairs={{0,1},{1,0},{2,3},{3,2},{4,5},{5,4},{6,7},{7,6},{8,9},{9,8},{10,11... | collective-permute-start | bytes 442376 | tf_op jit(solution)/shard_map/ppermute | solution.py:112
  64.1 2.4 %copy-start = (s32[8]{0:T(128)S(1)}, s32[8]{0:T(128)}, u32[]{:S(2)}) copy-start(s32[8]{0:T(128)} %order_ref.1) | copy-start | bytes 100

commit v2 on v1

--- a/solution.py
+++ b/solution.py
@@ -13,14 +13,13 @@
 NOPE = 128
 VD = 128
 HIDDEN = -1e30
-
-
-def attend_kernel(
-    slots, rows, halves, heads,
-    order_ref, start_ref, weight_ref, query_ref, *refs,
-):
-    piece_refs = refs[: 1 + 2 * (slots - 1)]
-    out_ref, latent, keys, sems = refs[1 + 2 * (slots - 1):]
+ROUNDS = ((4, 0, 4), (2, 0, 2), (1, 0, 1), (3, 2, 1), (5, 4, 1), (6, 4, 2), (7, 5, 2))
+
+
+def attend_kernel(slots, rows, halves, pair, *refs):
+    order_ref, start_ref, packed_ref, other_ref = refs[:4]
+    piece_refs = refs[4: 5 + 2 * (slots - 1)]
+    out_ref, latent, keys, sems = refs[5 + 2 * (slots - 1):]
     half = rows // halves
     me = lax.axis_index("ctx")
     core = lax.axis_index("tp")
@@ -39,8 +38,10 @@
         copy.start()
     for copy in copies:
         copy.wait()
-    total_rows = slots * rows
-    query_count = query_ref.shape[0] * query_ref.shape[1]
+    width = NOPE + VD
+    depth = other_ref.shape[1] // pair
+    query_rows = (packed_ref.shape[1] - pair * depth) // 3
+    query_count = slots * query_rows
     scale = math.log2(math.e) / math.sqrt(NOPE + ROPE)
     rope = latent[:, LAT:]
     tail = jnp.concatenate([rope, jnp.zeros_like(rope)], axis=1)
@@ -50,15 +51,23 @@
         jnp.int32, (query_count, rows), 0
     )
     limits = [start_ref[0] - order_ref[me ^ slot] * rows for slot in range(slots)]
-    for head in range(heads):
+    first = pair * depth
+    for head in range(2 * pair):
         buffer = head % 2
-        weight = weight_ref[:, :, head * (NOPE + VD):(head + 1) * (NOPE + VD)]
-        weight = weight.reshape(LAT, NOPE + VD)
+        which, member = divmod(head, pair)
+        weight_ref = packed_ref if which == 0 else other_ref
+        weight = weight_ref[:, member * depth:(member + 1) * depth, :].reshape(LAT, width)
         key_value = jnp.dot(latent[:, :LAT], weight, preferred_element_type=jnp.float32)
         key_value = key_value.astype(jnp.bfloat16)
         keys[buffer, :, :NOPE] = key_value[:, :NOPE]
         values = key_value[:, NOPE:]
-        query = query_ref[:, :, head * 256:(head + 1) * 256].reshape(query_count, 256)
+        begin = first + which * query_rows
+        part = packed_ref[:, begin:begin + query_rows, member * NOPE:(member + 1) * NOPE]
+        part = part.reshape(query_count, NOPE)
+        begin = first + 2 * query_rows
+        turned = packed_ref[:, begin:begin + query_rows, head * ROPE:(head + 1) * ROPE]
+        turned = turned.reshape(query_count, ROPE)
+        query = jnp.concatenate([part, turned, jnp.zeros_like(turned)], axis=1)
         scores = lax.dot_general(
             query, keys[buffer], (((1,), (1,)), ((), ())), preferred_element_type=jnp.float32
         )
@@ -81,31 +90,33 @@
 def split_by_heads(contexts, cores, queries, latent_cache, kv_weight, block_order, span_start):
     query_rows, head_count, query_width = queries.shape
     heads = head_count // contexts
+    pair = heads // 2
     rows = latent_cache.shape[0]
     half = rows // cores
-    weight_rows = kv_weight.shape[0]
+    depth = kv_weight.shape[0]
+    width = NOPE + VD
+    group = lax.axis_index("groups")
 
     def swap(array, bit):
         return lax.ppermute(array, "ctx", [(i, i ^ bit) for i in range(contexts)])
 
-    weight = kv_weight.reshape(weight_rows, contexts, heads * (NOPE + VD)).transpose(1, 0, 2)
-    padded = jnp.pad(queries, ((0, 0), (0, 0), (0, 256 - query_width)))
-    query = padded.reshape(query_rows, contexts, heads * 256).transpose(1, 0, 2)
-    packed = jnp.concatenate([weight, query], axis=1)
+    weight = kv_weight.reshape(depth, contexts, 2, pair, width)
+    weight = lax.dynamic_index_in_dim(weight, group, 2, keepdims=False)
+    weight = weight.transpose(1, 2, 0, 3).reshape(contexts, pair * depth, width)
+    query = queries.reshape(query_rows, contexts, 2, pair, query_width)
+    query = jnp.where(group == 0, query, query[:, :, ::-1])
+    straight = query[..., :NOPE].transpose(1, 2, 0, 3, 4)
+    straight = straight.reshape(contexts, 2 * query_rows, pair * NOPE)
+    turned = query[..., NOPE:].transpose(1, 0, 2, 3, 4)
+    turned = turned.reshape(contexts, query_rows, heads * ROPE)
+    packed = jnp.concatenate([weight, straight, turned], axis=1)
     packed = lax.all_to_all(packed, "ctx", 0, 0, tiled=True)
-    weight = packed[:, :weight_rows]
-    query = packed[:, weight_rows:]
+    other = lax.ppermute(packed[:, :pair * depth], "groups", [(0, 1), (1, 0)])
 
     core = lax.axis_index("tp")
     held = {0: lax.dynamic_slice_in_dim(latent_cache, core * half, half, 0)}
-    bits = []
-    bit = contexts // 2
-    while bit >= 1:
-        bits.append(bit)
-        bit //= 2
-    for bit in bits:
-        for slot in list(held):
-            held[slot | bit] = swap(held[slot], bit)
+    for slot, source, bit in ROUNDS:
+        held[slot] = swap(held[source], bit)
     pieces = [latent_cache]
     for slot in range(1, contexts):
         pieces.append(held[slot])
@@ -117,7 +128,7 @@
     on_chip = pl.BlockSpec(memory_space=pltpu.VMEM)
     scalars = pl.BlockSpec(memory_space=pltpu.SMEM)
     attended = pl.pallas_call(
-        functools.partial(attend_kernel, contexts, rows, cores, heads),
+        functools.partial(attend_kernel, contexts, rows, cores, pair),
         out_shape=jax.ShapeDtypeStruct((query_count, heads * VD), jnp.bfloat16),
         in_specs=[scalars, scalars, on_chip, on_chip] + [anywhere] * len(pieces),
         out_specs=on_chip,
@@ -128,10 +139,12 @@
         ],
         compiler_params=pltpu.CompilerParams(vmem_limit_bytes=48 * 2**20),
         name="attend",
-    )(block_order, span_start, weight, query, *pieces)
+    )(block_order, span_start, packed, other, *pieces)
     attended = attended.reshape(contexts, query_rows, heads * VD)
     attended = lax.all_to_all(attended, "ctx", 0, 0, tiled=True)
-    attended = attended.reshape(contexts, query_rows, heads, VD).transpose(1, 0, 2, 3)
+    attended = attended.reshape(contexts, query_rows, 2, pair, VD)
+    attended = jnp.where(group == 0, attended, attended[:, :, ::-1])
+    attended = attended.transpose(1, 0, 2, 3, 4)
     return attended.reshape(query_rows, head_count, VD)
 
 
@@ -228,8 +241,8 @@
 
     def local(queries, latent_cache, kv_weight, block_order, span_start):
         arrays = (queries, latent_cache, kv_weight, block_order, span_start)
-        whole_heads = queries.shape[1] % contexts == 0 and contexts & (contexts - 1) == 0
-        if whole_heads and cores == 2:
+        paired = queries.shape[1] % (2 * contexts) == 0 and contexts == len(ROUNDS) + 1
+        if paired and cores == 2 and mesh.shape["groups"] == 2:
             return split_by_heads(contexts, cores, *arrays)
         return split_by_context(*arrays)
 

time: 91 us -> 78.8 us (0.87)
  waiting for transfers between devices: 41.5 us -> 31.4 us
  local copies, waits for them, and re-layouts: 5.89 us -> 3.29 us
    ppermute x7, waiting for transfers between devices: 41.5 us -> 11.7 us  [swap(): return lax.ppermute(array, 'ctx', [(i, i ^ bit) for i in range(contexts)])]
    all_to_all x1, waiting for transfers between devices: 0.01 us -> 19 us  [split_by_heads(): packed = lax.all_to_all(packed, 'ctx', 0, 0, tiled=True)]
    slice x2 -> x1, local copies, waits for them, and re-layouts: 2.27 us -> 0.03 us  [split_by_heads(): other = lax.ppermute(packed[:, :pair * depth], 'groups', [(0, 1), (1, 0)])]
    ppermute x7, starting transfers between devices: 9.36 us -> 7.52 us  [swap(): return lax.ppermute(array, 'ctx', [(i, i ^ bit) for i in range(contexts)])]
    ppermute x0 -> x1, starting transfers between devices: none -> 1.58 us  [split_by_heads(): other = lax.ppermute(packed[:, :pair * depth], 'groups', [(0, 1), (1, 0)])]
    pad x1 -> x0, local copies, waits for them, and re-layouts: 1.08 us -> none  [split_by_heads(): padded = jnp.pad(queries, ((0, 0), (0, 0), (0, 256 - query_width)))]
    select_n x0 -> x2, other arithmetic: none -> 1.07 us  [the longest x1 0.8 us: split_by_heads(): attended = jnp.where(group == 0, attended, attended[:, :, ::-1])]
    reshape x6 -> x7, local copies, waits for them, and re-layouts: 2.3 us -> 2.16 us  [the longest x2 1.36 us: split_by_heads(): query = queries.reshape(query_rows, contexts, 2, pair, query_width)]
  transfers between devices with their start and end apart: 15 -> 16, of which waited for: 5 -> 6; matrix products, arithmetic and copies ran while one was open for 3% -> 0% of each run, Pallas kernels for 0% -> 0%
where the time goes in v2:
time: 78.8 us; the launch traced here: 78.5 us
  waiting for transfers between devices  31.4 us (40%)
  starting transfers between devices  17.6 us (22%)
  Pallas kernels  11.8 us (15%)
  blocking collectives  11.6 us (15%)
  local copies, waits for them, and re-layouts  3.29 us (4%)
  other arithmetic  2.01 us (3%)
  between operations  0.84 us (1%)
    all_to_all x1, waiting for transfers between devices, split_by_heads(): packed = lax.all_to_all(packed, 'ctx', 0, 0, tiled=True)  19 us
    pallas_call x1, Pallas kernels, split_by_heads(): pl.pallas_call(functools.partial(attend_kernel, contexts, rows, cores, pa...  11.8 us
    ppermute x7, waiting for transfers between devices, swap(): return lax.ppermute(array, 'ctx', [(i, i ^ bit) for i in range(contexts)])  11.7 us
    all_to_all x1, blocking collectives, split_by_heads(): attended = lax.all_to_all(attended, 'ctx', 0, 0, tiled=True)  11.6 us
    ppermute x7, starting transfers between devices, swap(): return lax.ppermute(array, 'ctx', [(i, i ^ bit) for i in range(contexts)])  7.52 us
    all_to_all x1, starting transfers between devices, split_by_heads(): packed = lax.all_to_all(packed, 'ctx', 0, 0, tiled=True)  7.38 us
    ppermute x1, starting transfers between devices, split_by_heads(): other = lax.ppermute(packed[:, :pair * depth], 'groups', [(0, 1), (1, 0)])  1.58 us
  transfers between devices with their start and end apart: 16, of which 6 were waited for; matrix products, arithmetic and copies ran while one was open for 0% of the time, Pallas kernels for 0%

profile of v2, /device:TPU:0, one launch (start us, length us, event | category | flops | bytes accessed | tf_op | source)
XLA Modules:
  0.0 78.5 jit_solution(9784977520097870030)
XLA Ops:
  0.0 1.2 %reshape.26 = bf16[16,8,2,2,192]{4,3,2,1,0:T(2,128)(2,1)S(1)} reshape(bf16[16,32,192]{2,1,0:T(8,128)(2,1)} %param.5) | data formatting | bytes 393216 | tf_op jit(solution)/shard_map/reshape | solution.py:106
  1.2 0.2 copy.8
  1.4 0.3 broadcast_select_fusion
  1.7 0.1 slice_bitcast_fusion.1
  1.8 0.1 slice_bitcast_fusion
  1.9 0.4 reshape.24
  2.3 0.4 constant_dynamic-slice_fusion.1
  2.7 0.2 copy.6
  2.9 0.1 copy.9
  3.0 0.1 reshape.27
  3.1 0.1 reshape.28
  3.3 0.9 %pad_maximum_fusion = bf16[8,176,256]{2,1,0:T(8,128)(2,1)} fusion(bf16[8,16,256]{2,1,0:T(8,128)(2,1)S(1)} %reshape.28, bf16[8,32,256]{2,1,0:T(8,128)(2,1)S(1)} %reshape.27, bf16[8,128,256]{2,1,0:T(8,128)(2,1)S(1)} %bitcast.14), kind=kLoop, calls=%fused_computation | loop fusion | flops 2162688 | bytes 1441792 | tf_op jit(solution)/shard_map/concatenate | solution.py:112
  4.2 7.4 %all-to-all-start = ((bf16[8,176,256]{2,1,0:T(8,128)(2,1)}), bf16[8,176,256]{2,1,0:T(8,128)(2,1)S(1)}, u32[]{:S(2)}, u32[]{:S(2)}) async-start(bf16[8,176,256]{2,1,0:T(8,128)(2,1)} %pad_maximum_fusion), calls=%async_computation | async-start | bytes 1441792 | tf_op jit(solution)/shard_map/all_to_all | solution.py:113
  11.6 0.2 copy.11.refs_4_
  11.8 3.0 %collective-permute-start.7 = (bf16[128,576]{1,0:T(8,128)(2,1)S(1)}, bf16[128,576]{1,0:T(8,128)(2,1)S(1)}, u32[]{:S(2)}, u32[]{:S(2)}) collective-permute-start(bf16[128,576]{1,0:T(8,128)(2,1)S(1)} %constant_dynamic-slice_fusion), channel_id=1, source_target_pairs={{0,8},{2,10},{4,12},{6,14},{8,0},{10,2},{12,4},{14,6},{1,9},{3,11}... | collective-permute-start | bytes 442376 | tf_op jit(solution)/shard_map/ppermute | solution.py:101
  14.8 1.5 %collective-permute-start.3 = (bf16[128,576]{1,0:T(8,128)(2,1)S(1)}, bf16[128,576]{1,0:T(8,128)(2,1)S(1)}, u32[]{:S(2)}, u32[]{:S(2)}) collective-permute-start(bf16[128,576]{1,0:T(8,128)(2,1)S(1)} %constant_dynamic-slice_fusion), channel_id=1, source_target_pairs={{0,4},{2,6},{4,0},{6,2},{8,12},{10,14},{12,8},{14,10},{1,5},{3,7},... | collective-permute-start | bytes 442376 | tf_op jit(solution)/shard_map/ppermute | solution.py:101
  16.3 19.0 %all-to-all-done.refs_2_ = bf16[8,176,256]{2,1,0:T(8,128)(2,1)S(1)} async-done(((bf16[8,176,256]{2,1,0:T(8,128)(2,1)}), bf16[8,176,256]{2,1,0:T(8,128)(2,1)S(1)}, u32[]{:S(2)}, u32[]{:S(2)}) %all-to-all-start) | async-done | bytes 720928 | tf_op jit(solution)/shard_map/all_to_all | solution.py:113
  35.3 1.6 %collective-permute-start = (bf16[8,128,256]{2,1,0:T(8,128)(2,1)S(1)}, bf16[8,128,256]{2,1,0:T(8,128)(2,1)S(1)}, u32[]{:S(2)}, u32[]{:S(2)}) collective-permute-start(bf16[8,128,256]{2,1,0:T(8,128)(2,1)S(1)} %slice.14), channel_id=1, source_target_pairs={{0,16},{16,0},{1,17},{17,1},{2,18},{18,2},{3,19},{19,3},{4,20},{20... | collective-permute-start | bytes 1572872 | tf_op jit(solution)/shard_map/ppermute | solution.py:114
  36.9 1.1 %collective-permute-start.1 = (bf16[128,576]{1,0:T(8,128)(2,1)S(1)}, bf16[128,576]{1,0:T(8,128)(2,1)S(1)}, u32[]{:S(2)}, u32[]{:S(2)}) collective-permute-start(bf16[128,576]{1,0:T(8,128)(2,1)S(1)} %constant_dynamic-slice_fusion), channel_id=1, source_target_pairs={{0,2},{2,0},{4,6},{6,4},{8,10},{10,8},{12,14},{14,12},{1,3},{3,1},... | collective-permute-start | bytes 442376 | tf_op jit(solution)/shard_map/ppermute | solution.py:101
  37.9 0.0 collective-permute-done.7.refs_11_
  37.9 1.0 %collective-permute-start.9 = (bf16[128,576]{1,0:T(8,128)(2,1)S(1)}, bf16[128,576]{1,0:T(8,128)(2,1)S(1)}, u32[]{:S(2)}, u32[]{:S(2)}) collective-permute-start(bf16[128,576]{1,0:T(8,128)(2,1)S(1)} %collective-permute-done.7.refs_11_), channel_id=1, source_target_pairs={{0,2},{2,0},{4,6},{6,4},{8,10},{10,8},{12,14},{14,12},{1,3},{3,1},... | collective-permute-start | bytes 442376 | tf_op jit(solution)/shard_map/ppermute | solution.py:101
  38.9 0.0 collective-permute-start.11
  38.9 0.0 collective-permute-done.3.refs_7_
  38.9 1.1 %collective-permute-start.5 = (bf16[128,576]{1,0:T(8,128)(2,1)S(1)}, bf16[128,576]{1,0:T(8,128)(2,1)S(1)}, u32[]{:S(2)}, u32[]{:S(2)}) collective-permute-start(bf16[128,576]{1,0:T(8,128)(2,1)S(1)} %collective-permute-done.3.refs_7_), channel_id=1, source_target_pairs={{0,2},{2,0},{4,6},{6,4},{8,10},{10,8},{12,14},{14,12},{1,3},{3,1},... | collective-permute-start | bytes 442376 | tf_op jit(solution)/shard_map/ppermute | solution.py:101
  40.0 4.0 %collective-permute-done.1.refs_5_ = bf16[128,576]{1,0:T(8,128)(2,1)S(1)} collective-permute-done((bf16[128,576]{1,0:T(8,128)(2,1)S(1)}, bf16[128,576]{1,0:T(8,128)(2,1)S(1)}, u32[]{:S(2)}, u32[]{:S(2)}) %collective-permute-start.1) | collective-permute-done | bytes 147488 | tf_op jit(solution)/shard_map/ppermute | solution.py:101
  43.9 0.0 collective-permute-start.8
  43.9 1.8 %collective-permute-done.9.refs_13_ = bf16[128,576]{1,0:T(8,128)(2,1)S(1)} collective-permute-done((bf16[128,576]{1,0:T(8,128)(2,1)S(1)}, bf16[128,576]{1,0:T(8,128)(2,1)S(1)}, u32[]{:S(2)}, u32[]{:S(2)}) %collective-permute-start.9) | collective-permute-done | bytes 147488 | tf_op jit(solution)/shard_map/ppermute | solution.py:101
  45.7 0.0 collective-permute-start.4
  45.7 0.0 collective-permute-done.11.refs_15_
  45.7 0.5 collective-permute-start.2
  46.2 1.2 %collective-permute-done.5.refs_9_ = bf16[128,576]{1,0:T(8,128)(2,1)S(1)} collective-permute-done((bf16[128,576]{1,0:T(8,128)(2,1)S(1)}, bf16[128,576]{1,0:T(8,128)(2,1)S(1)}, u32[]{:S(2)}, u32[]{:S(2)}) %collective-permute-start.5) | collective-permute-done | bytes 147488 | tf_op jit(solution)/shard_map/ppermute | solution.py:101
  47.4 0.0 collective-permute-start.13
  47.5 0.0 collective-permute-done.8.refs_12_
  47.5 0.0 collective-permute-start.10
  47.5 0.0 collective-permute-done.4.refs_8_
  47.5 0.5 collective-permute-start.12
  48.0 0.0 collective-permute-done.2.refs_6_
  48.0 0.1 collective-permute-start.6
  48.1 4.7 %collective-permute-done.13.refs_17_ = bf16[128,576]{1,0:T(8,128)(2,1)S(1)} collective-permute-done((bf16[128,576]{1,0:T(8,128)(2,1)S(1)}, bf16[128,576]{1,0:T(8,128)(2,1)S(1)}, u32[]{:S(2)}, u32[]{:S(2)}) %collective-permute-start.13) | collective-permute-done | bytes 147488 | tf_op jit(solution)/shard_map/ppermute | solution.py:101
  52.8 0.0 collective-permute-start.14
  53.4 0.0 collective-permute-done.12.refs_16_
  53.4 0.0 collective-permute-done.6.refs_10_
  53.5 0.7 collective-permute-done.14.refs_18_
  54.2 0.0 collective-permute-done.refs_3_
  54.2 11.8 %attend.1 = bf16[128,512]{1,0:T(8,128)(2,1)S(1)} custom-call(s32[8]{0:T(128)S(1)} %copy-done, s32[1]{0:T(128)S(6)} %copy.14.refs_1_, bf16[8,176,256]{2,1,0:T(8,128)(2,1)S(1)} %all-to-all-done.refs_2_, bf16[8,128,256]{2,1,0:T(8,128)(2,1)S(1)} %collective-permute-done.refs_3_, bf16[256,576]{1,0:T(8,128)(2,1)S(1)} %copy.11.refs_4_, ...), custom_call_target="tpu_custom_call" | custom-call | tf_op jit(solution)/shard_map/attend/pallas_call | solution.py:130
  66.0 11.6 %all_to_all.10 = bf16[8,16,512]{2,1,0:T(8,128)(2,1)S(1)} all-to-all(bf16[8,16,512]{2,1,0:T(8,128)(2,1)S(1)} %bitcast.13), channel_id=1, replica_groups=mesh['groups'=2,'ctx'=8,'tp'=2] {'ctx'}, dimensions={0} | all-to-all | bytes 262144 | tf_op jit(solution)/shard_map/all_to_all | solution.py:144
  77.6 0.1 copy.13
  77.7 0.8 %broadcast_select_fusion.1 = bf16[8,16,2,2,128]{4,3,2,0,1:T(2,128)(2,1)} fusion(bf16[8,16,2,2,128]{4,3,2,0,1:T(2,128)(2,1)S(1)} %copy.13, pred[]{:T(512)S(6)} %eq.4), kind=kLoop, calls=%fused_computation.2 | loop fusion | flops 65536 | bytes 262145 | tf_op jit(solution)/shard_map/jit(_where)/select_n | solution.py:146
  (10 shorter events, 0.1 us)
Async XLA Ops:
  0.0 1.9 %copy-start.1 = (bf16[64,32,256]{2,1,0:T(8,128)(2,1)S(1)}, bf16[64,32,256]{2,1,0:T(8,128)(2,1)}, u32[]{:S(2)}) copy-start(bf16[64,32,256]{2,1,0:T(8,128)(2,1)} %param.7) | copy-start | bytes 3145732
  4.2 7.4 %copy-start.2 = (bf16[256,576]{0,1:T(8,128)(2,1)S(1)}, bf16[256,576]{0,1:T(8,128)(2,1)}, u32[]{:S(2)}) copy-start(bf16[256,576]{0,1:T(8,128)(2,1)} %param.6) | copy-start | bytes 884740
  4.2 31.1 %all-to-all-start = ((bf16[8,176,256]{2,1,0:T(8,128)(2,1)}), bf16[8,176,256]{2,1,0:T(8,128)(2,1)S(1)}, u32[]{:S(2)}, u32[]{:S(2)}) async-start(bf16[8,176,256]{2,1,0:T(8,128)(2,1)} %pad_maximum_fusion), calls=%async_computation | async-start | bytes 1441792 | tf_op jit(solution)/shard_map/all_to_all | solution.py:113
  11.6 42.6 %copy-start = (s32[8]{0:T(128)S(1)}, s32[8]{0:T(128)}, u32[]{:S(2)}) copy-start(s32[8]{0:T(128)} %refs_0_.1) | copy-start | bytes 100
  11.8 26.1 %collective-permute-start.7 = (bf16[128,576]{1,0:T(8,128)(2,1)S(1)}, bf16[128,576]{1,0:T(8,128)(2,1)S(1)}, u32[]{:S(2)}, u32[]{:S(2)}) collective-permute-start(bf16[128,576]{1,0:T(8,128)(2,1)S(1)} %constant_dynamic-slice_fusion), channel_id=1, source_target_pairs={{0,8},{2,10},{4,12},{6,14},{8,0},{10,2},{12,4},{14,6},{1,9},{3,11}... | collective-permute-start | bytes 442376 | tf_op jit(solution)/shard_map/ppermute | solution.py:101
  14.8 24.1 %collective-permute-start.3 = (bf16[128,576]{1,0:T(8,128)(2,1)S(1)}, bf16[128,576]{1,0:T(8,128)(2,1)S(1)}, u32[]{:S(2)}, u32[]{:S(2)}) collective-permute-start(bf16[128,576]{1,0:T(8,128)(2,1)S(1)} %constant_dynamic-slice_fusion), channel_id=1, source_target_pairs={{0,4},{2,6},{4,0},{6,2},{8,12},{10,14},{12,8},{14,10},{1,5},{3,7},... | collective-permute-start | bytes 442376 | tf_op jit(solution)/shard_map/ppermute | solution.py:101
  35.3 18.9 %collective-permute-start = (bf16[8,128,256]{2,1,0:T(8,128)(2,1)S(1)}, bf16[8,128,256]{2,1,0:T(8,128)(2,1)S(1)}, u32[]{:S(2)}, u32[]{:S(2)}) collective-permute-start(bf16[8,128,256]{2,1,0:T(8,128)(2,1)S(1)} %slice.14), channel_id=1, source_target_pairs={{0,16},{16,0},{1,17},{17,1},{2,18},{18,2},{3,19},{19,3},{4,20},{20... | collective-permute-start | bytes 1572872 | tf_op jit(solution)/shard_map/ppermute | solution.py:114
  36.9 7.1 %collective-permute-start.1 = (bf16[128,576]{1,0:T(8,128)(2,1)S(1)}, bf16[128,576]{1,0:T(8,128)(2,1)S(1)}, u32[]{:S(2)}, u32[]{:S(2)}) collective-permute-start(bf16[128,576]{1,0:T(8,128)(2,1)S(1)} %constant_dynamic-slice_fusion), channel_id=1, source_target_pairs={{0,2},{2,0},{4,6},{6,4},{8,10},{10,8},{12,14},{14,12},{1,3},{3,1},... | collective-permute-start | bytes 442376 | tf_op jit(solution)/shard_map/ppermute | solution.py:101
  37.9 7.8 %collective-permute-start.9 = (bf16[128,576]{1,0:T(8,128)(2,1)S(1)}, bf16[128,576]{1,0:T(8,128)(2,1)S(1)}, u32[]{:S(2)}, u32[]{:S(2)}) collective-permute-start(bf16[128,576]{1,0:T(8,128)(2,1)S(1)} %collective-permute-done.7.refs_11_), channel_id=1, source_target_pairs={{0,2},{2,0},{4,6},{6,4},{8,10},{10,8},{12,14},{14,12},{1,3},{3,1},... | collective-permute-start | bytes 442376 | tf_op jit(solution)/shard_map/ppermute | solution.py:101
  38.9 6.8 %collective-permute-start.11 = (bf16[128,576]{1,0:T(8,128)(2,1)S(1)}, bf16[128,576]{1,0:T(8,128)(2,1)S(1)}, u32[]{:S(2)}, u32[]{:S(2)}) collective-permute-start(bf16[128,576]{1,0:T(8,128)(2,1)S(1)} %collective-permute-done.7.refs_11_), channel_id=1, source_target_pairs={{0,4},{2,6},{4,0},{6,2},{8,12},{10,14},{12,8},{14,10},{1,5},{3,7},... | collective-permute-start | bytes 442376 | tf_op jit(solution)/shard_map/ppermute | solution.py:101
  38.9 8.5 %collective-permute-start.5 = (bf16[128,576]{1,0:T(8,128)(2,1)S(1)}, bf16[128,576]{1,0:T(8,128)(2,1)S(1)}, u32[]{:S(2)}, u32[]{:S(2)}) collective-permute-start(bf16[128,576]{1,0:T(8,128)(2,1)S(1)} %collective-permute-done.3.refs_7_), channel_id=1, source_target_pairs={{0,2},{2,0},{4,6},{6,4},{8,10},{10,8},{12,14},{14,12},{1,3},{3,1},... | collective-permute-start | bytes 442376 | tf_op jit(solution)/shard_map/ppermute | solution.py:101
  43.9 3.5 %collective-permute-start.8 = (bf16[128,576]{1,0:T(8,128)(2,1)S(1)}, bf16[128,576]{1,0:T(8,128)(2,1)S(1)}, u32[]{:S(2)}, u32[]{:S(2)}) collective-permute-start(bf16[128,576]{1,0:T(8,128)(2,1)S(1)} %collective-permute-done.7.refs_11_), channel_id=1, source_target_pairs={{0,1},{1,0},{2,3},{3,2},{4,5},{5,4},{6,7},{7,6},{8,9},{9,8},{10,11... | collective-permute-start | bytes 442376 | tf_op jit(solution)/shard_map/ppermute | solution.py:123
  45.7 1.8 %collective-permute-start.4 = (bf16[128,576]{1,0:T(8,128)(2,1)S(1)}, bf16[128,576]{1,0:T(8,128)(2,1)S(1)}, u32[]{:S(2)}, u32[]{:S(2)}) collective-permute-start(bf16[128,576]{1,0:T(8,128)(2,1)S(1)} %collective-permute-done.3.refs_7_), channel_id=1, source_target_pairs={{0,1},{1,0},{2,3},{3,2},{4,5},{5,4},{6,7},{7,6},{8,9},{9,8},{10,11... | collective-permute-start | bytes 442376 | tf_op jit(solution)/shard_map/ppermute | solution.py:123
  45.7 2.3 %collective-permute-start.2 = (bf16[128,576]{1,0:T(8,128)(2,1)S(1)}, bf16[128,576]{1,0:T(8,128)(2,1)S(1)}, u32[]{:S(2)}, u32[]{:S(2)}) collective-permute-start(bf16[128,576]{1,0:T(8,128)(2,1)S(1)} %collective-permute-done.1.refs_5_), channel_id=1, source_target_pairs={{0,1},{1,0},{2,3},{3,2},{4,5},{5,4},{6,7},{7,6},{8,9},{9,8},{10,11... | collective-permute-start | bytes 442376 | tf_op jit(solution)/shard_map/ppermute | solution.py:123
  47.4 5.3 %collective-permute-start.13 = (bf16[128,576]{1,0:T(8,128)(2,1)S(1)}, bf16[128,576]{1,0:T(8,128)(2,1)S(1)}, u32[]{:S(2)}, u32[]{:S(2)}) collective-permute-start(bf16[128,576]{1,0:T(8,128)(2,1)S(1)} %collective-permute-done.9.refs_13_), channel_id=1, source_target_pairs={{0,4},{2,6},{4,0},{6,2},{8,12},{10,14},{12,8},{14,10},{1,5},{3,7},... | collective-permute-start | bytes 442376 | tf_op jit(solution)/shard_map/ppermute | solution.py:101
  47.5 6.0 %collective-permute-start.10 = (bf16[128,576]{1,0:T(8,128)(2,1)S(1)}, bf16[128,576]{1,0:T(8,128)(2,1)S(1)}, u32[]{:S(2)}, u32[]{:S(2)}) collective-permute-start(bf16[128,576]{1,0:T(8,128)(2,1)S(1)} %collective-permute-done.9.refs_13_), channel_id=1, source_target_pairs={{0,1},{1,0},{2,3},{3,2},{4,5},{5,4},{6,7},{7,6},{8,9},{9,8},{10,11... | collective-permute-start | bytes 442376 | tf_op jit(solution)/shard_map/ppermute | solution.py:123
  47.5 6.0 %collective-permute-start.12 = (bf16[128,576]{1,0:T(8,128)(2,1)S(1)}, bf16[128,576]{1,0:T(8,128)(2,1)S(1)}, u32[]{:S(2)}, u32[]{:S(2)}) collective-permute-start(bf16[128,576]{1,0:T(8,128)(2,1)S(1)} %collective-permute-done.11.refs_15_), channel_id=1, source_target_pairs={{0,1},{1,0},{2,3},{3,2},{4,5},{5,4},{6,7},{7,6},{8,9},{9,8},{10,11... | collective-permute-start | bytes 442376 | tf_op jit(solution)/shard_map/ppermute | solution.py:123
  48.0 5.5 %collective-permute-start.6 = (bf16[128,576]{1,0:T(8,128)(2,1)S(1)}, bf16[128,576]{1,0:T(8,128)(2,1)S(1)}, u32[]{:S(2)}, u32[]{:S(2)}) collective-permute-start(bf16[128,576]{1,0:T(8,128)(2,1)S(1)} %collective-permute-done.5.refs_9_), channel_id=1, source_target_pairs={{0,1},{1,0},{2,3},{3,2},{4,5},{5,4},{6,7},{7,6},{8,9},{9,8},{10,11... | collective-permute-start | bytes 442376 | tf_op jit(solution)/shard_map/ppermute | solution.py:123
  52.8 1.4 %collective-permute-start.14 = (bf16[128,576]{1,0:T(8,128)(2,1)S(1)}, bf16[128,576]{1,0:T(8,128)(2,1)S(1)}, u32[]{:S(2)}, u32[]{:S(2)}) collective-permute-start(bf16[128,576]{1,0:T(8,128)(2,1)S(1)} %collective-permute-done.13.refs_17_), channel_id=1, source_target_pairs={{0,1},{1,0},{2,3},{3,2},{4,5},{5,4},{6,7},{7,6},{8,9},{9,8},{10,11... | collective-permute-start | bytes 442376 | tf_op jit(solution)/shard_map/ppermute | solution.py:123

commit v3 on v2

--- a/solution.py
+++ b/solution.py
@@ -13,7 +13,8 @@
 NOPE = 128
 VD = 128
 HIDDEN = -1e30
-ROUNDS = ((4, 0, 4), (2, 0, 2), (1, 0, 1), (3, 2, 1), (5, 4, 1), (6, 4, 2), (7, 5, 2))
+EARLY = ((4, 0, 4), (2, 0, 2), (1, 0, 1), (3, 0, 3))
+LATE = ((5, 4, 1), (6, 4, 2), (7, 4, 3))
 
 
 def attend_kernel(slots, rows, halves, pair, *refs):
@@ -111,11 +112,14 @@
     turned = turned.reshape(contexts, query_rows, heads * ROPE)
     packed = jnp.concatenate([weight, straight, turned], axis=1)
     packed = lax.all_to_all(packed, "ctx", 0, 0, tiled=True)
-    other = lax.ppermute(packed[:, :pair * depth], "groups", [(0, 1), (1, 0)])
-
     core = lax.axis_index("tp")
     held = {0: lax.dynamic_slice_in_dim(latent_cache, core * half, half, 0)}
-    for slot, source, bit in ROUNDS:
+    for slot, source, bit in EARLY:
+        held[slot] = swap(held[source], bit)
+    waited = lax.optimization_barrier((packed, held[1], held[2], held[3]))
+    packed, held[1], held[2], held[3] = waited
+    other = lax.ppermute(packed[:, :pair * depth], "groups", [(0, 1), (1, 0)])
+    for slot, source, bit in LATE:
         held[slot] = swap(held[source], bit)
     pieces = [latent_cache]
     for slot in range(1, contexts):
@@ -241,7 +245,7 @@
 
     def local(queries, latent_cache, kv_weight, block_order, span_start):
         arrays = (queries, latent_cache, kv_weight, block_order, span_start)
-        paired = queries.shape[1] % (2 * contexts) == 0 and contexts == len(ROUNDS) + 1
+        paired = queries.shape[1] % (2 * contexts) == 0 and contexts == 1 + len(EARLY) + len(LATE)
         if paired and cores == 2 and mesh.shape["groups"] == 2:
             return split_by_heads(contexts, cores, *arrays)
         return split_by_context(*arrays)

time: 78.8 us -> 74.2 us (0.942)
  waiting for transfers between devices: 31.4 us -> 24.7 us
  starting transfers between devices: 17.6 us -> 20.5 us
    all_to_all x1, waiting for transfers between devices: 19 us -> 0.01 us  [split_by_heads(): packed = lax.all_to_all(packed, 'ctx', 0, 0, tiled=True)]
    ppermute x7, waiting for transfers between devices: 11.7 us -> 24.2 us  [swap(): return lax.ppermute(array, 'ctx', [(i, i ^ bit) for i in range(contexts)])]
    ppermute x7, starting transfers between devices: 7.52 us -> 9.95 us  [swap(): return lax.ppermute(array, 'ctx', [(i, i ^ bit) for i in range(contexts)])]
  transfers between devices with their start and end apart: 16 -> 16, of which waited for: 6 -> 7; matrix products, arithmetic and copies ran while one was open for 0% -> 0% of each run, Pallas kernels for 0% -> 0%
where the time goes in v3:
time: 74.2 us; the launch traced here: 73.9 us
  waiting for transfers between devices  24.7 us (33%)
  starting transfers between devices  20.5 us (28%)
  Pallas kernels  11.8 us (16%)
  blocking collectives  10.9 us (15%)
  local copies, waits for them, and re-layouts  3.29 us (4%)
  other arithmetic  2.01 us (3%)
  between operations  0.82 us (1%)
    ppermute x7, waiting for transfers between devices, swap(): return lax.ppermute(array, 'ctx', [(i, i ^ bit) for i in range(contexts)])  24.2 us
    pallas_call x1, Pallas kernels, split_by_heads(): pl.pallas_call(functools.partial(attend_kernel, contexts, rows, cores, pa...  11.8 us
    all_to_all x1, blocking collectives, split_by_heads(): attended = lax.all_to_all(attended, 'ctx', 0, 0, tiled=True)  10.9 us
    ppermute x7, starting transfers between devices, swap(): return lax.ppermute(array, 'ctx', [(i, i ^ bit) for i in range(contexts)])  9.95 us
    all_to_all x1, starting transfers between devices, split_by_heads(): packed = lax.all_to_all(packed, 'ctx', 0, 0, tiled=True)  7.38 us
    ppermute x1, starting transfers between devices, split_by_heads(): other = lax.ppermute(packed[:, :pair * depth], 'groups', [(0, 1), (1, 0)])  1.58 us
    ppermute x7, starting transfers between devices, split_by_heads(): pieces.append(lax.ppermute(held[slot], 'tp', [(0, 1), (1, 0)]))  1.53 us
  transfers between devices with their start and end apart: 16, of which 7 were waited for; matrix products, arithmetic and copies ran while one was open for 0% of the time, Pallas kernels for 0%

profile of v3, /device:TPU:0, one launch (start us, length us, event | category | flops | bytes accessed | tf_op | source)
XLA Modules:
  0.0 73.9 jit_solution(7431241127123361061)
XLA Ops:
  0.0 1.2 %reshape.26 = bf16[16,8,2,2,192]{4,3,2,1,0:T(2,128)(2,1)S(1)} reshape(bf16[16,32,192]{2,1,0:T(8,128)(2,1)} %param.5) | data formatting | bytes 393216 | tf_op jit(solution)/shard_map/reshape | solution.py:107
  1.2 0.2 copy.8
  1.4 0.3 broadcast_select_fusion
  1.7 0.1 slice_bitcast_fusion.1
  1.8 0.1 slice_bitcast_fusion
  1.9 0.4 reshape.24
  2.3 0.4 constant_dynamic-slice_fusion.1
  2.7 0.2 copy.6
  2.9 0.1 copy.9
  3.0 0.1 reshape.27
  3.1 0.1 reshape.28
  3.3 0.9 %pad_maximum_fusion = bf16[8,176,256]{2,1,0:T(8,128)(2,1)} fusion(bf16[8,16,256]{2,1,0:T(8,128)(2,1)S(1)} %reshape.28, bf16[8,32,256]{2,1,0:T(8,128)(2,1)S(1)} %reshape.27, bf16[8,128,256]{2,1,0:T(8,128)(2,1)S(1)} %bitcast.14), kind=kLoop, calls=%fused_computation | loop fusion | flops 2162688 | bytes 1441792 | tf_op jit(solution)/shard_map/concatenate | solution.py:113
  4.2 7.4 %all-to-all-start = ((bf16[8,176,256]{2,1,0:T(8,128)(2,1)}), bf16[8,176,256]{2,1,0:T(8,128)(2,1)S(1)}, u32[]{:S(2)}, u32[]{:S(2)}) async-start(bf16[8,176,256]{2,1,0:T(8,128)(2,1)} %pad_maximum_fusion), calls=%async_computation | async-start | bytes 1441792 | tf_op jit(solution)/shard_map/all_to_all | solution.py:114
  11.6 0.2 copy.10.refs_4_
  11.8 2.1 %collective-permute-start = (bf16[128,576]{1,0:T(8,128)(2,1)S(1)}, bf16[128,576]{1,0:T(8,128)(2,1)S(1)}, u32[]{:S(2)}, u32[]{:S(2)}) collective-permute-start(bf16[128,576]{1,0:T(8,128)(2,1)S(1)} %constant_dynamic-slice_fusion), channel_id=1, source_target_pairs={{0,2},{2,0},{4,6},{6,4},{8,10},{10,8},{12,14},{14,12},{1,3},{3,1},... | collective-permute-start | bytes 442376 | tf_op jit(solution)/shard_map/ppermute | solution.py:102
  13.9 1.5 %collective-permute-start.1 = (bf16[128,576]{1,0:T(8,128)(2,1)S(1)}, bf16[128,576]{1,0:T(8,128)(2,1)S(1)}, u32[]{:S(2)}, u32[]{:S(2)}) collective-permute-start(bf16[128,576]{1,0:T(8,128)(2,1)S(1)} %constant_dynamic-slice_fusion), channel_id=1, source_target_pairs={{0,4},{2,6},{4,0},{6,2},{8,12},{10,14},{12,8},{14,10},{1,5},{3,7},... | collective-permute-start | bytes 442376 | tf_op jit(solution)/shard_map/ppermute | solution.py:102
  15.4 0.1 collective-permute-start.2
  15.4 2.8 %collective-permute-start.7 = (bf16[128,576]{1,0:T(8,128)(2,1)S(1)}, bf16[128,576]{1,0:T(8,128)(2,1)S(1)}, u32[]{:S(2)}, u32[]{:S(2)}) collective-permute-start(bf16[128,576]{1,0:T(8,128)(2,1)S(1)} %constant_dynamic-slice_fusion), channel_id=1, source_target_pairs={{0,8},{2,10},{4,12},{6,14},{8,0},{10,2},{12,4},{14,6},{1,9},{3,11}... | collective-permute-start | bytes 442376 | tf_op jit(solution)/shard_map/ppermute | solution.py:102
  18.3 5.1 %collective-permute-done.refs_5_ = bf16[128,576]{1,0:T(8,128)(2,1)S(1)} collective-permute-done((bf16[128,576]{1,0:T(8,128)(2,1)S(1)}, bf16[128,576]{1,0:T(8,128)(2,1)S(1)}, u32[]{:S(2)}, u32[]{:S(2)}) %collective-permute-start) | collective-permute-done | bytes 147488 | tf_op jit(solution)/shard_map/ppermute | solution.py:102
  23.4 9.9 %collective-permute-done.1.refs_7_ = bf16[128,576]{1,0:T(8,128)(2,1)S(1)} collective-permute-done((bf16[128,576]{1,0:T(8,128)(2,1)S(1)}, bf16[128,576]{1,0:T(8,128)(2,1)S(1)}, u32[]{:S(2)}, u32[]{:S(2)}) %collective-permute-start.1) | collective-permute-done | bytes 147488 | tf_op jit(solution)/shard_map/ppermute | solution.py:102
  33.2 3.7 %collective-permute-done.2.refs_9_ = bf16[128,576]{1,0:T(8,128)(2,1)S(1)} collective-permute-done((bf16[128,576]{1,0:T(8,128)(2,1)S(1)}, bf16[128,576]{1,0:T(8,128)(2,1)S(1)}, u32[]{:S(2)}, u32[]{:S(2)}) %collective-permute-start.2) | collective-permute-done | bytes 147488 | tf_op jit(solution)/shard_map/ppermute | solution.py:102
  36.9 0.0 all-to-all-done.refs_2_
  37.0 1.6 %collective-permute-start.3 = (bf16[8,128,256]{2,1,0:T(8,128)(2,1)S(1)}, bf16[8,128,256]{2,1,0:T(8,128)(2,1)S(1)}, u32[]{:S(2)}, u32[]{:S(2)}) collective-permute-start(bf16[8,128,256]{2,1,0:T(8,128)(2,1)S(1)} %slice.11), channel_id=1, source_target_pairs={{0,16},{16,0},{1,17},{17,1},{2,18},{18,2},{3,19},{19,3},{4,20},{20... | collective-permute-start | bytes 1572872 | tf_op jit(solution)/shard_map/ppermute | solution.py:121
  38.6 0.0 collective-permute-done.7.refs_11_
  38.6 0.6 collective-permute-start.9
  39.1 0.8 %collective-permute-start.11 = (bf16[128,576]{1,0:T(8,128)(2,1)S(1)}, bf16[128,576]{1,0:T(8,128)(2,1)S(1)}, u32[]{:S(2)}, u32[]{:S(2)}) collective-permute-start(bf16[128,576]{1,0:T(8,128)(2,1)S(1)} %collective-permute-done.7.refs_11_), channel_id=1, source_target_pairs={{0,4},{2,6},{4,0},{6,2},{8,12},{10,14},{12,8},{14,10},{1,5},{3,7},... | collective-permute-start | bytes 442376 | tf_op jit(solution)/shard_map/ppermute | solution.py:102
  39.9 2.1 %collective-permute-start.13 = (bf16[128,576]{1,0:T(8,128)(2,1)S(1)}, bf16[128,576]{1,0:T(8,128)(2,1)S(1)}, u32[]{:S(2)}, u32[]{:S(2)}) collective-permute-start(bf16[128,576]{1,0:T(8,128)(2,1)S(1)} %collective-permute-done.7.refs_11_), channel_id=1, source_target_pairs={{0,6},{2,4},{4,2},{6,0},{8,14},{10,12},{12,10},{14,8},{1,7},{3,5},... | collective-permute-start | bytes 442376 | tf_op jit(solution)/shard_map/ppermute | solution.py:102
  42.1 0.0 collective-permute-start.8
  42.1 3.6 %collective-permute-done.9.refs_13_ = bf16[128,576]{1,0:T(8,128)(2,1)S(1)} collective-permute-done((bf16[128,576]{1,0:T(8,128)(2,1)S(1)}, bf16[128,576]{1,0:T(8,128)(2,1)S(1)}, u32[]{:S(2)}, u32[]{:S(2)}) %collective-permute-start.9) | collective-permute-done | bytes 147488 | tf_op jit(solution)/shard_map/ppermute | solution.py:102
  45.7 0.0 collective-permute-start.10
  45.7 0.0 collective-permute-done.11.refs_15_
  45.7 0.5 collective-permute-start.12
  46.2 2.0 %collective-permute-done.13.refs_17_ = bf16[128,576]{1,0:T(8,128)(2,1)S(1)} collective-permute-done((bf16[128,576]{1,0:T(8,128)(2,1)S(1)}, bf16[128,576]{1,0:T(8,128)(2,1)S(1)}, u32[]{:S(2)}, u32[]{:S(2)}) %collective-permute-start.13) | collective-permute-done | bytes 147488 | tf_op jit(solution)/shard_map/ppermute | solution.py:102
  48.2 0.0 collective-permute-start.14
  48.2 0.0 collective-permute-done.8.refs_12_
  48.2 0.5 collective-permute-start.4
  48.7 0.0 collective-permute-done.10.refs_14_
  48.7 0.1 collective-permute-start.5
  48.7 0.0 collective-permute-done.12.refs_16_
  48.8 0.4 collective-permute-start.6
  49.8 0.0 collective-permute-done.14.refs_18_
  49.9 0.0 collective-permute-done.4.refs_6_
  49.9 0.2 collective-permute-done.5.refs_8_
  50.1 0.2 collective-permute-done.6.refs_10_
  50.3 11.8 %attend.1 = bf16[128,512]{1,0:T(8,128)(2,1)S(1)} custom-call(s32[8]{0:T(128)S(1)} %copy-done, s32[1]{0:T(128)S(6)} %copy.14.refs_1_, bf16[8,176,256]{2,1,0:T(8,128)(2,1)S(1)} %all-to-all-done.refs_2_, bf16[8,128,256]{2,1,0:T(8,128)(2,1)S(1)} %collective-permute-done.3.refs_3_, bf16[256,576]{1,0:T(8,128)(2,1)S(1)} %copy.10.refs_4_, ...), custom_call_target="tpu_custom_call" | custom-call | tf_op jit(solution)/shard_map/attend/pallas_call | solution.py:134
  62.1 10.9 %all_to_all.10 = bf16[8,16,512]{2,1,0:T(8,128)(2,1)S(1)} all-to-all(bf16[8,16,512]{2,1,0:T(8,128)(2,1)S(1)} %bitcast.13), channel_id=1, replica_groups=mesh['groups'=2,'ctx'=8,'tp'=2] {'ctx'}, dimensions={0} | all-to-all | bytes 262144 | tf_op jit(solution)/shard_map/all_to_all | solution.py:148
  73.0 0.1 copy.13
  73.1 0.8 %broadcast_select_fusion.1 = bf16[8,16,2,2,128]{4,3,2,0,1:T(2,128)(2,1)} fusion(bf16[8,16,2,2,128]{4,3,2,0,1:T(2,128)(2,1)S(1)} %copy.13, pred[]{:T(512)S(6)} %eq.4), kind=kLoop, calls=%fused_computation.2 | loop fusion | flops 65536 | bytes 262145 | tf_op jit(solution)/shard_map/jit(_where)/select_n | solution.py:150
  (10 shorter events, 0.1 us)
Async XLA Ops:
  0.0 1.9 %copy-start.1 = (bf16[64,32,256]{2,1,0:T(8,128)(2,1)S(1)}, bf16[64,32,256]{2,1,0:T(8,128)(2,1)}, u32[]{:S(2)}) copy-start(bf16[64,32,256]{2,1,0:T(8,128)(2,1)} %param.7) | copy-start | bytes 3145732
  4.2 7.4 %copy-start.2 = (bf16[256,576]{0,1:T(8,128)(2,1)S(1)}, bf16[256,576]{0,1:T(8,128)(2,1)}, u32[]{:S(2)}) copy-start(bf16[256,576]{0,1:T(8,128)(2,1)} %param.6) | copy-start | bytes 884740
  4.2 32.8 %all-to-all-start = ((bf16[8,176,256]{2,1,0:T(8,128)(2,1)}), bf16[8,176,256]{2,1,0:T(8,128)(2,1)S(1)}, u32[]{:S(2)}, u32[]{:S(2)}) async-start(bf16[8,176,256]{2,1,0:T(8,128)(2,1)} %pad_maximum_fusion), calls=%async_computation | async-start | bytes 1441792 | tf_op jit(solution)/shard_map/all_to_all | solution.py:114
  11.6 38.7 %copy-start = (s32[8]{0:T(128)S(1)}, s32[8]{0:T(128)}, u32[]{:S(2)}) copy-start(s32[8]{0:T(128)} %refs_0_.1) | copy-start | bytes 100
  11.8 11.5 %collective-permute-start = (bf16[128,576]{1,0:T(8,128)(2,1)S(1)}, bf16[128,576]{1,0:T(8,128)(2,1)S(1)}, u32[]{:S(2)}, u32[]{:S(2)}) collective-permute-start(bf16[128,576]{1,0:T(8,128)(2,1)S(1)} %constant_dynamic-slice_fusion), channel_id=1, source_target_pairs={{0,2},{2,0},{4,6},{6,4},{8,10},{10,8},{12,14},{14,12},{1,3},{3,1},... | collective-permute-start | bytes 442376 | tf_op jit(solution)/shard_map/ppermute | solution.py:102
  13.9 19.3 %collective-permute-start.1 = (bf16[128,576]{1,0:T(8,128)(2,1)S(1)}, bf16[128,576]{1,0:T(8,128)(2,1)S(1)}, u32[]{:S(2)}, u32[]{:S(2)}) collective-permute-start(bf16[128,576]{1,0:T(8,128)(2,1)S(1)} %constant_dynamic-slice_fusion), channel_id=1, source_target_pairs={{0,4},{2,6},{4,0},{6,2},{8,12},{10,14},{12,8},{14,10},{1,5},{3,7},... | collective-permute-start | bytes 442376 | tf_op jit(solution)/shard_map/ppermute | solution.py:102
  15.4 21.6 %collective-permute-start.2 = (bf16[128,576]{1,0:T(8,128)(2,1)S(1)}, bf16[128,576]{1,0:T(8,128)(2,1)S(1)}, u32[]{:S(2)}, u32[]{:S(2)}) collective-permute-start(bf16[128,576]{1,0:T(8,128)(2,1)S(1)} %constant_dynamic-slice_fusion), channel_id=1, source_target_pairs={{0,6},{2,4},{4,2},{6,0},{8,14},{10,12},{12,10},{14,8},{1,7},{3,5},... | collective-permute-start | bytes 442376 | tf_op jit(solution)/shard_map/ppermute | solution.py:102
  15.4 23.1 %collective-permute-start.7 = (bf16[128,576]{1,0:T(8,128)(2,1)S(1)}, bf16[128,576]{1,0:T(8,128)(2,1)S(1)}, u32[]{:S(2)}, u32[]{:S(2)}) collective-permute-start(bf16[128,576]{1,0:T(8,128)(2,1)S(1)} %constant_dynamic-slice_fusion), channel_id=1, source_target_pairs={{0,8},{2,10},{4,12},{6,14},{8,0},{10,2},{12,4},{14,6},{1,9},{3,11}... | collective-permute-start | bytes 442376 | tf_op jit(solution)/shard_map/ppermute | solution.py:102
  37.0 13.3 %collective-permute-start.3 = (bf16[8,128,256]{2,1,0:T(8,128)(2,1)S(1)}, bf16[8,128,256]{2,1,0:T(8,128)(2,1)S(1)}, u32[]{:S(2)}, u32[]{:S(2)}) collective-permute-start(bf16[8,128,256]{2,1,0:T(8,128)(2,1)S(1)} %slice.11), channel_id=1, source_target_pairs={{0,16},{16,0},{1,17},{17,1},{2,18},{18,2},{3,19},{19,3},{4,20},{20... | collective-permute-start | bytes 1572872 | tf_op jit(solution)/shard_map/ppermute | solution.py:121
  38.6 7.1 %collective-permute-start.9 = (bf16[128,576]{1,0:T(8,128)(2,1)S(1)}, bf16[128,576]{1,0:T(8,128)(2,1)S(1)}, u32[]{:S(2)}, u32[]{:S(2)}) collective-permute-start(bf16[128,576]{1,0:T(8,128)(2,1)S(1)} %collective-permute-done.7.refs_11_), channel_id=1, source_target_pairs={{0,2},{2,0},{4,6},{6,4},{8,10},{10,8},{12,14},{14,12},{1,3},{3,1},... | collective-permute-start | bytes 442376 | tf_op jit(solution)/shard_map/ppermute | solution.py:102
  39.1 6.5 %collective-permute-start.11 = (bf16[128,576]{1,0:T(8,128)(2,1)S(1)}, bf16[128,576]{1,0:T(8,128)(2,1)S(1)}, u32[]{:S(2)}, u32[]{:S(2)}) collective-permute-start(bf16[128,576]{1,0:T(8,128)(2,1)S(1)} %collective-permute-done.7.refs_11_), channel_id=1, source_target_pairs={{0,4},{2,6},{4,0},{6,2},{8,12},{10,14},{12,8},{14,10},{1,5},{3,7},... | collective-permute-start | bytes 442376 | tf_op jit(solution)/shard_map/ppermute | solution.py:102
  39.9 8.2 %collective-permute-start.13 = (bf16[128,576]{1,0:T(8,128)(2,1)S(1)}, bf16[128,576]{1,0:T(8,128)(2,1)S(1)}, u32[]{:S(2)}, u32[]{:S(2)}) collective-permute-start(bf16[128,576]{1,0:T(8,128)(2,1)S(1)} %collective-permute-done.7.refs_11_), channel_id=1, source_target_pairs={{0,6},{2,4},{4,2},{6,0},{8,14},{10,12},{12,10},{14,8},{1,7},{3,5},... | collective-permute-start | bytes 442376 | tf_op jit(solution)/shard_map/ppermute | solution.py:102
  42.1 6.1 %collective-permute-start.8 = (bf16[128,576]{1,0:T(8,128)(2,1)S(1)}, bf16[128,576]{1,0:T(8,128)(2,1)S(1)}, u32[]{:S(2)}, u32[]{:S(2)}) collective-permute-start(bf16[128,576]{1,0:T(8,128)(2,1)S(1)} %collective-permute-done.7.refs_11_), channel_id=1, source_target_pairs={{0,1},{1,0},{2,3},{3,2},{4,5},{5,4},{6,7},{7,6},{8,9},{9,8},{10,11... | collective-permute-start | bytes 442376 | tf_op jit(solution)/shard_map/ppermute | solution.py:127
  45.7 3.0 %collective-permute-start.10 = (bf16[128,576]{1,0:T(8,128)(2,1)S(1)}, bf16[128,576]{1,0:T(8,128)(2,1)S(1)}, u32[]{:S(2)}, u32[]{:S(2)}) collective-permute-start(bf16[128,576]{1,0:T(8,128)(2,1)S(1)} %collective-permute-done.9.refs_13_), channel_id=1, source_target_pairs={{0,1},{1,0},{2,3},{3,2},{4,5},{5,4},{6,7},{7,6},{8,9},{9,8},{10,11... | collective-permute-start | bytes 442376 | tf_op jit(solution)/shard_map/ppermute | solution.py:127
  45.7 3.1 %collective-permute-start.12 = (bf16[128,576]{1,0:T(8,128)(2,1)S(1)}, bf16[128,576]{1,0:T(8,128)(2,1)S(1)}, u32[]{:S(2)}, u32[]{:S(2)}) collective-permute-start(bf16[128,576]{1,0:T(8,128)(2,1)S(1)} %collective-permute-done.11.refs_15_), channel_id=1, source_target_pairs={{0,1},{1,0},{2,3},{3,2},{4,5},{5,4},{6,7},{7,6},{8,9},{9,8},{10,11... | collective-permute-start | bytes 442376 | tf_op jit(solution)/shard_map/ppermute | solution.py:127
  48.2 1.7 %collective-permute-start.14 = (bf16[128,576]{1,0:T(8,128)(2,1)S(1)}, bf16[128,576]{1,0:T(8,128)(2,1)S(1)}, u32[]{:S(2)}, u32[]{:S(2)}) collective-permute-start(bf16[128,576]{1,0:T(8,128)(2,1)S(1)} %collective-permute-done.13.refs_17_), channel_id=1, source_target_pairs={{0,1},{1,0},{2,3},{3,2},{4,5},{5,4},{6,7},{7,6},{8,9},{9,8},{10,11... | collective-permute-start | bytes 442376 | tf_op jit(solution)/shard_map/ppermute | solution.py:127
  48.2 1.7 %collective-permute-start.4 = (bf16[128,576]{1,0:T(8,128)(2,1)S(1)}, bf16[128,576]{1,0:T(8,128)(2,1)S(1)}, u32[]{:S(2)}, u32[]{:S(2)}) collective-permute-start(bf16[128,576]{1,0:T(8,128)(2,1)S(1)} %collective-permute-done.refs_5_), channel_id=1, source_target_pairs={{0,1},{1,0},{2,3},{3,2},{4,5},{5,4},{6,7},{7,6},{8,9},{9,8},{10,11... | collective-permute-start | bytes 442376 | tf_op jit(solution)/shard_map/ppermute | solution.py:127
  48.7 1.4 %collective-permute-start.5 = (bf16[128,576]{1,0:T(8,128)(2,1)S(1)}, bf16[128,576]{1,0:T(8,128)(2,1)S(1)}, u32[]{:S(2)}, u32[]{:S(2)}) collective-permute-start(bf16[128,576]{1,0:T(8,128)(2,1)S(1)} %collective-permute-done.1.refs_7_), channel_id=1, source_target_pairs={{0,1},{1,0},{2,3},{3,2},{4,5},{5,4},{6,7},{7,6},{8,9},{9,8},{10,11... | collective-permute-start | bytes 442376 | tf_op jit(solution)/shard_map/ppermute | solution.py:127
  48.8 1.6 %collective-permute-start.6 = (bf16[128,576]{1,0:T(8,128)(2,1)S(1)}, bf16[128,576]{1,0:T(8,128)(2,1)S(1)}, u32[]{:S(2)}, u32[]{:S(2)}) collective-permute-start(bf16[128,576]{1,0:T(8,128)(2,1)S(1)} %collective-permute-done.2.refs_9_), channel_id=1, source_target_pairs={{0,1},{1,0},{2,3},{3,2},{4,5},{5,4},{6,7},{7,6},{8,9},{9,8},{10,11... | collective-permute-start | bytes 442376 | tf_op jit(solution)/shard_map/ppermute | solution.py:127

commit v4 on v3

--- a/solution.py
+++ b/solution.py
@@ -13,38 +13,45 @@
 NOPE = 128
 VD = 128
 HIDDEN = -1e30
-EARLY = ((4, 0, 4), (2, 0, 2), (1, 0, 1), (3, 0, 3))
-LATE = ((5, 4, 1), (6, 4, 2), (7, 4, 3))
-
-
-def attend_kernel(slots, rows, halves, pair, *refs):
-    order_ref, start_ref, packed_ref, other_ref = refs[:4]
-    piece_refs = refs[4: 5 + 2 * (slots - 1)]
-    out_ref, latent, keys, sems = refs[5 + 2 * (slots - 1):]
-    half = rows // halves
+CHUNK = 512
+EARLY = ((4, 0, 4), (1, 0, 1), (2, 0, 2))
+LATE = ((3, 2, 1), (5, 4, 1), (6, 4, 2), (7, 5, 2))
+
+
+def attend_kernel(slots, rows, pair, which, *refs):
+    order_ref, start_ref, packed_ref = refs[:3]
+    if which == 0:
+        weight_ref = packed_ref
+        refs = refs[3:]
+    else:
+        weight_ref, done_ref = refs[3:5]
+        refs = refs[5:]
+    piece_refs = refs[:5]
+    out_ref, latent, keys, values, sems = refs[5:]
+    near = slots // 2
     me = lax.axis_index("ctx")
     core = lax.axis_index("tp")
-    copies = [pltpu.make_async_copy(piece_refs[0], latent.at[pl.ds(0, rows)], sems.at[0])]
-    for slot in range(1, slots):
-        for which in range(2):
-            at = core if which == 0 else 1 - core
-            place = pl.multiple_of(slot * rows + at * half, half)
-            index = 2 * slot - 1 + which
-            copies.append(
-                pltpu.make_async_copy(
-                    piece_refs[index], latent.at[pl.ds(place, half)], sems.at[index]
-                )
-            )
+    places = [
+        latent.at[0],
+        latent.at[pl.ds(1, near - 1), core],
+        latent.at[pl.ds(1, near - 1), 1 - core],
+        latent.at[pl.ds(near, near), core],
+        latent.at[pl.ds(near, near), 1 - core],
+    ]
+    copies = [
+        pltpu.make_async_copy(piece, place, sems.at[index])
+        for index, (piece, place) in enumerate(zip(piece_refs, places))
+    ]
     for copy in copies:
         copy.start()
     for copy in copies:
         copy.wait()
     width = NOPE + VD
-    depth = other_ref.shape[1] // pair
+    depth = LAT // slots
     query_rows = (packed_ref.shape[1] - pair * depth) // 3
     query_count = slots * query_rows
     scale = math.log2(math.e) / math.sqrt(NOPE + ROPE)
-    rope = latent[:, LAT:]
+    rope = latent[..., LAT:].reshape(slots * rows, ROPE)
     tail = jnp.concatenate([rope, jnp.zeros_like(rope)], axis=1)
     for buffer in range(2):
         keys[buffer, :, NOPE:] = tail
@@ -53,15 +60,23 @@
     )
     limits = [start_ref[0] - order_ref[me ^ slot] * rows for slot in range(slots)]
     first = pair * depth
-    for head in range(2 * pair):
-        buffer = head % 2
-        which, member = divmod(head, pair)
-        weight_ref = packed_ref if which == 0 else other_ref
+    place = 0
+    if which == 1:
+        group = lax.axis_index("groups")
+        out_ref[:, pl.ds(pl.multiple_of(group * pair * VD, pair * VD), pair * VD)] = done_ref[...]
+        place = pl.multiple_of((1 - group) * pair * VD, pair * VD)
+    results = []
+    for member in range(pair):
+        head = which * pair + member
+        buffer = member % 2
         weight = weight_ref[:, member * depth:(member + 1) * depth, :].reshape(LAT, width)
-        key_value = jnp.dot(latent[:, :LAT], weight, preferred_element_type=jnp.float32)
-        key_value = key_value.astype(jnp.bfloat16)
-        keys[buffer, :, :NOPE] = key_value[:, :NOPE]
-        values = key_value[:, NOPE:]
+        for begin in range(0, slots * rows, CHUNK):
+            part = pl.ds(begin, CHUNK)
+            held = latent[begin // rows:(begin + CHUNK) // rows, :, :, :LAT].reshape(CHUNK, LAT)
+            projected = jnp.dot(held, weight, preferred_element_type=jnp.float32)
+            projected = projected.astype(jnp.bfloat16)
+            keys[buffer, part, :NOPE] = projected[:, :NOPE]
+            values[buffer, part, :] = projected[:, NOPE:]
         begin = first + which * query_rows
         part = packed_ref[:, begin:begin + query_rows, member * NOPE:(member + 1) * NOPE]
         part = part.reshape(query_count, NOPE)
@@ -84,8 +99,9 @@
         top = jnp.max(scores, axis=1, keepdims=True)
         probs = jnp.exp2((scores - top) * scale)
         totals = jnp.sum(probs, axis=1, keepdims=True)
-        result = jnp.dot(probs.astype(jnp.bfloat16), values, preferred_element_type=jnp.float32)
-        out_ref[:, head * VD:(head + 1) * VD] = (result / totals).astype(jnp.bfloat16)
+        result = jnp.dot(probs.astype(jnp.bfloat16), values[buffer], preferred_element_type=jnp.float32)
+        results.append((result / totals).astype(jnp.bfloat16))
+    out_ref[:, pl.ds(place, pair * VD)] = jnp.concatenate(results, axis=1)
 
 
 def split_by_heads(contexts, cores, queries, latent_cache, kv_weight, block_order, span_start):
@@ -111,44 +127,57 @@
     turned = query[..., NOPE:].transpose(1, 0, 2, 3, 4)
     turned = turned.reshape(contexts, query_rows, heads * ROPE)
     packed = jnp.concatenate([weight, straight, turned], axis=1)
-    packed = lax.all_to_all(packed, "ctx", 0, 0, tiled=True)
+    def trade(array):
+        return lax.ppermute(array, "tp", [(0, 1), (1, 0)])
+
     core = lax.axis_index("tp")
     held = {0: lax.dynamic_slice_in_dim(latent_cache, core * half, half, 0)}
     for slot, source, bit in EARLY:
         held[slot] = swap(held[source], bit)
-    waited = lax.optimization_barrier((packed, held[1], held[2], held[3]))
-    packed, held[1], held[2], held[3] = waited
-    other = lax.ppermute(packed[:, :pair * depth], "groups", [(0, 1), (1, 0)])
+    waited = lax.optimization_barrier((packed, latent_cache, held[4], held[1], held[2]))
+    packed, latent_cache, held[4], held[1], held[2] = waited
+    packed = lax.all_to_all(packed, "ctx", 0, 0, tiled=True)
     for slot, source, bit in LATE:
         held[slot] = swap(held[source], bit)
-    pieces = [latent_cache]
-    for slot in range(1, contexts):
-        pieces.append(held[slot])
-        pieces.append(lax.ppermute(held[slot], "tp", [(0, 1), (1, 0)]))
+    near = contexts // 2
+    close = jnp.stack([held[slot] for slot in range(1, near)])
+    waited = lax.optimization_barrier((packed, held[3], held[5], held[6]))
+    packed, held[3], held[5], held[6] = waited
+    other = lax.ppermute(packed[:, :pair * depth], "groups", [(0, 1), (1, 0)])
+    far = jnp.stack([held[slot] for slot in range(near, contexts)])
+    own = latent_cache.reshape(cores, half, latent_cache.shape[1])
+    close_other = jnp.stack([trade(held[slot]) for slot in range(1, near)])
+    far_other = jnp.stack([trade(held[slot]) for slot in range(near, contexts)])
+    pieces = [own, close, close_other, far, far_other]
 
     total_rows = contexts * rows
     query_count = contexts * query_rows
     anywhere = pl.BlockSpec(memory_space=pl.ANY)
     on_chip = pl.BlockSpec(memory_space=pltpu.VMEM)
     scalars = pl.BlockSpec(memory_space=pltpu.SMEM)
-    attended = pl.pallas_call(
-        functools.partial(attend_kernel, contexts, rows, cores, pair),
-        out_shape=jax.ShapeDtypeStruct((query_count, heads * VD), jnp.bfloat16),
-        in_specs=[scalars, scalars, on_chip, on_chip] + [anywhere] * len(pieces),
-        out_specs=on_chip,
-        scratch_shapes=[
-            pltpu.VMEM((total_rows, LAT + ROPE), jnp.bfloat16),
-            pltpu.VMEM((2, total_rows, 256), jnp.bfloat16),
-            pltpu.SemaphoreType.DMA((len(pieces),)),
-        ],
-        compiler_params=pltpu.CompilerParams(vmem_limit_bytes=48 * 2**20),
-        name="attend",
-    )(block_order, span_start, packed, other, *pieces)
+
+    def attend(which, out_heads, operands):
+        return pl.pallas_call(
+            functools.partial(attend_kernel, contexts, rows, pair, which),
+            out_shape=jax.ShapeDtypeStruct((query_count, out_heads * VD), jnp.bfloat16),
+            in_specs=[scalars, scalars] + [on_chip] * len(operands) + [anywhere] * len(pieces),
+            out_specs=on_chip,
+            scratch_shapes=[
+                pltpu.VMEM((contexts, cores, half, LAT + ROPE), jnp.bfloat16),
+                pltpu.VMEM((2, total_rows, 256), jnp.bfloat16),
+                pltpu.VMEM((2, total_rows, VD), jnp.bfloat16),
+                pltpu.SemaphoreType.DMA((len(pieces),)),
+            ],
+            compiler_params=pltpu.CompilerParams(vmem_limit_bytes=16 * 2**20),
+            cost_estimate=pl.CostEstimate(flops=1048576, bytes_accessed=1 << 20, transcendentals=0),
+            name="attend_" + ("first", "second")[which],
+        )(block_order, span_start, *operands, *pieces)
+
+    attended = attend(0, pair, [packed])
+    attended = attend(1, heads, [packed, other, attended])
     attended = attended.reshape(contexts, query_rows, heads * VD)
     attended = lax.all_to_all(attended, "ctx", 0, 0, tiled=True)
-    attended = attended.reshape(contexts, query_rows, 2, pair, VD)
-    attended = jnp.where(group == 0, attended, attended[:, :, ::-1])
-    attended = attended.transpose(1, 0, 2, 3, 4)
+    attended = attended.reshape(contexts, query_rows, heads, VD).transpose(1, 0, 2, 3)
     return attended.reshape(query_rows, head_count, VD)
 
 
@@ -245,7 +274,7 @@
 
     def local(queries, latent_cache, kv_weight, block_order, span_start):
         arrays = (queries, latent_cache, kv_weight, block_order, span_start)
-        paired = queries.shape[1] % (2 * contexts) == 0 and contexts == 1 + len(EARLY) + len(LATE)
+        paired = queries.shape[1] % (2 * contexts) == 0 and contexts == 8
         if paired and cores == 2 and mesh.shape["groups"] == 2:
             return split_by_heads(contexts, cores, *arrays)
         return split_by_context(*arrays)

time: 74.2 us -> 68.6 us (0.925)
  waiting for transfers between devices: 24.7 us -> 20 us
  Pallas kernels: 11.8 us -> 7.39 us
  local copies, waits for them, and re-layouts: 3.29 us -> 4.96 us
  other arithmetic: 2.01 us -> 3.56 us
  blocking collectives: 10.9 us -> 11.8 us
  starting transfers between devices: 20.5 us -> 19.7 us
    ppermute x7, waiting for transfers between devices: 24.2 us -> 15.3 us  [swap(): return lax.ppermute(array, 'ctx', [(i, i ^ bit) for i in range(contexts)])]
    ppermute x1, waiting for transfers between devices: 0.01 us -> 4.72 us  [split_by_heads(): other = lax.ppermute(packed[:, :pair * depth], 'groups', [(0, 1), (1, 0)])]
    pallas_call x1 -> x2, Pallas kernels: 11.8 us -> 7.39 us  [attend(): pl.pallas_call(functools.partial(attend_kernel, contexts, rows, pair, whi...]
    all_to_all x1, starting transfers between devices: 7.38 us -> 3.8 us  [split_by_heads(): packed = lax.all_to_all(packed, 'ctx', 0, 0, tiled=True)]
    ppermute x7, starting transfers between devices: 9.95 us -> 12.7 us  [swap(): return lax.ppermute(array, 'ctx', [(i, i ^ bit) for i in range(contexts)])]
    another operation x0 -> x4, other arithmetic: none -> 2.35 us  [the longest x1 1.08 us: split_by_heads(): close_other = jnp.stack([trade(held[slot]) for slot in range(1, near)])]
    all_to_all x1, blocking collectives: 10.9 us -> 11.8 us  [split_by_heads(): attended = lax.all_to_all(attended, 'ctx', 0, 0, tiled=True)]
    dynamic_slice x1, local copies, waits for them, and re-layouts: 0.02 us -> 0.92 us  [split_by_heads(): held = {0: lax.dynamic_slice_in_dim(latent_cache, core * half, half, 0)}]
  transfers between devices with their start and end apart: 16 -> 16, of which waited for: 7 -> 5; matrix products, arithmetic and copies ran while one was open for 0% -> 10% of each run, Pallas kernels for 0% -> 5%
where the time goes in v4:
time: 68.6 us; the launch traced here: 68.3 us
  waiting for transfers between devices  20 us (29%)
  starting transfers between devices  19.7 us (29%)
  blocking collectives  11.8 us (17%)
  Pallas kernels  7.39 us (11%)
  local copies, waits for them, and re-layouts  4.96 us (7%)
  other arithmetic  3.56 us (5%)
  between operations  0.86 us (1%)
    ppermute x7, waiting for transfers between devices, swap(): return lax.ppermute(array, 'ctx', [(i, i ^ bit) for i in range(contexts)])  15.3 us
    ppermute x7, starting transfers between devices, swap(): return lax.ppermute(array, 'ctx', [(i, i ^ bit) for i in range(contexts)])  12.7 us
    all_to_all x1, blocking collectives, split_by_heads(): attended = lax.all_to_all(attended, 'ctx', 0, 0, tiled=True)  11.8 us
    pallas_call x2, Pallas kernels, attend(): pl.pallas_call(functools.partial(attend_kernel, contexts, rows, pair, whi...  7.39 us
    ppermute x1, waiting for transfers between devices, split_by_heads(): other = lax.ppermute(packed[:, :pair * depth], 'groups', [(0, 1), (1, 0)])  4.72 us
    all_to_all x1, starting transfers between devices, split_by_heads(): packed = lax.all_to_all(packed, 'ctx', 0, 0, tiled=True)  3.8 us
    ppermute x7, starting transfers between devices, trade(): return lax.ppermute(array, 'tp', [(0, 1), (1, 0)])  1.6 us
    ppermute x1, starting transfers between devices, split_by_heads(): other = lax.ppermute(packed[:, :pair * depth], 'groups', [(0, 1), (1, 0)])  1.58 us
  transfers between devices with their start and end apart: 16, of which 5 were waited for; matrix products, arithmetic and copies ran while one was open for 10% of the time, Pallas kernels for 5%

profile of v4, /device:TPU:0, one launch (start us, length us, event | category | flops | bytes accessed | tf_op | source)
XLA Modules:
  0.0 68.3 jit_solution(9270872977006083392)
XLA Ops:
  0.0 0.9 %constant_dynamic-slice_fusion = bf16[128,576]{0,1:T(8,128)(2,1)S(1)} fusion(bf16[256,576]{0,1:T(8,128)(2,1)} %param.6, s32[]{:T(128)S(6)} %select_n.18), kind=kLoop, calls=%fused_computation.8 | loop fusion | bytes 294916 | tf_op jit(solution)/shard_map/dynamic_slice | solution.py:134
  0.9 0.2 copy.13
  1.1 3.1 %collective-permute-start.2 = (bf16[128,576]{1,0:T(8,128)(2,1)S(1)}, bf16[128,576]{1,0:T(8,128)(2,1)S(1)}, u32[]{:S(2)}, u32[]{:S(2)}) collective-permute-start(bf16[128,576]{1,0:T(8,128)(2,1)S(1)} %copy.13), channel_id=1, source_target_pairs={{0,4},{2,6},{4,0},{6,2},{8,12},{10,14},{12,8},{14,10},{1,5},{3,7},... | collective-permute-start | bytes 442376 | tf_op jit(solution)/shard_map/ppermute | solution.py:118
  4.2 1.5 %collective-permute-start.1 = (bf16[128,576]{1,0:T(8,128)(2,1)S(1)}, bf16[128,576]{1,0:T(8,128)(2,1)S(1)}, u32[]{:S(2)}, u32[]{:S(2)}) collective-permute-start(bf16[128,576]{1,0:T(8,128)(2,1)S(1)} %copy.13), channel_id=1, source_target_pairs={{0,2},{2,0},{4,6},{6,4},{8,10},{10,8},{12,14},{14,12},{1,3},{3,1},... | collective-permute-start | bytes 442376 | tf_op jit(solution)/shard_map/ppermute | solution.py:118
  5.7 2.6 %collective-permute-start = (bf16[128,576]{1,0:T(8,128)(2,1)S(1)}, bf16[128,576]{1,0:T(8,128)(2,1)S(1)}, u32[]{:S(2)}, u32[]{:S(2)}) collective-permute-start(bf16[128,576]{1,0:T(8,128)(2,1)S(1)} %copy.13), channel_id=1, source_target_pairs={{0,8},{2,10},{4,12},{6,14},{8,0},{10,2},{12,4},{14,6},{1,9},{3,11}... | collective-permute-start | bytes 442376 | tf_op jit(solution)/shard_map/ppermute | solution.py:118
  8.3 1.2 %reshape.29 = bf16[16,8,2,2,192]{4,3,2,1,0:T(2,128)(2,1)S(1)} reshape(bf16[16,32,192]{2,1,0:T(8,128)(2,1)} %param.5) | data formatting | bytes 393216 | tf_op jit(solution)/shard_map/reshape | solution.py:123
  9.4 0.2 copy.8
  9.6 0.3 broadcast_select_fusion
  9.9 0.1 slice_bitcast_fusion
  10.0 0.1 slice_bitcast_fusion.1
  10.1 0.4 reshape.27
  10.6 0.4 constant_dynamic-slice_fusion.1
  11.0 0.1 reshape.31
  11.1 0.1 copy.9
  11.2 0.1 reshape.30
  11.3 0.2 copy.6
  11.5 0.9 %pad_maximum_fusion = bf16[8,176,256]{2,1,0:T(8,128)(2,1)} fusion(bf16[8,16,256]{2,1,0:T(8,128)(2,1)S(1)} %reshape.31, bf16[8,32,256]{2,1,0:T(8,128)(2,1)S(1)} %reshape.30, bf16[8,128,256]{2,1,0:T(8,128)(2,1)S(1)} %bitcast.31), kind=kLoop, calls=%fused_computation | loop fusion | flops 2162688 | bytes 1441792 | tf_op jit(solution)/shard_map/concatenate | solution.py:129
  12.4 0.0 collective-permute-done.2
  12.5 0.0 collective-permute-done.1
  12.5 3.0 %collective-permute-done = bf16[128,576]{1,0:T(8,128)(2,1)S(1)} collective-permute-done((bf16[128,576]{1,0:T(8,128)(2,1)S(1)}, bf16[128,576]{1,0:T(8,128)(2,1)S(1)}, u32[]{:S(2)}, u32[]{:S(2)}) %collective-permute-start) | collective-permute-done | bytes 147488 | tf_op jit(solution)/shard_map/ppermute | solution.py:118
  15.5 3.8 %all-to-all-start = ((bf16[8,176,256]{2,1,0:T(8,128)(2,1)}), bf16[8,176,256]{2,1,0:T(8,128)(2,1)S(1)}, u32[]{:S(2)}, u32[]{:S(2)}) async-start(bf16[8,176,256]{2,1,0:T(8,128)(2,1)} %pad_maximum_fusion), calls=%async_computation | async-start | bytes 1441792 | tf_op jit(solution)/shard_map/all_to_all | solution.py:139
  19.3 2.0 %collective-permute-start.4 = (bf16[128,576]{1,0:T(8,128)(2,1)S(1)}, bf16[128,576]{1,0:T(8,128)(2,1)S(1)}, u32[]{:S(2)}, u32[]{:S(2)}) collective-permute-start(bf16[128,576]{1,0:T(8,128)(2,1)S(1)} %collective-permute-done), channel_id=1, source_target_pairs={{0,2},{2,0},{4,6},{6,4},{8,10},{10,8},{12,14},{14,12},{1,3},{3,1},... | collective-permute-start | bytes 442376 | tf_op jit(solution)/shard_map/ppermute | solution.py:118
  21.3 0.0 collective-permute-start.3
  21.3 2.0 %collective-permute-start.5 = (bf16[128,576]{1,0:T(8,128)(2,1)S(1)}, bf16[128,576]{1,0:T(8,128)(2,1)S(1)}, u32[]{:S(2)}, u32[]{:S(2)}) collective-permute-start(bf16[128,576]{1,0:T(8,128)(2,1)S(1)} %collective-permute-done), channel_id=1, source_target_pairs={{0,4},{2,6},{4,0},{6,2},{8,12},{10,14},{12,8},{14,10},{1,5},{3,7},... | collective-permute-start | bytes 442376 | tf_op jit(solution)/shard_map/ppermute | solution.py:118
  23.3 0.0 collective-permute-start.8
  23.3 0.5 collective-permute-start.7
  23.8 9.0 %collective-permute-done.4 = bf16[128,576]{1,0:T(8,128)(2,1)S(1)} collective-permute-done((bf16[128,576]{1,0:T(8,128)(2,1)S(1)}, bf16[128,576]{1,0:T(8,128)(2,1)S(1)}, u32[]{:S(2)}, u32[]{:S(2)}) %collective-permute-start.4) | collective-permute-done | bytes 147488 | tf_op jit(solution)/shard_map/ppermute | solution.py:118
  32.8 1.5 %collective-permute-start.10 = (bf16[128,576]{1,0:T(8,128)(2,1)S(1)}, bf16[128,576]{1,0:T(8,128)(2,1)S(1)}, u32[]{:S(2)}, u32[]{:S(2)}) collective-permute-start(bf16[128,576]{1,0:T(8,128)(2,1)S(1)} %collective-permute-done.4), channel_id=1, source_target_pairs={{0,4},{2,6},{4,0},{6,2},{8,12},{10,14},{12,8},{14,10},{1,5},{3,7},... | collective-permute-start | bytes 442376 | tf_op jit(solution)/shard_map/ppermute | solution.py:118
  34.3 1.3 %collective-permute-done.3 = bf16[128,576]{1,0:T(8,128)(2,1)} collective-permute-done((bf16[128,576]{1,0:T(8,128)(2,1)S(1)}, bf16[128,576]{1,0:T(8,128)(2,1)}, u32[]{:S(2)}, u32[]{:S(2)}) %collective-permute-start.3) | collective-permute-done | bytes 147488 | tf_op jit(solution)/shard_map/ppermute | solution.py:118
  35.6 2.0 %collective-permute-done.5 = bf16[128,576]{1,0:T(8,128)(2,1)S(1)} collective-permute-done((bf16[128,576]{1,0:T(8,128)(2,1)S(1)}, bf16[128,576]{1,0:T(8,128)(2,1)S(1)}, u32[]{:S(2)}, u32[]{:S(2)}) %collective-permute-start.5) | collective-permute-done | bytes 147488 | tf_op jit(solution)/shard_map/ppermute | solution.py:118
  37.6 0.0 all-to-all-done.refs_2_
  37.6 0.0 collective-permute-start.9
  37.6 1.6 %collective-permute-start.6 = (bf16[8,128,256]{2,1,0:T(8,128)(2,1)S(1)}, bf16[8,128,256]{2,1,0:T(8,128)(2,1)S(1)}, u32[]{:S(2)}, u32[]{:S(2)}) collective-permute-start(bf16[8,128,256]{2,1,0:T(8,128)(2,1)S(1)} %slice.11), channel_id=1, source_target_pairs={{0,16},{16,0},{1,17},{17,1},{2,18},{18,2},{3,19},{19,3},{4,20},{20... | collective-permute-start | bytes 1572872 | tf_op jit(solution)/shard_map/ppermute | solution.py:146
  39.9 0.2 copy.11
  40.1 1.0 %pad_maximum_fusion.3.refs_4_.refs_6_ = bf16[3,128,576]{2,1,0:T(8,128)(2,1)S(1)} fusion(bf16[1,128,576]{2,1,0:T(8,128)(2,1)} %bitcast.8, bf16[1,128,576]{2,1,0:T(8,128)(2,1)S(1)} %bitcast.40, bf16[1,128,576]{2,1,0:T(8,128)(2,1)S(1)} %bitcast.41), kind=kLoop, calls=%fused_computation.4 | loop fusion | flops 442368 | bytes 884736 | tf_op jit(solution)/shard_map/stack | solution.py:143
  41.1 0.3 collective-permute-start.11
  41.4 0.3 collective-permute-start.14
  41.7 0.2 collective-permute-start.12
  41.9 0.3 collective-permute-start.13
  42.2 0.1 pad_maximum_fusion.1.refs_6_.refs_8_
  42.3 0.0 copy-start
  42.4 1.1 %pad_maximum_fusion.4.refs_5_.refs_7_ = bf16[3,128,576]{2,1,0:T(8,128)(2,1)S(1)} fusion(bf16[1,128,576]{2,1,0:T(8,128)(2,1)} %bitcast.11, bf16[1,128,576]{2,1,0:T(8,128)(2,1)S(1)} %bitcast.42, bf16[1,128,576]{2,1,0:T(8,128)(2,1)} %bitcast.9), kind=kLoop, calls=%fused_computation.5 | loop fusion | flops 442368 | bytes 884736 | tf_op jit(solution)/shard_map/stack | solution.py:149
  43.5 0.1 pad_maximum_fusion.2.refs_7_.refs_9_
  43.6 3.7 %attend_first.1.refs_4_ = bf16[128,256]{1,0:T(8,128)(2,1)S(1)} custom-call(s32[8]{0:T(128)S(1)} %copy-done, s32[1]{0:T(128)S(6)} %copy.14.refs_1_, bf16[8,176,256]{2,1,0:T(8,128)(2,1)S(1)} %all-to-all-done.refs_2_, bf16[2,128,576]{2,1,0:T(8,128)(2,1)S(1)} %bitcast.28, bf16[3,128,576]{2,1,0:T(8,128)(2,1)S(1)} %pad_maximum_fusion.3.refs_4_.refs_6_, ...), custom_call_target="tpu_custom_call" | custom-call | flops 1048576 | bytes 1048576 | tf_op jit(solution)/shard_map/attend_first/pallas_call | solution.py:160
  47.3 4.7 %collective-permute-done.6.refs_3_ = bf16[8,128,256]{2,1,0:T(8,128)(2,1)S(1)} collective-permute-done((bf16[8,128,256]{2,1,0:T(8,128)(2,1)S(1)}, bf16[8,128,256]{2,1,0:T(8,128)(2,1)S(1)}, u32[]{:S(2)}, u32[]{:S(2)}) %collective-permute-start.6) | collective-permute-done | bytes 524320 | tf_op jit(solution)/shard_map/ppermute | solution.py:146
  52.1 3.7 %attend_second.1 = bf16[128,512]{1,0:T(8,128)(2,1)S(1)} custom-call(s32[8]{0:T(128)S(1)} %copy-done, s32[1]{0:T(128)S(6)} %copy.14.refs_1_, bf16[8,176,256]{2,1,0:T(8,128)(2,1)S(1)} %all-to-all-done.refs_2_, bf16[8,128,256]{2,1,0:T(8,128)(2,1)S(1)} %collective-permute-done.6.refs_3_, bf16[128,256]{1,0:T(8,128)(2,1)S(1)} %attend_first.1.refs_4_, ...), custom_call_target="tpu_custom_call" | custom-call | flops 1048576 | bytes 1048576 | tf_op jit(solution)/shard_map/attend_second/pallas_call | solution.py:160
  55.8 11.8 %all_to_all.10 = bf16[8,16,512]{2,1,0:T(8,128)(2,1)S(1)} all-to-all(bf16[8,16,512]{2,1,0:T(8,128)(2,1)S(1)} %bitcast.30), channel_id=1, replica_groups=mesh['groups'=2,'ctx'=8,'tp'=2] {'ctx'}, dimensions={0} | all-to-all | bytes 262144 | tf_op jit(solution)/shard_map/all_to_all | solution.py:179
  67.6 0.7 %copy.12 = bf16[8,16,4,128]{3,2,0,1:T(4,128)(2,1)} copy(bf16[8,16,4,128]{3,2,1,0:T(4,128)(2,1)S(1)} %reshape.34) | data formatting | bytes 262144 | tf_op jit(solution)/shard_map/reshape | solution.py:180
  (15 shorter events, 0.1 us)
Async XLA Ops:
  1.1 11.4 %collective-permute-start.2 = (bf16[128,576]{1,0:T(8,128)(2,1)S(1)}, bf16[128,576]{1,0:T(8,128)(2,1)S(1)}, u32[]{:S(2)}, u32[]{:S(2)}) collective-permute-start(bf16[128,576]{1,0:T(8,128)(2,1)S(1)} %copy.13), channel_id=1, source_target_pairs={{0,4},{2,6},{4,0},{6,2},{8,12},{10,14},{12,8},{14,10},{1,5},{3,7},... | collective-permute-start | bytes 442376 | tf_op jit(solution)/shard_map/ppermute | solution.py:118
  4.2 8.3 %collective-permute-start.1 = (bf16[128,576]{1,0:T(8,128)(2,1)S(1)}, bf16[128,576]{1,0:T(8,128)(2,1)S(1)}, u32[]{:S(2)}, u32[]{:S(2)}) collective-permute-start(bf16[128,576]{1,0:T(8,128)(2,1)S(1)} %copy.13), channel_id=1, source_target_pairs={{0,2},{2,0},{4,6},{6,4},{8,10},{10,8},{12,14},{14,12},{1,3},{3,1},... | collective-permute-start | bytes 442376 | tf_op jit(solution)/shard_map/ppermute | solution.py:118
  5.7 9.8 %collective-permute-start = (bf16[128,576]{1,0:T(8,128)(2,1)S(1)}, bf16[128,576]{1,0:T(8,128)(2,1)S(1)}, u32[]{:S(2)}, u32[]{:S(2)}) collective-permute-start(bf16[128,576]{1,0:T(8,128)(2,1)S(1)} %copy.13), channel_id=1, source_target_pairs={{0,8},{2,10},{4,12},{6,14},{8,0},{10,2},{12,4},{14,6},{1,9},{3,11}... | collective-permute-start | bytes 442376 | tf_op jit(solution)/shard_map/ppermute | solution.py:118
  8.3 1.9 %copy-start.1 = (bf16[64,32,256]{2,1,0:T(8,128)(2,1)S(1)}, bf16[64,32,256]{2,1,0:T(8,128)(2,1)}, u32[]{:S(2)}) copy-start(bf16[64,32,256]{2,1,0:T(8,128)(2,1)} %param.7) | copy-start | bytes 3145732
  12.4 27.4 %copy-start.2 = (bf16[256,576]{0,1:T(8,128)(2,1)S(1)}, bf16[256,576]{0,1:T(8,128)(2,1)}, u32[]{:S(2)}) copy-start(bf16[256,576]{0,1:T(8,128)(2,1)} %param.6) | copy-start | bytes 884740
  15.5 22.1 %all-to-all-start = ((bf16[8,176,256]{2,1,0:T(8,128)(2,1)}), bf16[8,176,256]{2,1,0:T(8,128)(2,1)S(1)}, u32[]{:S(2)}, u32[]{:S(2)}) async-start(bf16[8,176,256]{2,1,0:T(8,128)(2,1)} %pad_maximum_fusion), calls=%async_computation | async-start | bytes 1441792 | tf_op jit(solution)/shard_map/all_to_all | solution.py:139
  19.3 13.5 %collective-permute-start.4 = (bf16[128,576]{1,0:T(8,128)(2,1)S(1)}, bf16[128,576]{1,0:T(8,128)(2,1)S(1)}, u32[]{:S(2)}, u32[]{:S(2)}) collective-permute-start(bf16[128,576]{1,0:T(8,128)(2,1)S(1)} %collective-permute-done), channel_id=1, source_target_pairs={{0,2},{2,0},{4,6},{6,4},{8,10},{10,8},{12,14},{14,12},{1,3},{3,1},... | collective-permute-start | bytes 442376 | tf_op jit(solution)/shard_map/ppermute | solution.py:118
  21.3 14.3 %collective-permute-start.3 = (bf16[128,576]{1,0:T(8,128)(2,1)S(1)}, bf16[128,576]{1,0:T(8,128)(2,1)}, u32[]{:S(2)}, u32[]{:S(2)}) collective-permute-start(bf16[128,576]{1,0:T(8,128)(2,1)S(1)} %collective-permute-done.2), channel_id=1, source_target_pairs={{0,2},{2,0},{4,6},{6,4},{8,10},{10,8},{12,14},{14,12},{1,3},{3,1},... | collective-permute-start | bytes 442376 | tf_op jit(solution)/shard_map/ppermute | solution.py:118
  21.3 16.3 %collective-permute-start.5 = (bf16[128,576]{1,0:T(8,128)(2,1)S(1)}, bf16[128,576]{1,0:T(8,128)(2,1)S(1)}, u32[]{:S(2)}, u32[]{:S(2)}) collective-permute-start(bf16[128,576]{1,0:T(8,128)(2,1)S(1)} %collective-permute-done), channel_id=1, source_target_pairs={{0,4},{2,6},{4,0},{6,2},{8,12},{10,14},{12,8},{14,10},{1,5},{3,7},... | collective-permute-start | bytes 442376 | tf_op jit(solution)/shard_map/ppermute | solution.py:118
  23.3 18.4 %collective-permute-start.8 = (bf16[128,576]{1,0:T(8,128)(2,1)S(1)}, bf16[128,576]{1,0:T(8,128)(2,1)S(1)}, u32[]{:S(2)}, u32[]{:S(2)}) collective-permute-start(bf16[128,576]{1,0:T(8,128)(2,1)S(1)} %collective-permute-done.2), channel_id=1, source_target_pairs={{0,1},{1,0},{2,3},{3,2},{4,5},{5,4},{6,7},{7,6},{8,9},{9,8},{10,11... | collective-permute-start | bytes 442376 | tf_op jit(solution)/shard_map/ppermute | solution.py:131
  23.3 17.8 %collective-permute-start.7 = (bf16[128,576]{1,0:T(8,128)(2,1)S(1)}, bf16[128,576]{1,0:T(8,128)(2,1)}, u32[]{:S(2)}, u32[]{:S(2)}) collective-permute-start(bf16[128,576]{1,0:T(8,128)(2,1)S(1)} %collective-permute-done.1), channel_id=1, source_target_pairs={{0,1},{1,0},{2,3},{3,2},{4,5},{5,4},{6,7},{7,6},{8,9},{9,8},{10,11... | collective-permute-start | bytes 442376 | tf_op jit(solution)/shard_map/ppermute | solution.py:131
  32.8 8.6 %collective-permute-start.10 = (bf16[128,576]{1,0:T(8,128)(2,1)S(1)}, bf16[128,576]{1,0:T(8,128)(2,1)S(1)}, u32[]{:S(2)}, u32[]{:S(2)}) collective-permute-start(bf16[128,576]{1,0:T(8,128)(2,1)S(1)} %collective-permute-done.4), channel_id=1, source_target_pairs={{0,4},{2,6},{4,0},{6,2},{8,12},{10,14},{12,8},{14,10},{1,5},{3,7},... | collective-permute-start | bytes 442376 | tf_op jit(solution)/shard_map/ppermute | solution.py:118
  37.6 4.3 %collective-permute-start.9 = (bf16[128,576]{1,0:T(8,128)(2,1)}, bf16[128,576]{1,0:T(8,128)(2,1)}, u32[]{:S(2)}, u32[]{:S(2)}) collective-permute-start(bf16[128,576]{1,0:T(8,128)(2,1)} %collective-permute-done.3), channel_id=1, source_target_pairs={{0,1},{1,0},{2,3},{3,2},{4,5},{5,4},{6,7},{7,6},{8,9},{9,8},{10,11... | collective-permute-start | bytes 442376 | tf_op jit(solution)/shard_map/ppermute | solution.py:131
  37.6 14.4 %collective-permute-start.6 = (bf16[8,128,256]{2,1,0:T(8,128)(2,1)S(1)}, bf16[8,128,256]{2,1,0:T(8,128)(2,1)S(1)}, u32[]{:S(2)}, u32[]{:S(2)}) collective-permute-start(bf16[8,128,256]{2,1,0:T(8,128)(2,1)S(1)} %slice.11), channel_id=1, source_target_pairs={{0,16},{16,0},{1,17},{17,1},{2,18},{18,2},{3,19},{19,3},{4,20},{20... | collective-permute-start | bytes 1572872 | tf_op jit(solution)/shard_map/ppermute | solution.py:146
  41.1 2.3 %collective-permute-start.11 = (bf16[128,576]{1,0:T(8,128)(2,1)S(1)}, bf16[128,576]{1,0:T(8,128)(2,1)S(1)}, u32[]{:S(2)}, u32[]{:S(2)}) collective-permute-start(bf16[128,576]{1,0:T(8,128)(2,1)S(1)} %collective-permute-done), channel_id=1, source_target_pairs={{0,1},{1,0},{2,3},{3,2},{4,5},{5,4},{6,7},{7,6},{8,9},{9,8},{10,11... | collective-permute-start | bytes 442376 | tf_op jit(solution)/shard_map/ppermute | solution.py:131
  41.4 2.0 %collective-permute-start.14 = (bf16[128,576]{1,0:T(8,128)(2,1)S(1)}, bf16[128,576]{1,0:T(8,128)(2,1)S(1)}, u32[]{:S(2)}, u32[]{:S(2)}) collective-permute-start(bf16[128,576]{1,0:T(8,128)(2,1)S(1)} %collective-permute-done.10), channel_id=1, source_target_pairs={{0,1},{1,0},{2,3},{3,2},{4,5},{5,4},{6,7},{7,6},{8,9},{9,8},{10,11... | collective-permute-start | bytes 442376 | tf_op jit(solution)/shard_map/ppermute | solution.py:131
  41.7 1.8 %collective-permute-start.12 = (bf16[128,576]{1,0:T(8,128)(2,1)S(1)}, bf16[128,576]{1,0:T(8,128)(2,1)S(1)}, u32[]{:S(2)}, u32[]{:S(2)}) collective-permute-start(bf16[128,576]{1,0:T(8,128)(2,1)S(1)} %collective-permute-done.4), channel_id=1, source_target_pairs={{0,1},{1,0},{2,3},{3,2},{4,5},{5,4},{6,7},{7,6},{8,9},{9,8},{10,11... | collective-permute-start | bytes 442376 | tf_op jit(solution)/shard_map/ppermute | solution.py:131
  41.9 1.5 %collective-permute-start.13 = (bf16[128,576]{1,0:T(8,128)(2,1)S(1)}, bf16[128,576]{1,0:T(8,128)(2,1)S(1)}, u32[]{:S(2)}, u32[]{:S(2)}) collective-permute-start(bf16[128,576]{1,0:T(8,128)(2,1)S(1)} %collective-permute-done.5), channel_id=1, source_target_pairs={{0,1},{1,0},{2,3},{3,2},{4,5},{5,4},{6,7},{7,6},{8,9},{9,8},{10,11... | collective-permute-start | bytes 442376 | tf_op jit(solution)/shard_map/ppermute | solution.py:131
  42.3 1.3 %copy-start = (s32[8]{0:T(128)S(1)}, s32[8]{0:T(128)}, u32[]{:S(2)}) copy-start(s32[8]{0:T(128)} %refs_0_.3) | copy-start | bytes 100

commit v5 on v4

--- a/solution.py
+++ b/solution.py
@@ -127,6 +127,7 @@
     turned = query[..., NOPE:].transpose(1, 0, 2, 3, 4)
     turned = turned.reshape(contexts, query_rows, heads * ROPE)
     packed = jnp.concatenate([weight, straight, turned], axis=1)
+
     def trade(array):
         return lax.ppermute(array, "tp", [(0, 1), (1, 0)])
 
@@ -141,8 +142,6 @@
         held[slot] = swap(held[source], bit)
     near = contexts // 2
     close = jnp.stack([held[slot] for slot in range(1, near)])
-    waited = lax.optimization_barrier((packed, held[3], held[5], held[6]))
-    packed, held[3], held[5], held[6] = waited
     other = lax.ppermute(packed[:, :pair * depth], "groups", [(0, 1), (1, 0)])
     far = jnp.stack([held[slot] for slot in range(near, contexts)])
     own = latent_cache.reshape(cores, half, latent_cache.shape[1])

time: 68.6 us -> 66.5 us (0.969)
  waiting for transfers between devices: 20 us -> 16.4 us
  blocking collectives: 11.8 us -> 13.2 us
    ppermute x1, waiting for transfers between devices: 4.72 us -> 1.25 us  [split_by_heads(): other = lax.ppermute(packed[:, :pair * depth], 'groups', [(0, 1), (1, 0)])]
    all_to_all x1, blocking collectives: 11.8 us -> 13.2 us  [split_by_heads(): attended = lax.all_to_all(attended, 'ctx', 0, 0, tiled=True)]
  transfers between devices with their start and end apart: 16 -> 16, of which waited for: 5 -> 5; matrix products, arithmetic and copies ran while one was open for 10% -> 10% of each run, Pallas kernels for 5% -> 6%
where the time goes in v5:
time: 66.5 us; the launch traced here: 66.2 us
  starting transfers between devices  19.5 us (29%)
  waiting for transfers between devices  16.4 us (25%)
  blocking collectives  13.2 us (20%)
  Pallas kernels  7.39 us (11%)
  local copies, waits for them, and re-layouts  5.29 us (8%)
  other arithmetic  3.55 us (5%)
  between operations  0.87 us (1%)
    ppermute x7, waiting for transfers between devices, swap(): return lax.ppermute(array, 'ctx', [(i, i ^ bit) for i in range(contexts)])  14.6 us
    all_to_all x1, blocking collectives, split_by_heads(): attended = lax.all_to_all(attended, 'ctx', 0, 0, tiled=True)  13.2 us
    ppermute x7, starting transfers between devices, swap(): return lax.ppermute(array, 'ctx', [(i, i ^ bit) for i in range(contexts)])  12.5 us
    pallas_call x2, Pallas kernels, attend(): pl.pallas_call(functools.partial(attend_kernel, contexts, rows, pair, whi...  7.39 us
    all_to_all x1, starting transfers between devices, split_by_heads(): packed = lax.all_to_all(packed, 'ctx', 0, 0, tiled=True)  3.8 us
    ppermute x7, starting transfers between devices, trade(): return lax.ppermute(array, 'tp', [(0, 1), (1, 0)])  1.58 us
    ppermute x1, starting transfers between devices, split_by_heads(): other = lax.ppermute(packed[:, :pair * depth], 'groups', [(0, 1), (1, 0)])  1.58 us
    reshape x2, local copies, waits for them, and re-layouts, split_by_heads(): query = queries.reshape(query_rows, contexts, 2, pair, query_width)  1.36 us
  transfers between devices with their start and end apart: 16, of which 5 were waited for; matrix products, arithmetic and copies ran while one was open for 10% of the time, Pallas kernels for 6%

profile of v5, /device:TPU:0, one launch (start us, length us, event | category | flops | bytes accessed | tf_op | source)
XLA Modules:
  0.0 66.2 jit_solution(18224975905905790221)
XLA Ops:
  0.0 0.9 %constant_dynamic-slice_fusion = bf16[128,576]{0,1:T(8,128)(2,1)S(1)} fusion(bf16[256,576]{0,1:T(8,128)(2,1)} %param.6, s32[]{:T(128)S(6)} %select_n.18), kind=kLoop, calls=%fused_computation.8 | loop fusion | bytes 294916 | tf_op jit(solution)/shard_map/dynamic_slice | solution.py:135
  0.9 0.2 copy.13
  1.1 3.1 %collective-permute-start.2 = (bf16[128,576]{1,0:T(8,128)(2,1)S(1)}, bf16[128,576]{1,0:T(8,128)(2,1)S(1)}, u32[]{:S(2)}, u32[]{:S(2)}) collective-permute-start(bf16[128,576]{1,0:T(8,128)(2,1)S(1)} %copy.13), channel_id=1, source_target_pairs={{0,4},{2,6},{4,0},{6,2},{8,12},{10,14},{12,8},{14,10},{1,5},{3,7},... | collective-permute-start | bytes 442376 | tf_op jit(solution)/shard_map/ppermute | solution.py:118
  4.2 1.5 %collective-permute-start.1 = (bf16[128,576]{1,0:T(8,128)(2,1)S(1)}, bf16[128,576]{1,0:T(8,128)(2,1)S(1)}, u32[]{:S(2)}, u32[]{:S(2)}) collective-permute-start(bf16[128,576]{1,0:T(8,128)(2,1)S(1)} %copy.13), channel_id=1, source_target_pairs={{0,2},{2,0},{4,6},{6,4},{8,10},{10,8},{12,14},{14,12},{1,3},{3,1},... | collective-permute-start | bytes 442376 | tf_op jit(solution)/shard_map/ppermute | solution.py:118
  5.7 2.6 %collective-permute-start = (bf16[128,576]{1,0:T(8,128)(2,1)S(1)}, bf16[128,576]{1,0:T(8,128)(2,1)S(1)}, u32[]{:S(2)}, u32[]{:S(2)}) collective-permute-start(bf16[128,576]{1,0:T(8,128)(2,1)S(1)} %copy.13), channel_id=1, source_target_pairs={{0,8},{2,10},{4,12},{6,14},{8,0},{10,2},{12,4},{14,6},{1,9},{3,11}... | collective-permute-start | bytes 442376 | tf_op jit(solution)/shard_map/ppermute | solution.py:118
  8.3 1.2 %reshape.29 = bf16[16,8,2,2,192]{4,3,2,1,0:T(2,128)(2,1)S(1)} reshape(bf16[16,32,192]{2,1,0:T(8,128)(2,1)} %param.5) | data formatting | bytes 393216 | tf_op jit(solution)/shard_map/reshape | solution.py:123
  9.4 0.2 copy.8
  9.6 0.3 broadcast_select_fusion
  9.9 0.1 slice_bitcast_fusion
  10.0 0.1 slice_bitcast_fusion.1
  10.1 0.4 reshape.27
  10.6 0.4 constant_dynamic-slice_fusion.1
  11.0 0.1 reshape.31
  11.1 0.1 copy.9
  11.2 0.1 reshape.30
  11.3 0.2 copy.6
  11.5 0.9 %pad_maximum_fusion = bf16[8,176,256]{2,1,0:T(8,128)(2,1)} fusion(bf16[8,16,256]{2,1,0:T(8,128)(2,1)S(1)} %reshape.31, bf16[8,32,256]{2,1,0:T(8,128)(2,1)S(1)} %reshape.30, bf16[8,128,256]{2,1,0:T(8,128)(2,1)S(1)} %bitcast.31), kind=kLoop, calls=%fused_computation | loop fusion | flops 2162688 | bytes 1441792 | tf_op jit(solution)/shard_map/concatenate | solution.py:129
  12.4 0.0 collective-permute-done.2
  12.5 0.0 collective-permute-done.1
  12.5 3.0 %collective-permute-done = bf16[128,576]{1,0:T(8,128)(2,1)S(1)} collective-permute-done((bf16[128,576]{1,0:T(8,128)(2,1)S(1)}, bf16[128,576]{1,0:T(8,128)(2,1)S(1)}, u32[]{:S(2)}, u32[]{:S(2)}) %collective-permute-start) | collective-permute-done | bytes 147488 | tf_op jit(solution)/shard_map/ppermute | solution.py:118
  15.5 3.8 %all-to-all-start = ((bf16[8,176,256]{2,1,0:T(8,128)(2,1)}), bf16[8,176,256]{2,1,0:T(8,128)(2,1)S(1)}, u32[]{:S(2)}, u32[]{:S(2)}) async-start(bf16[8,176,256]{2,1,0:T(8,128)(2,1)} %pad_maximum_fusion), calls=%async_computation | async-start | bytes 1441792 | tf_op jit(solution)/shard_map/all_to_all | solution.py:140
  19.3 2.0 %collective-permute-start.4 = (bf16[128,576]{1,0:T(8,128)(2,1)S(1)}, bf16[128,576]{1,0:T(8,128)(2,1)}, u32[]{:S(2)}, u32[]{:S(2)}) collective-permute-start(bf16[128,576]{1,0:T(8,128)(2,1)S(1)} %collective-permute-done.2), channel_id=1, source_target_pairs={{0,2},{2,0},{4,6},{6,4},{8,10},{10,8},{12,14},{14,12},{1,3},{3,1},... | collective-permute-start | bytes 442376 | tf_op jit(solution)/shard_map/ppermute | solution.py:118
  21.3 0.0 collective-permute-start.8
  21.3 0.0 collective-permute-start.5
  21.3 0.5 collective-permute-start.6
  21.8 2.0 %collective-permute-start.9 = (bf16[128,576]{1,0:T(8,128)(2,1)S(1)}, bf16[128,576]{1,0:T(8,128)(2,1)S(1)}, u32[]{:S(2)}, u32[]{:S(2)}) collective-permute-start(bf16[128,576]{1,0:T(8,128)(2,1)S(1)} %collective-permute-done), channel_id=1, source_target_pairs={{0,4},{2,6},{4,0},{6,2},{8,12},{10,14},{12,8},{14,10},{1,5},{3,7},... | collective-permute-start | bytes 442376 | tf_op jit(solution)/shard_map/ppermute | solution.py:118
  23.8 9.1 %collective-permute-done.4 = bf16[128,576]{1,0:T(8,128)(2,1)} collective-permute-done((bf16[128,576]{1,0:T(8,128)(2,1)S(1)}, bf16[128,576]{1,0:T(8,128)(2,1)}, u32[]{:S(2)}, u32[]{:S(2)}) %collective-permute-start.4) | collective-permute-done | bytes 147488 | tf_op jit(solution)/shard_map/ppermute | solution.py:118
  32.9 0.0 collective-permute-start.7
  32.9 2.6 %collective-permute-done.8 = bf16[128,576]{1,0:T(8,128)(2,1)S(1)} collective-permute-done((bf16[128,576]{1,0:T(8,128)(2,1)S(1)}, bf16[128,576]{1,0:T(8,128)(2,1)S(1)}, u32[]{:S(2)}, u32[]{:S(2)}) %collective-permute-start.8) | collective-permute-done | bytes 147488 | tf_op jit(solution)/shard_map/ppermute | solution.py:118
  35.5 1.3 %collective-permute-start.10 = (bf16[128,576]{1,0:T(8,128)(2,1)S(1)}, bf16[128,576]{1,0:T(8,128)(2,1)S(1)}, u32[]{:S(2)}, u32[]{:S(2)}) collective-permute-start(bf16[128,576]{1,0:T(8,128)(2,1)S(1)} %collective-permute-done.8), channel_id=1, source_target_pairs={{0,4},{2,6},{4,0},{6,2},{8,12},{10,14},{12,8},{14,10},{1,5},{3,7},... | collective-permute-start | bytes 442376 | tf_op jit(solution)/shard_map/ppermute | solution.py:118
  36.7 0.5 all-to-all-done.refs_2_
  37.3 1.6 %collective-permute-start.3 = (bf16[8,128,256]{2,1,0:T(8,128)(2,1)S(1)}, bf16[8,128,256]{2,1,0:T(8,128)(2,1)S(1)}, u32[]{:S(2)}, u32[]{:S(2)}) collective-permute-start(bf16[8,128,256]{2,1,0:T(8,128)(2,1)S(1)} %slice.14), channel_id=1, source_target_pairs={{0,16},{16,0},{1,17},{17,1},{2,18},{18,2},{3,19},{19,3},{4,20},{20... | collective-permute-start | bytes 1572872 | tf_op jit(solution)/shard_map/ppermute | solution.py:145
  39.6 0.2 copy.11
  39.8 1.0 %pad_maximum_fusion.3.refs_4_.refs_6_ = bf16[3,128,576]{2,1,0:T(8,128)(2,1)S(1)} fusion(bf16[1,128,576]{2,1,0:T(8,128)(2,1)} %bitcast.8, bf16[1,128,576]{2,1,0:T(8,128)(2,1)S(1)} %bitcast.40, bf16[1,128,576]{2,1,0:T(8,128)(2,1)S(1)} %bitcast.41), kind=kLoop, calls=%fused_computation.4 | loop fusion | flops 442368 | bytes 884736 | tf_op jit(solution)/shard_map/stack | solution.py:144
  40.8 0.1 collective-permute-start.11
  40.9 0.5 collective-permute-start.12
  41.4 0.1 collective-permute-start.13
  41.4 0.4 collective-permute-start.14
  41.9 1.1 %pad_maximum_fusion.4.refs_5_.refs_7_ = bf16[3,128,576]{2,1,0:T(8,128)(2,1)S(1)} fusion(bf16[1,128,576]{2,1,0:T(8,128)(2,1)} %bitcast.11, bf16[1,128,576]{2,1,0:T(8,128)(2,1)} %bitcast.10, bf16[1,128,576]{2,1,0:T(8,128)(2,1)S(1)} %bitcast.42), kind=kLoop, calls=%fused_computation.5 | loop fusion | flops 442368 | bytes 884736 | tf_op jit(solution)/shard_map/stack | solution.py:148
  43.0 0.0 copy-start
  43.0 0.1 pad_maximum_fusion.1.refs_6_.refs_8_
  43.1 0.1 pad_maximum_fusion.2.refs_7_.refs_9_
  43.3 0.3 copy-done
  43.6 3.7 %attend_first.1.refs_4_ = bf16[128,256]{1,0:T(8,128)(2,1)S(1)} custom-call(s32[8]{0:T(128)S(1)} %copy-done, s32[1]{0:T(128)S(6)} %copy.14.refs_1_, bf16[8,176,256]{2,1,0:T(8,128)(2,1)S(1)} %all-to-all-done.refs_2_, bf16[2,128,576]{2,1,0:T(8,128)(2,1)S(1)} %bitcast.28, bf16[3,128,576]{2,1,0:T(8,128)(2,1)S(1)} %pad_maximum_fusion.3.refs_4_.refs_6_, ...), custom_call_target="tpu_custom_call" | custom-call | flops 1048576 | bytes 1048576 | tf_op jit(solution)/shard_map/attend_first/pallas_call | solution.py:159
  47.3 1.3 %collective-permute-done.3.refs_3_ = bf16[8,128,256]{2,1,0:T(8,128)(2,1)S(1)} collective-permute-done((bf16[8,128,256]{2,1,0:T(8,128)(2,1)S(1)}, bf16[8,128,256]{2,1,0:T(8,128)(2,1)S(1)}, u32[]{:S(2)}, u32[]{:S(2)}) %collective-permute-start.3) | collective-permute-done | bytes 524320 | tf_op jit(solution)/shard_map/ppermute | solution.py:145
  48.6 3.7 %attend_second.1 = bf16[128,512]{1,0:T(8,128)(2,1)S(1)} custom-call(s32[8]{0:T(128)S(1)} %copy-done, s32[1]{0:T(128)S(6)} %copy.14.refs_1_, bf16[8,176,256]{2,1,0:T(8,128)(2,1)S(1)} %all-to-all-done.refs_2_, bf16[8,128,256]{2,1,0:T(8,128)(2,1)S(1)} %collective-permute-done.3.refs_3_, bf16[128,256]{1,0:T(8,128)(2,1)S(1)} %attend_first.1.refs_4_, ...), custom_call_target="tpu_custom_call" | custom-call | flops 1048576 | bytes 1048576 | tf_op jit(solution)/shard_map/attend_second/pallas_call | solution.py:159
  52.3 13.2 %all_to_all.10 = bf16[8,16,512]{2,1,0:T(8,128)(2,1)S(1)} all-to-all(bf16[8,16,512]{2,1,0:T(8,128)(2,1)S(1)} %bitcast.30), channel_id=1, replica_groups=mesh['groups'=2,'ctx'=8,'tp'=2] {'ctx'}, dimensions={0} | all-to-all | bytes 262144 | tf_op jit(solution)/shard_map/all_to_all | solution.py:178
  65.5 0.7 %copy.12 = bf16[8,16,4,128]{3,2,0,1:T(4,128)(2,1)} copy(bf16[8,16,4,128]{3,2,1,0:T(4,128)(2,1)S(1)} %reshape.34) | data formatting | bytes 262144 | tf_op jit(solution)/shard_map/reshape | solution.py:179
  (15 shorter events, 0.1 us)
Async XLA Ops:
  1.1 11.4 %collective-permute-start.2 = (bf16[128,576]{1,0:T(8,128)(2,1)S(1)}, bf16[128,576]{1,0:T(8,128)(2,1)S(1)}, u32[]{:S(2)}, u32[]{:S(2)}) collective-permute-start(bf16[128,576]{1,0:T(8,128)(2,1)S(1)} %copy.13), channel_id=1, source_target_pairs={{0,4},{2,6},{4,0},{6,2},{8,12},{10,14},{12,8},{14,10},{1,5},{3,7},... | collective-permute-start | bytes 442376 | tf_op jit(solution)/shard_map/ppermute | solution.py:118
  4.2 8.3 %collective-permute-start.1 = (bf16[128,576]{1,0:T(8,128)(2,1)S(1)}, bf16[128,576]{1,0:T(8,128)(2,1)S(1)}, u32[]{:S(2)}, u32[]{:S(2)}) collective-permute-start(bf16[128,576]{1,0:T(8,128)(2,1)S(1)} %copy.13), channel_id=1, source_target_pairs={{0,2},{2,0},{4,6},{6,4},{8,10},{10,8},{12,14},{14,12},{1,3},{3,1},... | collective-permute-start | bytes 442376 | tf_op jit(solution)/shard_map/ppermute | solution.py:118
  5.7 9.8 %collective-permute-start = (bf16[128,576]{1,0:T(8,128)(2,1)S(1)}, bf16[128,576]{1,0:T(8,128)(2,1)S(1)}, u32[]{:S(2)}, u32[]{:S(2)}) collective-permute-start(bf16[128,576]{1,0:T(8,128)(2,1)S(1)} %copy.13), channel_id=1, source_target_pairs={{0,8},{2,10},{4,12},{6,14},{8,0},{10,2},{12,4},{14,6},{1,9},{3,11}... | collective-permute-start | bytes 442376 | tf_op jit(solution)/shard_map/ppermute | solution.py:118
  8.3 1.9 %copy-start.1 = (bf16[64,32,256]{2,1,0:T(8,128)(2,1)S(1)}, bf16[64,32,256]{2,1,0:T(8,128)(2,1)}, u32[]{:S(2)}) copy-start(bf16[64,32,256]{2,1,0:T(8,128)(2,1)} %param.7) | copy-start | bytes 3145732
  12.4 27.1 %copy-start.2 = (bf16[256,576]{0,1:T(8,128)(2,1)S(1)}, bf16[256,576]{0,1:T(8,128)(2,1)}, u32[]{:S(2)}) copy-start(bf16[256,576]{0,1:T(8,128)(2,1)} %param.6) | copy-start | bytes 884740
  15.5 21.8 %all-to-all-start = ((bf16[8,176,256]{2,1,0:T(8,128)(2,1)}), bf16[8,176,256]{2,1,0:T(8,128)(2,1)S(1)}, u32[]{:S(2)}, u32[]{:S(2)}) async-start(bf16[8,176,256]{2,1,0:T(8,128)(2,1)} %pad_maximum_fusion), calls=%async_computation | async-start | bytes 1441792 | tf_op jit(solution)/shard_map/all_to_all | solution.py:140
  19.3 13.6 %collective-permute-start.4 = (bf16[128,576]{1,0:T(8,128)(2,1)S(1)}, bf16[128,576]{1,0:T(8,128)(2,1)}, u32[]{:S(2)}, u32[]{:S(2)}) collective-permute-start(bf16[128,576]{1,0:T(8,128)(2,1)S(1)} %collective-permute-done.2), channel_id=1, source_target_pairs={{0,2},{2,0},{4,6},{6,4},{8,10},{10,8},{12,14},{14,12},{1,3},{3,1},... | collective-permute-start | bytes 442376 | tf_op jit(solution)/shard_map/ppermute | solution.py:118
  21.3 14.2 %collective-permute-start.8 = (bf16[128,576]{1,0:T(8,128)(2,1)S(1)}, bf16[128,576]{1,0:T(8,128)(2,1)S(1)}, u32[]{:S(2)}, u32[]{:S(2)}) collective-permute-start(bf16[128,576]{1,0:T(8,128)(2,1)S(1)} %collective-permute-done), channel_id=1, source_target_pairs={{0,2},{2,0},{4,6},{6,4},{8,10},{10,8},{12,14},{14,12},{1,3},{3,1},... | collective-permute-start | bytes 442376 | tf_op jit(solution)/shard_map/ppermute | solution.py:118
  21.3 16.0 %collective-permute-start.5 = (bf16[128,576]{1,0:T(8,128)(2,1)S(1)}, bf16[128,576]{1,0:T(8,128)(2,1)S(1)}, u32[]{:S(2)}, u32[]{:S(2)}) collective-permute-start(bf16[128,576]{1,0:T(8,128)(2,1)S(1)} %collective-permute-done.1), channel_id=1, source_target_pairs={{0,1},{1,0},{2,3},{3,2},{4,5},{5,4},{6,7},{7,6},{8,9},{9,8},{10,11... | collective-permute-start | bytes 442376 | tf_op jit(solution)/shard_map/ppermute | solution.py:132
  21.3 19.4 %collective-permute-start.6 = (bf16[128,576]{1,0:T(8,128)(2,1)S(1)}, bf16[128,576]{1,0:T(8,128)(2,1)}, u32[]{:S(2)}, u32[]{:S(2)}) collective-permute-start(bf16[128,576]{1,0:T(8,128)(2,1)S(1)} %collective-permute-done.2), channel_id=1, source_target_pairs={{0,1},{1,0},{2,3},{3,2},{4,5},{5,4},{6,7},{7,6},{8,9},{9,8},{10,11... | collective-permute-start | bytes 442376 | tf_op jit(solution)/shard_map/ppermute | solution.py:132
  21.8 19.0 %collective-permute-start.9 = (bf16[128,576]{1,0:T(8,128)(2,1)S(1)}, bf16[128,576]{1,0:T(8,128)(2,1)S(1)}, u32[]{:S(2)}, u32[]{:S(2)}) collective-permute-start(bf16[128,576]{1,0:T(8,128)(2,1)S(1)} %collective-permute-done), channel_id=1, source_target_pairs={{0,4},{2,6},{4,0},{6,2},{8,12},{10,14},{12,8},{14,10},{1,5},{3,7},... | collective-permute-start | bytes 442376 | tf_op jit(solution)/shard_map/ppermute | solution.py:118
  32.9 8.5 %collective-permute-start.7 = (bf16[128,576]{1,0:T(8,128)(2,1)}, bf16[128,576]{1,0:T(8,128)(2,1)}, u32[]{:S(2)}, u32[]{:S(2)}) collective-permute-start(bf16[128,576]{1,0:T(8,128)(2,1)} %collective-permute-done.4), channel_id=1, source_target_pairs={{0,1},{1,0},{2,3},{3,2},{4,5},{5,4},{6,7},{7,6},{8,9},{9,8},{10,11... | collective-permute-start | bytes 442376 | tf_op jit(solution)/shard_map/ppermute | solution.py:132
  35.5 6.0 %collective-permute-start.10 = (bf16[128,576]{1,0:T(8,128)(2,1)S(1)}, bf16[128,576]{1,0:T(8,128)(2,1)S(1)}, u32[]{:S(2)}, u32[]{:S(2)}) collective-permute-start(bf16[128,576]{1,0:T(8,128)(2,1)S(1)} %collective-permute-done.8), channel_id=1, source_target_pairs={{0,4},{2,6},{4,0},{6,2},{8,12},{10,14},{12,8},{14,10},{1,5},{3,7},... | collective-permute-start | bytes 442376 | tf_op jit(solution)/shard_map/ppermute | solution.py:118
  37.3 11.3 %collective-permute-start.3 = (bf16[8,128,256]{2,1,0:T(8,128)(2,1)S(1)}, bf16[8,128,256]{2,1,0:T(8,128)(2,1)S(1)}, u32[]{:S(2)}, u32[]{:S(2)}) collective-permute-start(bf16[8,128,256]{2,1,0:T(8,128)(2,1)S(1)} %slice.14), channel_id=1, source_target_pairs={{0,16},{16,0},{1,17},{17,1},{2,18},{18,2},{3,19},{19,3},{4,20},{20... | collective-permute-start | bytes 1572872 | tf_op jit(solution)/shard_map/ppermute | solution.py:145
  40.8 2.3 %collective-permute-start.11 = (bf16[128,576]{1,0:T(8,128)(2,1)S(1)}, bf16[128,576]{1,0:T(8,128)(2,1)S(1)}, u32[]{:S(2)}, u32[]{:S(2)}) collective-permute-start(bf16[128,576]{1,0:T(8,128)(2,1)S(1)} %collective-permute-done), channel_id=1, source_target_pairs={{0,1},{1,0},{2,3},{3,2},{4,5},{5,4},{6,7},{7,6},{8,9},{9,8},{10,11... | collective-permute-start | bytes 442376 | tf_op jit(solution)/shard_map/ppermute | solution.py:132
  40.9 2.3 %collective-permute-start.12 = (bf16[128,576]{1,0:T(8,128)(2,1)S(1)}, bf16[128,576]{1,0:T(8,128)(2,1)S(1)}, u32[]{:S(2)}, u32[]{:S(2)}) collective-permute-start(bf16[128,576]{1,0:T(8,128)(2,1)S(1)} %collective-permute-done.8), channel_id=1, source_target_pairs={{0,1},{1,0},{2,3},{3,2},{4,5},{5,4},{6,7},{7,6},{8,9},{9,8},{10,11... | collective-permute-start | bytes 442376 | tf_op jit(solution)/shard_map/ppermute | solution.py:132
  41.4 1.8 %collective-permute-start.13 = (bf16[128,576]{1,0:T(8,128)(2,1)S(1)}, bf16[128,576]{1,0:T(8,128)(2,1)S(1)}, u32[]{:S(2)}, u32[]{:S(2)}) collective-permute-start(bf16[128,576]{1,0:T(8,128)(2,1)S(1)} %collective-permute-done.9), channel_id=1, source_target_pairs={{0,1},{1,0},{2,3},{3,2},{4,5},{5,4},{6,7},{7,6},{8,9},{9,8},{10,11... | collective-permute-start | bytes 442376 | tf_op jit(solution)/shard_map/ppermute | solution.py:132
  41.4 1.7 %collective-permute-start.14 = (bf16[128,576]{1,0:T(8,128)(2,1)S(1)}, bf16[128,576]{1,0:T(8,128)(2,1)S(1)}, u32[]{:S(2)}, u32[]{:S(2)}) collective-permute-start(bf16[128,576]{1,0:T(8,128)(2,1)S(1)} %collective-permute-done.10), channel_id=1, source_target_pairs={{0,1},{1,0},{2,3},{3,2},{4,5},{5,4},{6,7},{7,6},{8,9},{9,8},{10,11... | collective-permute-start | bytes 442376 | tf_op jit(solution)/shard_map/ppermute | solution.py:132
  43.0 0.7 copy-start

commit v6 on v5

--- a/solution.py
+++ b/solution.py
@@ -13,12 +13,11 @@
 NOPE = 128
 VD = 128
 HIDDEN = -1e30
-CHUNK = 512
 EARLY = ((4, 0, 4), (1, 0, 1), (2, 0, 2))
 LATE = ((3, 2, 1), (5, 4, 1), (6, 4, 2), (7, 5, 2))
 
 
-def attend_kernel(slots, rows, pair, which, *refs):
+def attend_kernel(slots, pair, which, *refs):
     order_ref, start_ref, packed_ref = refs[:3]
     if which == 0:
         weight_ref = packed_ref
@@ -26,81 +25,74 @@
     else:
         weight_ref, done_ref = refs[3:5]
         refs = refs[5:]
-    piece_refs = refs[:5]
-    out_ref, latent, keys, values, sems = refs[5:]
-    near = slots // 2
+    own_ref, *piece_refs, out_ref = refs
     me = lax.axis_index("ctx")
     core = lax.axis_index("tp")
-    places = [
-        latent.at[0],
-        latent.at[pl.ds(1, near - 1), core],
-        latent.at[pl.ds(1, near - 1), 1 - core],
-        latent.at[pl.ds(near, near), core],
-        latent.at[pl.ds(near, near), 1 - core],
-    ]
-    copies = [
-        pltpu.make_async_copy(piece, place, sems.at[index])
-        for index, (piece, place) in enumerate(zip(piece_refs, places))
-    ]
-    for copy in copies:
-        copy.start()
-    for copy in copies:
-        copy.wait()
+    rows = own_ref.shape[1]
+    half = rows // 2
     width = NOPE + VD
     depth = LAT // slots
     query_rows = (packed_ref.shape[1] - pair * depth) // 3
     query_count = slots * query_rows
     scale = math.log2(math.e) / math.sqrt(NOPE + ROPE)
-    rope = latent[..., LAT:].reshape(slots * rows, ROPE)
-    tail = jnp.concatenate([rope, jnp.zeros_like(rope)], axis=1)
-    for buffer in range(2):
-        keys[buffer, :, NOPE:] = tail
-    ahead = lax.broadcasted_iota(jnp.int32, (query_count, rows), 1) - lax.broadcasted_iota(
-        jnp.int32, (query_count, rows), 0
-    )
-    limits = [start_ref[0] - order_ref[me ^ slot] * rows for slot in range(slots)]
     first = pair * depth
-    place = 0
-    if which == 1:
-        group = lax.axis_index("groups")
-        out_ref[:, pl.ds(pl.multiple_of(group * pair * VD, pair * VD), pair * VD)] = done_ref[...]
-        place = pl.multiple_of((1 - group) * pair * VD, pair * VD)
-    results = []
+    weights, queries = [], []
     for member in range(pair):
         head = which * pair + member
-        buffer = member % 2
-        weight = weight_ref[:, member * depth:(member + 1) * depth, :].reshape(LAT, width)
-        for begin in range(0, slots * rows, CHUNK):
-            part = pl.ds(begin, CHUNK)
-            held = latent[begin // rows:(begin + CHUNK) // rows, :, :, :LAT].reshape(CHUNK, LAT)
-            projected = jnp.dot(held, weight, preferred_element_type=jnp.float32)
-            projected = projected.astype(jnp.bfloat16)
-            keys[buffer, part, :NOPE] = projected[:, :NOPE]
-            values[buffer, part, :] = projected[:, NOPE:]
+        weights.append(weight_ref[:, member * depth:(member + 1) * depth, :].reshape(LAT, width))
         begin = first + which * query_rows
         part = packed_ref[:, begin:begin + query_rows, member * NOPE:(member + 1) * NOPE]
         part = part.reshape(query_count, NOPE)
         begin = first + 2 * query_rows
         turned = packed_ref[:, begin:begin + query_rows, head * ROPE:(head + 1) * ROPE]
         turned = turned.reshape(query_count, ROPE)
-        query = jnp.concatenate([part, turned, jnp.zeros_like(turned)], axis=1)
-        scores = lax.dot_general(
-            query, keys[buffer], (((1,), (1,)), ((), ())), preferred_element_type=jnp.float32
+        queries.append(jnp.concatenate([part, turned, jnp.zeros_like(turned)], axis=1))
+    weights = jnp.concatenate(weights, axis=1).T
+    ahead = lax.broadcasted_iota(jnp.int32, (query_count, half), 1) - lax.broadcasted_iota(
+        jnp.int32, (query_count, half), 0
+    )
+    scores = [[] for _ in range(pair)]
+    values = [[] for _ in range(pair)]
+    for base in range(0, slots, 4):
+        parts, visible = [], []
+        for slot in range(base, base + 4):
+            places = (0, half)
+            if slot > 0:
+                places = (core * half, (1 - core) * half)
+                parts += [piece_refs[2 * slot - 2][...], piece_refs[2 * slot - 1][...]]
+            else:
+                parts.append(own_ref[...])
+            limit = start_ref[0] - order_ref[me ^ slot] * rows
+            visible += [ahead <= limit - place for place in places]
+        latent = jnp.concatenate(parts, axis=1)
+        visible = jnp.concatenate(visible, axis=1)
+        projected = jnp.dot(weights, latent[:LAT], preferred_element_type=jnp.float32)
+        projected = projected.astype(jnp.bfloat16)
+        rope = latent[LAT:]
+        for member in range(pair):
+            begin = member * width
+            keys = jnp.concatenate(
+                [projected[begin:begin + NOPE], rope, jnp.zeros_like(rope)], axis=0
+            )
+            score = jnp.dot(queries[member], keys, preferred_element_type=jnp.float32)
+            scores[member].append(jnp.where(visible, score, HIDDEN))
+            values[member].append(projected[begin + NOPE:begin + width])
+    results = []
+    for member in range(pair):
+        score = jnp.concatenate(scores[member], axis=1)
+        top = jnp.max(score, axis=1, keepdims=True)
+        probs = jnp.exp2((score - top) * scale)
+        totals = jnp.sum(probs, axis=1, keepdims=True)
+        result = lax.dot_general(
+            probs.astype(jnp.bfloat16), jnp.concatenate(values[member], axis=1),
+            (((1,), (1,)), ((), ())), preferred_element_type=jnp.float32,
         )
-        scores = jnp.concatenate(
-            [
-                jnp.where(
-                    ahead <= limits[slot], scores[:, slot * rows:(slot + 1) * rows], HIDDEN
-                )
-                for slot in range(slots)
-            ],
-            axis=1,
-        )
-        top = jnp.max(scores, axis=1, keepdims=True)
-        probs = jnp.exp2((scores - top) * scale)
-        totals = jnp.sum(probs, axis=1, keepdims=True)
-        result = jnp.dot(probs.astype(jnp.bfloat16), values[buffer], preferred_element_type=jnp.float32)
         results.append((result / totals).astype(jnp.bfloat16))
+    place = 0
+    if which == 1:
+        group = lax.axis_index("groups")
+        out_ref[:, pl.ds(pl.multiple_of(group * pair * VD, pair * VD), pair * VD)] = done_ref[...]
+        place = pl.multiple_of((1 - group) * pair * VD, pair * VD)
     out_ref[:, pl.ds(place, pair * VD)] = jnp.concatenate(results, axis=1)
 
 
@@ -132,41 +124,32 @@
         return lax.ppermute(array, "tp", [(0, 1), (1, 0)])
 
     core = lax.axis_index("tp")
-    held = {0: lax.dynamic_slice_in_dim(latent_cache, core * half, half, 0)}
+    turned_cache = latent_cache.T
+    held = {0: lax.dynamic_slice_in_dim(turned_cache, core * half, half, 1)}
     for slot, source, bit in EARLY:
         held[slot] = swap(held[source], bit)
-    waited = lax.optimization_barrier((packed, latent_cache, held[4], held[1], held[2]))
-    packed, latent_cache, held[4], held[1], held[2] = waited
+    waited = lax.optimization_barrier((packed, held[4], held[1], held[2]))
+    packed, held[4], held[1], held[2] = waited
     packed = lax.all_to_all(packed, "ctx", 0, 0, tiled=True)
     for slot, source, bit in LATE:
         held[slot] = swap(held[source], bit)
-    near = contexts // 2
-    close = jnp.stack([held[slot] for slot in range(1, near)])
+    traded = {slot: trade(held[slot]) for slot in (1, 2)}
+    packed, held[3], held[5], held[6], traded[1], traded[2] = lax.optimization_barrier((packed, held[3], held[5], held[6], traded[1], traded[2]))
     other = lax.ppermute(packed[:, :pair * depth], "groups", [(0, 1), (1, 0)])
-    far = jnp.stack([held[slot] for slot in range(near, contexts)])
-    own = latent_cache.reshape(cores, half, latent_cache.shape[1])
-    close_other = jnp.stack([trade(held[slot]) for slot in range(1, near)])
-    far_other = jnp.stack([trade(held[slot]) for slot in range(near, contexts)])
-    pieces = [own, close, close_other, far, far_other]
-
-    total_rows = contexts * rows
+    pieces = [turned_cache]
+    for slot in range(1, contexts):
+        pieces += [held[slot], traded.get(slot, None) if slot in traded else trade(held[slot])]
+
     query_count = contexts * query_rows
-    anywhere = pl.BlockSpec(memory_space=pl.ANY)
     on_chip = pl.BlockSpec(memory_space=pltpu.VMEM)
     scalars = pl.BlockSpec(memory_space=pltpu.SMEM)
 
     def attend(which, out_heads, operands):
         return pl.pallas_call(
-            functools.partial(attend_kernel, contexts, rows, pair, which),
+            functools.partial(attend_kernel, contexts, pair, which),
             out_shape=jax.ShapeDtypeStruct((query_count, out_heads * VD), jnp.bfloat16),
-            in_specs=[scalars, scalars] + [on_chip] * len(operands) + [anywhere] * len(pieces),
+            in_specs=[scalars, scalars] + [on_chip] * (len(operands) + len(pieces)),
             out_specs=on_chip,
-            scratch_shapes=[
-                pltpu.VMEM((contexts, cores, half, LAT + ROPE), jnp.bfloat16),
-                pltpu.VMEM((2, total_rows, 256), jnp.bfloat16),
-                pltpu.VMEM((2, total_rows, VD), jnp.bfloat16),
-                pltpu.SemaphoreType.DMA((len(pieces),)),
-            ],
             compiler_params=pltpu.CompilerParams(vmem_limit_bytes=16 * 2**20),
             cost_estimate=pl.CostEstimate(flops=1048576, bytes_accessed=1 << 20, transcendentals=0),
             name="attend_" + ("first", "second")[which],

time: 66.5 us -> 66 us (level)
  waiting for transfers between devices: 16.4 us -> 21.9 us
  other arithmetic: 3.55 us -> 1.21 us
  Pallas kernels: 7.39 us -> 5.63 us
  blocking collectives: 13.2 us -> 12.1 us
    ppermute x7, waiting for transfers between devices: 14.6 us -> 18.3 us  [swap(): return lax.ppermute(array, 'ctx', [(i, i ^ bit) for i in range(contexts)])]
    another operation x4 -> x0, other arithmetic: 2.34 us -> none  [the longest x1 1.08 us: split_by_heads(): close_other = jnp.stack([trade(held[slot]) for slot in range(1, near)])]
    all_to_all x1, waiting for transfers between devices: 0.51 us -> 2.34 us  [split_by_heads(): packed = lax.all_to_all(packed, 'ctx', 0, 0, tiled=True)]
    pallas_call x2, Pallas kernels: 7.39 us -> 5.63 us  [attend(): pl.pallas_call(functools.partial(attend_kernel, contexts, pair, which), o...]
    all_to_all x1, blocking collectives: 13.2 us -> 12.1 us  [split_by_heads(): attended = lax.all_to_all(attended, 'ctx', 0, 0, tiled=True)]
    ppermute x7, starting transfers between devices: 12.5 us -> 11.6 us  [swap(): return lax.ppermute(array, 'ctx', [(i, i ^ bit) for i in range(contexts)])]
  transfers between devices with their start and end apart: 16 -> 16, of which waited for: 5 -> 9; matrix products, arithmetic and copies ran while one was open for 10% -> 6% of each run, Pallas kernels for 6% -> 4%
where the time goes in v6:
time: 66 us; the launch traced here: 65.8 us
  waiting for transfers between devices  21.9 us (33%)
  starting transfers between devices  19 us (29%)
  blocking collectives  12.1 us (18%)
  Pallas kernels  5.63 us (9%)
  local copies, waits for them, and re-layouts  5.17 us (8%)
  other arithmetic  1.21 us (2%)
  between operations  0.8 us (1%)
    ppermute x7, waiting for transfers between devices, swap(): return lax.ppermute(array, 'ctx', [(i, i ^ bit) for i in range(contexts)])  18.3 us
    all_to_all x1, blocking collectives, split_by_heads(): attended = lax.all_to_all(attended, 'ctx', 0, 0, tiled=True)  12.1 us
    ppermute x7, starting transfers between devices, swap(): return lax.ppermute(array, 'ctx', [(i, i ^ bit) for i in range(contexts)])  11.6 us
    pallas_call x2, Pallas kernels, attend(): pl.pallas_call(functools.partial(attend_kernel, contexts, pair, which), o...  5.63 us
    all_to_all x1, starting transfers between devices, split_by_heads(): packed = lax.all_to_all(packed, 'ctx', 0, 0, tiled=True)  4.25 us
    all_to_all x1, waiting for transfers between devices, split_by_heads(): packed = lax.all_to_all(packed, 'ctx', 0, 0, tiled=True)  2.34 us
    ppermute x1, starting transfers between devices, split_by_heads(): other = lax.ppermute(packed[:, :pair * depth], 'groups', [(0, 1), (1, 0)])  1.58 us
    dynamic_slice x1, local copies, waits for them, and re-layouts, split_by_heads(): held = {0: lax.dynamic_slice_in_dim(turned_cache, core * half, half, 1)}  1.58 us
  transfers between devices with their start and end apart: 16, of which 9 were waited for; matrix products, arithmetic and copies ran while one was open for 6% of the time, Pallas kernels for 4%

profile of v6, /device:TPU:0, one launch (start us, length us, event | category | flops | bytes accessed | tf_op | source)
XLA Modules:
  0.0 65.8 jit_solution(16875594782694058860)
XLA Ops:
  0.0 1.6 %dynamic-slice_bitcast_fusion = bf16[576,128]{1,0:T(8,128)(2,1)} fusion(bf16[256,576]{0,1:T(8,128)(2,1)} %param.6, s32[]{:T(128)S(6)} %select_n.18), kind=kLoop, calls=%fused_computation.2 | loop fusion | bytes 294916 | tf_op jit(solution)/shard_map/dynamic_slice | solution.py:128
  1.6 4.0 %collective-permute-start = (bf16[576,128]{1,0:T(8,128)(2,1)}, bf16[576,128]{1,0:T(8,128)(2,1)S(1)}, u32[]{:S(2)}, u32[]{:S(2)}) collective-permute-start(bf16[576,128]{1,0:T(8,128)(2,1)} %dynamic-slice_bitcast_fusion), channel_id=1, source_target_pairs={{0,8},{2,10},{4,12},{6,14},{8,0},{10,2},{12,4},{14,6},{1,9},{3,11}... | collective-permute-start | bytes 442376 | tf_op jit(solution)/shard_map/ppermute | solution.py:110
  5.6 1.5 %collective-permute-start.1 = (bf16[576,128]{1,0:T(8,128)(2,1)}, bf16[576,128]{1,0:T(8,128)(2,1)S(1)}, u32[]{:S(2)}, u32[]{:S(2)}) collective-permute-start(bf16[576,128]{1,0:T(8,128)(2,1)} %dynamic-slice_bitcast_fusion), channel_id=1, source_target_pairs={{0,2},{2,0},{4,6},{6,4},{8,10},{10,8},{12,14},{14,12},{1,3},{3,1},... | collective-permute-start | bytes 442376 | tf_op jit(solution)/shard_map/ppermute | solution.py:110
  7.1 1.6 %collective-permute-start.2 = (bf16[576,128]{1,0:T(8,128)(2,1)}, bf16[576,128]{1,0:T(8,128)(2,1)S(1)}, u32[]{:S(2)}, u32[]{:S(2)}) collective-permute-start(bf16[576,128]{1,0:T(8,128)(2,1)} %dynamic-slice_bitcast_fusion), channel_id=1, source_target_pairs={{0,4},{2,6},{4,0},{6,2},{8,12},{10,14},{12,8},{14,10},{1,5},{3,7},... | collective-permute-start | bytes 442376 | tf_op jit(solution)/shard_map/ppermute | solution.py:110
  8.7 1.1 %reshape.26 = bf16[16,8,2,2,192]{4,3,2,1,0:T(2,128)(2,1)S(1)} reshape(bf16[16,32,192]{2,1,0:T(8,128)(2,1)} %param.5) | data formatting | bytes 393216 | tf_op jit(solution)/shard_map/reshape | solution.py:115
  9.8 0.2 copy.8
  10.0 0.3 broadcast_select_fusion
  10.3 0.1 slice_bitcast_fusion
  10.4 0.1 slice_bitcast_fusion.1
  10.5 0.4 reshape.24
  10.9 0.4 constant_dynamic-slice_fusion
  11.3 0.1 reshape.28
  11.5 0.1 copy.9
  11.6 0.1 reshape.27
  11.7 0.2 copy.6
  11.9 0.9 %pad_maximum_fusion = bf16[8,176,256]{2,1,0:T(8,128)(2,1)} fusion(bf16[8,16,256]{2,1,0:T(8,128)(2,1)S(1)} %reshape.28, bf16[8,32,256]{2,1,0:T(8,128)(2,1)S(1)} %reshape.27, bf16[8,128,256]{2,1,0:T(8,128)(2,1)S(1)} %bitcast.19), kind=kLoop, calls=%fused_computation | loop fusion | flops 2162688 | bytes 1441792 | tf_op jit(solution)/shard_map/concatenate | solution.py:121
  12.8 0.1 collective-permute-done.refs_10_.refs_12_
  12.9 0.0 collective-permute-done.1.refs_4_.refs_6_
  12.9 1.4 %collective-permute-done.2.refs_6_.refs_8_ = bf16[576,128]{1,0:T(8,128)(2,1)S(1)} collective-permute-done((bf16[576,128]{1,0:T(8,128)(2,1)}, bf16[576,128]{1,0:T(8,128)(2,1)S(1)}, u32[]{:S(2)}, u32[]{:S(2)}) %collective-permute-start.2) | collective-permute-done | bytes 147488 | tf_op jit(solution)/shard_map/ppermute | solution.py:110
  14.3 4.2 %all-to-all-start = ((bf16[8,176,256]{2,1,0:T(8,128)(2,1)}), bf16[8,176,256]{2,1,0:T(8,128)(2,1)S(1)}, u32[]{:S(2)}, u32[]{:S(2)}) async-start(bf16[8,176,256]{2,1,0:T(8,128)(2,1)} %pad_maximum_fusion), calls=%async_computation | async-start | bytes 1441792 | tf_op jit(solution)/shard_map/all_to_all | solution.py:133
  18.6 2.0 %collective-permute-start.3 = (bf16[576,128]{1,0:T(8,128)(2,1)S(1)}, bf16[576,128]{1,0:T(8,128)(2,1)S(1)}, u32[]{:S(2)}, u32[]{:S(2)}) collective-permute-start(bf16[576,128]{1,0:T(8,128)(2,1)S(1)} %collective-permute-done.2.refs_6_.refs_8_), channel_id=1, source_target_pairs={{0,2},{2,0},{4,6},{6,4},{8,10},{10,8},{12,14},{14,12},{1,3},{3,1},... | collective-permute-start | bytes 442376 | tf_op jit(solution)/shard_map/ppermute | solution.py:110
  20.6 0.0 collective-permute-start.4
  20.7 2.0 %collective-permute-start.5 = (bf16[576,128]{1,0:T(8,128)(2,1)S(1)}, bf16[576,128]{1,0:T(8,128)(2,1)S(1)}, u32[]{:S(2)}, u32[]{:S(2)}) collective-permute-start(bf16[576,128]{1,0:T(8,128)(2,1)S(1)} %collective-permute-done.refs_10_.refs_12_), channel_id=1, source_target_pairs={{0,4},{2,6},{4,0},{6,2},{8,12},{10,14},{12,8},{14,10},{1,5},{3,7},... | collective-permute-start | bytes 442376 | tf_op jit(solution)/shard_map/ppermute | solution.py:110
  22.6 0.0 collective-permute-start.6
  22.6 0.5 collective-permute-start.7
  23.2 9.2 %collective-permute-done.3.refs_8_.refs_10_ = bf16[576,128]{1,0:T(8,128)(2,1)S(1)} collective-permute-done((bf16[576,128]{1,0:T(8,128)(2,1)S(1)}, bf16[576,128]{1,0:T(8,128)(2,1)S(1)}, u32[]{:S(2)}, u32[]{:S(2)}) %collective-permute-start.3) | collective-permute-done | bytes 147488 | tf_op jit(solution)/shard_map/ppermute | solution.py:110
  32.3 2.9 %collective-permute-done.4.refs_12_.refs_14_ = bf16[576,128]{1,0:T(8,128)(2,1)S(1)} collective-permute-done((bf16[576,128]{1,0:T(8,128)(2,1)S(1)}, bf16[576,128]{1,0:T(8,128)(2,1)S(1)}, u32[]{:S(2)}, u32[]{:S(2)}) %collective-permute-start.4) | collective-permute-done | bytes 147488 | tf_op jit(solution)/shard_map/ppermute | solution.py:110
  35.2 0.0 collective-permute-done.5.refs_14_.refs_16_
  35.2 0.0 collective-permute-done.6.refs_5_.refs_7_
  35.2 0.0 collective-permute-done.7.refs_7_.refs_9_
  35.2 2.3 %all-to-all-done.refs_2_ = bf16[8,176,256]{2,1,0:T(8,128)(2,1)S(1)} async-done(((bf16[8,176,256]{2,1,0:T(8,128)(2,1)}), bf16[8,176,256]{2,1,0:T(8,128)(2,1)S(1)}, u32[]{:S(2)}, u32[]{:S(2)}) %all-to-all-start) | async-done | bytes 720928 | tf_op jit(solution)/shard_map/all_to_all | solution.py:133
  37.6 1.6 %collective-permute-start.8 = (bf16[8,128,256]{2,1,0:T(8,128)(2,1)S(1)}, bf16[8,128,256]{2,1,0:T(8,128)(2,1)S(1)}, u32[]{:S(2)}, u32[]{:S(2)}) collective-permute-start(bf16[8,128,256]{2,1,0:T(8,128)(2,1)S(1)} %slice.11), channel_id=1, source_target_pairs={{0,16},{16,0},{1,17},{17,1},{2,18},{18,2},{3,19},{19,3},{4,20},{20... | collective-permute-start | bytes 1572872 | tf_op jit(solution)/shard_map/ppermute | solution.py:138
  39.1 0.4 collective-permute-start.13
  39.6 0.0 collective-permute-start.10
  39.6 4.7 %collective-permute-done.13.refs_16_.refs_18_ = bf16[576,128]{1,0:T(8,128)(2,1)S(1)} collective-permute-done((bf16[576,128]{1,0:T(8,128)(2,1)S(1)}, bf16[576,128]{1,0:T(8,128)(2,1)S(1)}, u32[]{:S(2)}, u32[]{:S(2)}) %collective-permute-start.13) | collective-permute-done | bytes 147488 | tf_op jit(solution)/shard_map/ppermute | solution.py:110
  44.3 0.0 collective-permute-start.14
  44.3 0.5 collective-permute-start.9
  44.8 0.0 collective-permute-start.11
  44.8 0.0 collective-permute-done.10.refs_11_.refs_13_
  44.8 0.5 collective-permute-start.12
  46.0 0.0 collective-permute-done.9.refs_9_.refs_11_
  46.0 0.2 collective-permute-done.11.refs_13_.refs_15_
  46.2 0.2 collective-permute-done.12.refs_15_.refs_17_
  46.4 2.8 %attend_first.1.refs_4_ = bf16[128,256]{1,0:T(8,128)(2,1)S(1)} custom-call(s32[8]{0:T(128)S(1)} %copy-done.1, s32[1]{0:T(128)S(6)} %copy.11.refs_1_, bf16[8,176,256]{2,1,0:T(8,128)(2,1)S(1)} %all-to-all-done.refs_2_, bf16[576,256]{1,0:T(8,128)(2,1)S(1)} %bitcast.16, bf16[576,128]{1,0:T(8,128)(2,1)S(1)} %collective-permute-done.1.refs_4_.refs_6_, ...), custom_call_target="tpu_custom_call" | custom-call | flops 1048576 | bytes 1048576 | tf_op jit(solution)/shard_map/attend_first/pallas_call | solution.py:148
  49.2 0.9 %collective-permute-done.8.refs_3_ = bf16[8,128,256]{2,1,0:T(8,128)(2,1)S(1)} collective-permute-done((bf16[8,128,256]{2,1,0:T(8,128)(2,1)S(1)}, bf16[8,128,256]{2,1,0:T(8,128)(2,1)S(1)}, u32[]{:S(2)}, u32[]{:S(2)}) %collective-permute-start.8) | collective-permute-done | bytes 524320 | tf_op jit(solution)/shard_map/ppermute | solution.py:138
  50.1 2.8 %attend_second.1 = bf16[128,512]{1,0:T(8,128)(2,1)S(1)} custom-call(s32[8]{0:T(128)S(1)} %copy-done.1, s32[1]{0:T(128)S(6)} %copy.11.refs_1_, bf16[8,176,256]{2,1,0:T(8,128)(2,1)S(1)} %all-to-all-done.refs_2_, bf16[8,128,256]{2,1,0:T(8,128)(2,1)S(1)} %collective-permute-done.8.refs_3_, bf16[128,256]{1,0:T(8,128)(2,1)S(1)} %attend_first.1.refs_4_, ...), custom_call_target="tpu_custom_call" | custom-call | flops 1048576 | bytes 1048576 | tf_op jit(solution)/shard_map/attend_second/pallas_call | solution.py:148
  52.9 12.1 %all_to_all.10 = bf16[8,16,512]{2,1,0:T(8,128)(2,1)S(1)} all-to-all(bf16[8,16,512]{2,1,0:T(8,128)(2,1)S(1)} %bitcast.18), channel_id=1, replica_groups=mesh['groups'=2,'ctx'=8,'tp'=2] {'ctx'}, dimensions={0} | all-to-all | bytes 262144 | tf_op jit(solution)/shard_map/all_to_all | solution.py:161
  65.1 0.7 %copy.10 = bf16[8,16,4,128]{3,2,0,1:T(4,128)(2,1)} copy(bf16[8,16,4,128]{3,2,1,0:T(4,128)(2,1)S(1)} %reshape.30) | data formatting | bytes 262144 | tf_op jit(solution)/shard_map/reshape | solution.py:162
  (9 shorter events, 0.1 us)
Async XLA Ops:
  1.6 8.9 %copy-start.2 = (bf16[64,32,256]{2,1,0:T(8,128)(2,1)S(1)}, bf16[64,32,256]{2,1,0:T(8,128)(2,1)}, u32[]{:S(2)}) copy-start(bf16[64,32,256]{2,1,0:T(8,128)(2,1)} %param.7) | copy-start | bytes 3145732
  1.6 11.4 %collective-permute-start = (bf16[576,128]{1,0:T(8,128)(2,1)}, bf16[576,128]{1,0:T(8,128)(2,1)S(1)}, u32[]{:S(2)}, u32[]{:S(2)}) collective-permute-start(bf16[576,128]{1,0:T(8,128)(2,1)} %dynamic-slice_bitcast_fusion), channel_id=1, source_target_pairs={{0,8},{2,10},{4,12},{6,14},{8,0},{10,2},{12,4},{14,6},{1,9},{3,11}... | collective-permute-start | bytes 442376 | tf_op jit(solution)/shard_map/ppermute | solution.py:110
  5.6 7.3 %collective-permute-start.1 = (bf16[576,128]{1,0:T(8,128)(2,1)}, bf16[576,128]{1,0:T(8,128)(2,1)S(1)}, u32[]{:S(2)}, u32[]{:S(2)}) collective-permute-start(bf16[576,128]{1,0:T(8,128)(2,1)} %dynamic-slice_bitcast_fusion), channel_id=1, source_target_pairs={{0,2},{2,0},{4,6},{6,4},{8,10},{10,8},{12,14},{14,12},{1,3},{3,1},... | collective-permute-start | bytes 442376 | tf_op jit(solution)/shard_map/ppermute | solution.py:110
  7.1 7.2 %collective-permute-start.2 = (bf16[576,128]{1,0:T(8,128)(2,1)}, bf16[576,128]{1,0:T(8,128)(2,1)S(1)}, u32[]{:S(2)}, u32[]{:S(2)}) collective-permute-start(bf16[576,128]{1,0:T(8,128)(2,1)} %dynamic-slice_bitcast_fusion), channel_id=1, source_target_pairs={{0,4},{2,6},{4,0},{6,2},{8,12},{10,14},{12,8},{14,10},{1,5},{3,7},... | collective-permute-start | bytes 442376 | tf_op jit(solution)/shard_map/ppermute | solution.py:110
  12.8 33.6 %copy-start = (bf16[256,576]{0,1:T(8,128)(2,1)S(1)}, bf16[256,576]{0,1:T(8,128)(2,1)}, u32[]{:S(2)}) copy-start(bf16[256,576]{0,1:T(8,128)(2,1)} %param.6) | copy-start | bytes 884740
  12.8 33.6 %copy-start.1 = (s32[8]{0:T(128)S(1)}, s32[8]{0:T(128)}, u32[]{:S(2)}) copy-start(s32[8]{0:T(128)} %refs_0_.3) | copy-start | bytes 100
  14.3 23.2 %all-to-all-start = ((bf16[8,176,256]{2,1,0:T(8,128)(2,1)}), bf16[8,176,256]{2,1,0:T(8,128)(2,1)S(1)}, u32[]{:S(2)}, u32[]{:S(2)}) async-start(bf16[8,176,256]{2,1,0:T(8,128)(2,1)} %pad_maximum_fusion), calls=%async_computation | async-start | bytes 1441792 | tf_op jit(solution)/shard_map/all_to_all | solution.py:133
  18.6 13.7 %collective-permute-start.3 = (bf16[576,128]{1,0:T(8,128)(2,1)S(1)}, bf16[576,128]{1,0:T(8,128)(2,1)S(1)}, u32[]{:S(2)}, u32[]{:S(2)}) collective-permute-start(bf16[576,128]{1,0:T(8,128)(2,1)S(1)} %collective-permute-done.2.refs_6_.refs_8_), channel_id=1, source_target_pairs={{0,2},{2,0},{4,6},{6,4},{8,10},{10,8},{12,14},{14,12},{1,3},{3,1},... | collective-permute-start | bytes 442376 | tf_op jit(solution)/shard_map/ppermute | solution.py:110
  20.6 14.6 %collective-permute-start.4 = (bf16[576,128]{1,0:T(8,128)(2,1)S(1)}, bf16[576,128]{1,0:T(8,128)(2,1)S(1)}, u32[]{:S(2)}, u32[]{:S(2)}) collective-permute-start(bf16[576,128]{1,0:T(8,128)(2,1)S(1)} %collective-permute-done.refs_10_.refs_12_), channel_id=1, source_target_pairs={{0,2},{2,0},{4,6},{6,4},{8,10},{10,8},{12,14},{14,12},{1,3},{3,1},... | collective-permute-start | bytes 442376 | tf_op jit(solution)/shard_map/ppermute | solution.py:110
  20.7 14.5 %collective-permute-start.5 = (bf16[576,128]{1,0:T(8,128)(2,1)S(1)}, bf16[576,128]{1,0:T(8,128)(2,1)S(1)}, u32[]{:S(2)}, u32[]{:S(2)}) collective-permute-start(bf16[576,128]{1,0:T(8,128)(2,1)S(1)} %collective-permute-done.refs_10_.refs_12_), channel_id=1, source_target_pairs={{0,4},{2,6},{4,0},{6,2},{8,12},{10,14},{12,8},{14,10},{1,5},{3,7},... | collective-permute-start | bytes 442376 | tf_op jit(solution)/shard_map/ppermute | solution.py:110
  22.6 12.5 %collective-permute-start.6 = (bf16[576,128]{1,0:T(8,128)(2,1)S(1)}, bf16[576,128]{1,0:T(8,128)(2,1)S(1)}, u32[]{:S(2)}, u32[]{:S(2)}) collective-permute-start(bf16[576,128]{1,0:T(8,128)(2,1)S(1)} %collective-permute-done.1.refs_4_.refs_6_), channel_id=1, source_target_pairs={{0,1},{1,0},{2,3},{3,2},{4,5},{5,4},{6,7},{7,6},{8,9},{9,8},{10,11... | collective-permute-start | bytes 442376 | tf_op jit(solution)/shard_map/ppermute | solution.py:124
  22.6 12.5 %collective-permute-start.7 = (bf16[576,128]{1,0:T(8,128)(2,1)S(1)}, bf16[576,128]{1,0:T(8,128)(2,1)S(1)}, u32[]{:S(2)}, u32[]{:S(2)}) collective-permute-start(bf16[576,128]{1,0:T(8,128)(2,1)S(1)} %collective-permute-done.2.refs_6_.refs_8_), channel_id=1, source_target_pairs={{0,1},{1,0},{2,3},{3,2},{4,5},{5,4},{6,7},{7,6},{8,9},{9,8},{10,11... | collective-permute-start | bytes 442376 | tf_op jit(solution)/shard_map/ppermute | solution.py:124
  37.6 12.5 %collective-permute-start.8 = (bf16[8,128,256]{2,1,0:T(8,128)(2,1)S(1)}, bf16[8,128,256]{2,1,0:T(8,128)(2,1)S(1)}, u32[]{:S(2)}, u32[]{:S(2)}) collective-permute-start(bf16[8,128,256]{2,1,0:T(8,128)(2,1)S(1)} %slice.11), channel_id=1, source_target_pairs={{0,16},{16,0},{1,17},{17,1},{2,18},{18,2},{3,19},{19,3},{4,20},{20... | collective-permute-start | bytes 1572872 | tf_op jit(solution)/shard_map/ppermute | solution.py:138
  39.1 5.1 %collective-permute-start.13 = (bf16[576,128]{1,0:T(8,128)(2,1)S(1)}, bf16[576,128]{1,0:T(8,128)(2,1)S(1)}, u32[]{:S(2)}, u32[]{:S(2)}) collective-permute-start(bf16[576,128]{1,0:T(8,128)(2,1)S(1)} %collective-permute-done.4.refs_12_.refs_14_), channel_id=1, source_target_pairs={{0,4},{2,6},{4,0},{6,2},{8,12},{10,14},{12,8},{14,10},{1,5},{3,7},... | collective-permute-start | bytes 442376 | tf_op jit(solution)/shard_map/ppermute | solution.py:110
  39.6 5.2 %collective-permute-start.10 = (bf16[576,128]{1,0:T(8,128)(2,1)S(1)}, bf16[576,128]{1,0:T(8,128)(2,1)S(1)}, u32[]{:S(2)}, u32[]{:S(2)}) collective-permute-start(bf16[576,128]{1,0:T(8,128)(2,1)S(1)} %collective-permute-done.refs_10_.refs_12_), channel_id=1, source_target_pairs={{0,1},{1,0},{2,3},{3,2},{4,5},{5,4},{6,7},{7,6},{8,9},{9,8},{10,11... | collective-permute-start | bytes 442376 | tf_op jit(solution)/shard_map/ppermute | solution.py:124
  44.3 1.7 %collective-permute-start.14 = (bf16[576,128]{1,0:T(8,128)(2,1)S(1)}, bf16[576,128]{1,0:T(8,128)(2,1)S(1)}, u32[]{:S(2)}, u32[]{:S(2)}) collective-permute-start(bf16[576,128]{1,0:T(8,128)(2,1)S(1)} %collective-permute-done.13.refs_16_.refs_18_), channel_id=1, source_target_pairs={{0,1},{1,0},{2,3},{3,2},{4,5},{5,4},{6,7},{7,6},{8,9},{9,8},{10,11... | collective-permute-start | bytes 442376 | tf_op jit(solution)/shard_map/ppermute | solution.py:124
  44.3 1.7 %collective-permute-start.9 = (bf16[576,128]{1,0:T(8,128)(2,1)S(1)}, bf16[576,128]{1,0:T(8,128)(2,1)S(1)}, u32[]{:S(2)}, u32[]{:S(2)}) collective-permute-start(bf16[576,128]{1,0:T(8,128)(2,1)S(1)} %collective-permute-done.3.refs_8_.refs_10_), channel_id=1, source_target_pairs={{0,1},{1,0},{2,3},{3,2},{4,5},{5,4},{6,7},{7,6},{8,9},{9,8},{10,11... | collective-permute-start | bytes 442376 | tf_op jit(solution)/shard_map/ppermute | solution.py:124
  44.8 1.4 %collective-permute-start.11 = (bf16[576,128]{1,0:T(8,128)(2,1)S(1)}, bf16[576,128]{1,0:T(8,128)(2,1)S(1)}, u32[]{:S(2)}, u32[]{:S(2)}) collective-permute-start(bf16[576,128]{1,0:T(8,128)(2,1)S(1)} %collective-permute-done.4.refs_12_.refs_14_), channel_id=1, source_target_pairs={{0,1},{1,0},{2,3},{3,2},{4,5},{5,4},{6,7},{7,6},{8,9},{9,8},{10,11... | collective-permute-start | bytes 442376 | tf_op jit(solution)/shard_map/ppermute | solution.py:124
  44.8 1.6 %collective-permute-start.12 = (bf16[576,128]{1,0:T(8,128)(2,1)S(1)}, bf16[576,128]{1,0:T(8,128)(2,1)S(1)}, u32[]{:S(2)}, u32[]{:S(2)}) collective-permute-start(bf16[576,128]{1,0:T(8,128)(2,1)S(1)} %collective-permute-done.5.refs_14_.refs_16_), channel_id=1, source_target_pairs={{0,1},{1,0},{2,3},{3,2},{4,5},{5,4},{6,7},{7,6},{8,9},{9,8},{10,11... | collective-permute-start | bytes 442376 | tf_op jit(solution)/shard_map/ppermute | solution.py:124

commit v7 on v6

--- a/solution.py
+++ b/solution.py
@@ -18,15 +18,18 @@
 
 
 def attend_kernel(slots, pair, which, *refs):
+    me = lax.axis_index("ctx")
     order_ref, start_ref, packed_ref = refs[:3]
     if which == 0:
         weight_ref = packed_ref
         refs = refs[3:]
     else:
-        weight_ref, done_ref = refs[3:5]
-        refs = refs[5:]
+        kept_ref, others_ref, done_ref = refs[3:6]
+        *refs, weight_ref = refs[6:]
+        weight_ref[me] = kept_ref[...]
+        for step in range(1, slots):
+            weight_ref[lax.rem(me + step, slots)] = others_ref[step - 1]
     own_ref, *piece_refs, out_ref = refs
-    me = lax.axis_index("ctx")
     core = lax.axis_index("tp")
     rows = own_ref.shape[1]
     half = rows // 2
@@ -112,6 +115,10 @@
     weight = kv_weight.reshape(depth, contexts, 2, pair, width)
     weight = lax.dynamic_index_in_dim(weight, group, 2, keepdims=False)
     weight = weight.transpose(1, 2, 0, 3).reshape(contexts, pair * depth, width)
+    me = lax.axis_index("ctx")
+    kept = kv_weight.reshape(depth, contexts, 2, pair, width)
+    kept = lax.dynamic_slice(kept, (0, me, 1 - group, 0, 0), (depth, 1, 1, pair, width))
+    kept = kept.reshape(depth, pair, width).transpose(1, 0, 2).reshape(pair * depth, width)
     query = queries.reshape(query_rows, contexts, 2, pair, query_width)
     query = jnp.where(group == 0, query, query[:, :, ::-1])
     straight = query[..., :NOPE].transpose(1, 2, 0, 3, 4)
@@ -134,8 +141,12 @@
     for slot, source, bit in LATE:
         held[slot] = swap(held[source], bit)
     traded = {slot: trade(held[slot]) for slot in (1, 2)}
-    packed, held[3], held[5], held[6], traded[1], traded[2] = lax.optimization_barrier((packed, held[3], held[5], held[6], traded[1], traded[2]))
-    other = lax.ppermute(packed[:, :pair * depth], "groups", [(0, 1), (1, 0)])
+    packed, kept, held[3], held[5], held[6], traded[1], traded[2] = lax.optimization_barrier((packed, kept, held[3], held[5], held[6], traded[1], traded[2]))
+    others = packed[:, :pair * depth]
+    others = lax.dynamic_slice_in_dim(
+        jnp.concatenate([others, others]), me + 1, contexts - 1, 0
+    )
+    others = lax.ppermute(others, "groups", [(0, 1), (1, 0)])
     pieces = [turned_cache]
     for slot in range(1, contexts):
         pieces += [held[slot], traded.get(slot, None) if slot in traded else trade(held[slot])]
@@ -150,13 +161,14 @@
             out_shape=jax.ShapeDtypeStruct((query_count, out_heads * VD), jnp.bfloat16),
             in_specs=[scalars, scalars] + [on_chip] * (len(operands) + len(pieces)),
             out_specs=on_chip,
+            scratch_shapes=[pltpu.VMEM((contexts, pair * depth, width), jnp.bfloat16)] * which,
             compiler_params=pltpu.CompilerParams(vmem_limit_bytes=16 * 2**20),
             cost_estimate=pl.CostEstimate(flops=1048576, bytes_accessed=1 << 20, transcendentals=0),
             name="attend_" + ("first", "second")[which],
         )(block_order, span_start, *operands, *pieces)
 
     attended = attend(0, pair, [packed])
-    attended = attend(1, heads, [packed, other, attended])
+    attended = attend(1, heads, [packed, kept, others, attended])
     attended = attended.reshape(contexts, query_rows, heads * VD)
     attended = lax.all_to_all(attended, "ctx", 0, 0, tiled=True)
     attended = attended.reshape(contexts, query_rows, heads, VD).transpose(1, 0, 2, 3)

time: 66 us -> 64.1 us (0.971)
  waiting for transfers between devices: 21.9 us -> 20.7 us
    ppermute x1, waiting for transfers between devices: 0.85 us -> 0.01 us  [split_by_heads(): others = lax.ppermute(others, 'groups', [(0, 1), (1, 0)])]
    dynamic_slice x1, local copies, waits for them, and re-layouts: 1.58 us -> 0.92 us  [split_by_heads(): held = {0: lax.dynamic_slice_in_dim(turned_cache, core * half, half, 1)}]
  transfers between devices with their start and end apart: 16 -> 16, of which waited for: 9 -> 7; matrix products, arithmetic and copies ran while one was open for 6% -> 6% of each run, Pallas kernels for 4% -> 4%
where the time goes in v7:
time: 64.1 us; the launch traced here: 63.8 us
  waiting for transfers between devices  20.7 us (32%)
  starting transfers between devices  19 us (30%)
  blocking collectives  11.6 us (18%)
  Pallas kernels  5.67 us (9%)
  local copies, waits for them, and re-layouts  4.59 us (7%)
  other arithmetic  1.4 us (2%)
  between operations  0.85 us (1%)
    ppermute x7, waiting for transfers between devices, swap(): return lax.ppermute(array, 'ctx', [(i, i ^ bit) for i in range(contexts)])  17.9 us
    ppermute x7, starting transfers between devices, swap(): return lax.ppermute(array, 'ctx', [(i, i ^ bit) for i in range(contexts)])  11.7 us
    all_to_all x1, blocking collectives, split_by_heads(): attended = lax.all_to_all(attended, 'ctx', 0, 0, tiled=True)  11.6 us
    pallas_call x2, Pallas kernels, attend(): pl.pallas_call(functools.partial(attend_kernel, contexts, pair, which), o...  5.67 us
    all_to_all x1, starting transfers between devices, split_by_heads(): packed = lax.all_to_all(packed, 'ctx', 0, 0, tiled=True)  4.24 us
    all_to_all x1, waiting for transfers between devices, split_by_heads(): packed = lax.all_to_all(packed, 'ctx', 0, 0, tiled=True)  2.34 us
    ppermute x1, starting transfers between devices, split_by_heads(): others = lax.ppermute(others, 'groups', [(0, 1), (1, 0)])  1.58 us
    ppermute x7, starting transfers between devices, trade(): return lax.ppermute(array, 'tp', [(0, 1), (1, 0)])  1.53 us
  transfers between devices with their start and end apart: 16, of which 7 were waited for; matrix products, arithmetic and copies ran while one was open for 6% of the time, Pallas kernels for 4%

profile of v7, /device:TPU:0, one launch (start us, length us, event | category | flops | bytes accessed | tf_op | source)
XLA Modules:
  0.0 63.8 jit_solution(2747829767240285403)
XLA Ops:
  0.0 0.9 %dynamic-slice_bitcast_fusion = bf16[576,128]{1,0:T(8,128)(2,1)S(1)} fusion(bf16[256,576]{0,1:T(8,128)(2,1)} %param.6, s32[]{:T(128)S(6)} %select_n.27), kind=kLoop, calls=%fused_computation.5 | loop fusion | bytes 294916 | tf_op jit(solution)/shard_map/dynamic_slice | solution.py:135
  0.9 0.0 copy-start.2
  0.9 4.1 %collective-permute-start = (bf16[576,128]{1,0:T(8,128)(2,1)S(1)}, bf16[576,128]{1,0:T(8,128)(2,1)S(1)}, u32[]{:S(2)}, u32[]{:S(2)}) collective-permute-start(bf16[576,128]{1,0:T(8,128)(2,1)S(1)} %dynamic-slice_bitcast_fusion), channel_id=1, source_target_pairs={{0,8},{2,10},{4,12},{6,14},{8,0},{10,2},{12,4},{14,6},{1,9},{3,11}... | collective-permute-start | bytes 442376 | tf_op jit(solution)/shard_map/ppermute | solution.py:113
  5.0 1.5 %collective-permute-start.1 = (bf16[576,128]{1,0:T(8,128)(2,1)S(1)}, bf16[576,128]{1,0:T(8,128)(2,1)S(1)}, u32[]{:S(2)}, u32[]{:S(2)}) collective-permute-start(bf16[576,128]{1,0:T(8,128)(2,1)S(1)} %dynamic-slice_bitcast_fusion), channel_id=1, source_target_pairs={{0,2},{2,0},{4,6},{6,4},{8,10},{10,8},{12,14},{14,12},{1,3},{3,1},... | collective-permute-start | bytes 442376 | tf_op jit(solution)/shard_map/ppermute | solution.py:113
  6.5 1.6 %collective-permute-start.2 = (bf16[576,128]{1,0:T(8,128)(2,1)S(1)}, bf16[576,128]{1,0:T(8,128)(2,1)S(1)}, u32[]{:S(2)}, u32[]{:S(2)}) collective-permute-start(bf16[576,128]{1,0:T(8,128)(2,1)S(1)} %dynamic-slice_bitcast_fusion), channel_id=1, source_target_pairs={{0,4},{2,6},{4,0},{6,2},{8,12},{10,14},{12,8},{14,10},{1,5},{3,7},... | collective-permute-start | bytes 442376 | tf_op jit(solution)/shard_map/ppermute | solution.py:113
  8.1 1.1 %reshape.33 = bf16[16,8,2,2,192]{4,3,2,1,0:T(2,128)(2,1)S(1)} reshape(bf16[16,32,192]{2,1,0:T(8,128)(2,1)} %param.5) | data formatting | bytes 393216 | tf_op jit(solution)/shard_map/reshape | solution.py:122
  9.2 0.2 copy.8
  9.4 0.3 broadcast_select_fusion
  9.7 0.1 slice_bitcast_fusion
  9.8 0.1 slice_bitcast_fusion.1
  9.9 0.4 reshape.31
  10.3 0.4 constant_dynamic-slice_fusion.1
  10.8 0.1 reshape.35
  10.9 0.1 copy.9
  11.0 0.1 reshape.34
  11.1 0.2 copy.6
  11.3 0.9 %pad_maximum_fusion = bf16[8,176,256]{2,1,0:T(8,128)(2,1)} fusion(bf16[8,16,256]{2,1,0:T(8,128)(2,1)S(1)} %reshape.35, bf16[8,32,256]{2,1,0:T(8,128)(2,1)S(1)} %reshape.34, bf16[8,128,256]{2,1,0:T(8,128)(2,1)S(1)} %bitcast.25), kind=kLoop, calls=%fused_computation.2 | loop fusion | flops 2162688 | bytes 1441792 | tf_op jit(solution)/shard_map/concatenate | solution.py:128
  12.2 0.0 collective-permute-done.refs_10_.refs_13_
  12.2 0.0 collective-permute-done.1.refs_4_.refs_7_
  12.2 1.3 %collective-permute-done.2.refs_6_.refs_9_ = bf16[576,128]{1,0:T(8,128)(2,1)S(1)} collective-permute-done((bf16[576,128]{1,0:T(8,128)(2,1)S(1)}, bf16[576,128]{1,0:T(8,128)(2,1)S(1)}, u32[]{:S(2)}, u32[]{:S(2)}) %collective-permute-start.2) | collective-permute-done | bytes 147488 | tf_op jit(solution)/shard_map/ppermute | solution.py:113
  13.6 4.2 %all-to-all-start = ((bf16[8,176,256]{2,1,0:T(8,128)(2,1)}), bf16[8,176,256]{2,1,0:T(8,128)(2,1)S(1)}, u32[]{:S(2)}, u32[]{:S(2)}) async-start(bf16[8,176,256]{2,1,0:T(8,128)(2,1)} %pad_maximum_fusion), calls=%async_computation | async-start | bytes 1441792 | tf_op jit(solution)/shard_map/all_to_all | solution.py:140
  17.8 2.0 %collective-permute-start.3 = (bf16[576,128]{1,0:T(8,128)(2,1)S(1)}, bf16[576,128]{1,0:T(8,128)(2,1)S(1)}, u32[]{:S(2)}, u32[]{:S(2)}) collective-permute-start(bf16[576,128]{1,0:T(8,128)(2,1)S(1)} %collective-permute-done.2.refs_6_.refs_9_), channel_id=1, source_target_pairs={{0,2},{2,0},{4,6},{6,4},{8,10},{10,8},{12,14},{14,12},{1,3},{3,1},... | collective-permute-start | bytes 442376 | tf_op jit(solution)/shard_map/ppermute | solution.py:113
  19.8 0.0 collective-permute-start.4
  19.9 2.0 %collective-permute-start.5 = (bf16[576,128]{1,0:T(8,128)(2,1)S(1)}, bf16[576,128]{1,0:T(8,128)(2,1)S(1)}, u32[]{:S(2)}, u32[]{:S(2)}) collective-permute-start(bf16[576,128]{1,0:T(8,128)(2,1)S(1)} %collective-permute-done.refs_10_.refs_13_), channel_id=1, source_target_pairs={{0,4},{2,6},{4,0},{6,2},{8,12},{10,14},{12,8},{14,10},{1,5},{3,7},... | collective-permute-start | bytes 442376 | tf_op jit(solution)/shard_map/ppermute | solution.py:113
  21.8 0.0 collective-permute-start.6
  21.8 0.5 collective-permute-start.7
  22.4 0.1 constant_dynamic-slice_fusion
  22.4 0.0 copy-start
  22.5 0.0 copy-start.1
  22.5 9.0 %collective-permute-done.3.refs_8_.refs_11_ = bf16[576,128]{1,0:T(8,128)(2,1)S(1)} collective-permute-done((bf16[576,128]{1,0:T(8,128)(2,1)S(1)}, bf16[576,128]{1,0:T(8,128)(2,1)S(1)}, u32[]{:S(2)}, u32[]{:S(2)}) %collective-permute-start.3) | collective-permute-done | bytes 147488 | tf_op jit(solution)/shard_map/ppermute | solution.py:113
  31.5 2.9 %collective-permute-done.4.refs_12_.refs_15_ = bf16[576,128]{1,0:T(8,128)(2,1)S(1)} collective-permute-done((bf16[576,128]{1,0:T(8,128)(2,1)S(1)}, bf16[576,128]{1,0:T(8,128)(2,1)S(1)}, u32[]{:S(2)}, u32[]{:S(2)}) %collective-permute-start.4) | collective-permute-done | bytes 147488 | tf_op jit(solution)/shard_map/ppermute | solution.py:113
  34.4 0.0 collective-permute-done.5.refs_14_.refs_17_
  34.4 0.0 collective-permute-done.6.refs_5_.refs_8_
  34.4 0.0 collective-permute-done.7.refs_7_.refs_10_
  34.4 2.3 %all-to-all-done.refs_2_ = bf16[8,176,256]{2,1,0:T(8,128)(2,1)S(1)} async-done(((bf16[8,176,256]{2,1,0:T(8,128)(2,1)}), bf16[8,176,256]{2,1,0:T(8,128)(2,1)S(1)}, u32[]{:S(2)}, u32[]{:S(2)}) %all-to-all-start) | async-done | bytes 720928 | tf_op jit(solution)/shard_map/all_to_all | solution.py:140
  36.8 0.2 fusion
  37.0 1.6 %collective-permute-start.8 = (bf16[7,128,256]{2,1,0:T(8,128)(2,1)S(1)}, bf16[7,128,256]{2,1,0:T(8,128)(2,1)S(1)}, u32[]{:S(2)}, u32[]{:S(2)}) collective-permute-start(bf16[7,128,256]{2,1,0:T(8,128)(2,1)S(1)} %fusion), channel_id=1, source_target_pairs={{0,16},{16,0},{1,17},{17,1},{2,18},{18,2},{3,19},{19,3},{4,20},{20... | collective-permute-start | bytes 1376264 | tf_op jit(solution)/shard_map/ppermute | solution.py:149
  38.5 0.4 collective-permute-start.13
  39.0 4.7 %collective-permute-done.13.refs_16_.refs_19_ = bf16[576,128]{1,0:T(8,128)(2,1)S(1)} collective-permute-done((bf16[576,128]{1,0:T(8,128)(2,1)S(1)}, bf16[576,128]{1,0:T(8,128)(2,1)S(1)}, u32[]{:S(2)}, u32[]{:S(2)}) %collective-permute-start.13) | collective-permute-done | bytes 147488 | tf_op jit(solution)/shard_map/ppermute | solution.py:113
  43.7 0.5 collective-permute-start.9
  44.2 0.0 collective-permute-start.11
  44.2 0.5 collective-permute-start.12
  45.4 0.2 collective-permute-done.11.refs_13_.refs_16_
  45.6 0.2 collective-permute-done.12.refs_15_.refs_18_
  45.8 2.8 %attend_first.1.refs_5_ = bf16[128,256]{1,0:T(8,128)(2,1)S(1)} custom-call(s32[8]{0:T(128)S(1)} %copy-done.1, s32[1]{0:T(128)S(6)} %copy.12.refs_1_, bf16[8,176,256]{2,1,0:T(8,128)(2,1)S(1)} %all-to-all-done.refs_2_, bf16[576,256]{1,0:T(8,128)(2,1)S(1)} %bitcast.21, bf16[576,128]{1,0:T(8,128)(2,1)S(1)} %collective-permute-done.1.refs_4_.refs_7_, ...), custom_call_target="tpu_custom_call" | custom-call | flops 1048576 | bytes 1048576 | tf_op jit(solution)/shard_map/attend_first/pallas_call | solution.py:159
  48.6 2.9 %attend_second.1 = bf16[128,512]{1,0:T(8,128)(2,1)S(1)} custom-call(s32[8]{0:T(128)S(1)} %copy-done.1, s32[1]{0:T(128)S(6)} %copy.12.refs_1_, bf16[8,176,256]{2,1,0:T(8,128)(2,1)S(1)} %all-to-all-done.refs_2_, bf16[128,256]{1,0:T(8,128)(2,1)S(1)} %bitcast.24, bf16[7,128,256]{2,1,0:T(8,128)(2,1)S(1)} %collective-permute-done.8.refs_4_, ...), custom_call_target="tpu_custom_call" | custom-call | flops 1048576 | bytes 1048576 | tf_op jit(solution)/shard_map/attend_second/pallas_call | solution.py:159
  51.5 11.6 %all_to_all.10 = bf16[8,16,512]{2,1,0:T(8,128)(2,1)S(1)} all-to-all(bf16[8,16,512]{2,1,0:T(8,128)(2,1)S(1)} %bitcast.23), channel_id=1, replica_groups=mesh['groups'=2,'ctx'=8,'tp'=2] {'ctx'}, dimensions={0} | all-to-all | bytes 262144 | tf_op jit(solution)/shard_map/all_to_all | solution.py:173
  63.1 0.7 %copy.11 = bf16[8,16,4,128]{3,2,0,1:T(4,128)(2,1)} copy(bf16[8,16,4,128]{3,2,1,0:T(4,128)(2,1)S(1)} %reshape.39) | data formatting | bytes 262144 | tf_op jit(solution)/shard_map/reshape | solution.py:174
  (12 shorter events, 0.1 us)
Async XLA Ops:
  0.9 9.0 %copy-start.2 = (bf16[64,32,256]{2,1,0:T(8,128)(2,1)S(1)}, bf16[64,32,256]{2,1,0:T(8,128)(2,1)}, u32[]{:S(2)}) copy-start(bf16[64,32,256]{2,1,0:T(8,128)(2,1)} %param.7) | copy-start | bytes 3145732
  0.9 11.3 %collective-permute-start = (bf16[576,128]{1,0:T(8,128)(2,1)S(1)}, bf16[576,128]{1,0:T(8,128)(2,1)S(1)}, u32[]{:S(2)}, u32[]{:S(2)}) collective-permute-start(bf16[576,128]{1,0:T(8,128)(2,1)S(1)} %dynamic-slice_bitcast_fusion), channel_id=1, source_target_pairs={{0,8},{2,10},{4,12},{6,14},{8,0},{10,2},{12,4},{14,6},{1,9},{3,11}... | collective-permute-start | bytes 442376 | tf_op jit(solution)/shard_map/ppermute | solution.py:113
  5.0 7.2 %collective-permute-start.1 = (bf16[576,128]{1,0:T(8,128)(2,1)S(1)}, bf16[576,128]{1,0:T(8,128)(2,1)S(1)}, u32[]{:S(2)}, u32[]{:S(2)}) collective-permute-start(bf16[576,128]{1,0:T(8,128)(2,1)S(1)} %dynamic-slice_bitcast_fusion), channel_id=1, source_target_pairs={{0,2},{2,0},{4,6},{6,4},{8,10},{10,8},{12,14},{14,12},{1,3},{3,1},... | collective-permute-start | bytes 442376 | tf_op jit(solution)/shard_map/ppermute | solution.py:113
  6.5 7.0 %collective-permute-start.2 = (bf16[576,128]{1,0:T(8,128)(2,1)S(1)}, bf16[576,128]{1,0:T(8,128)(2,1)S(1)}, u32[]{:S(2)}, u32[]{:S(2)}) collective-permute-start(bf16[576,128]{1,0:T(8,128)(2,1)S(1)} %dynamic-slice_bitcast_fusion), channel_id=1, source_target_pairs={{0,4},{2,6},{4,0},{6,2},{8,12},{10,14},{12,8},{14,10},{1,5},{3,7},... | collective-permute-start | bytes 442376 | tf_op jit(solution)/shard_map/ppermute | solution.py:113
  13.6 23.2 %all-to-all-start = ((bf16[8,176,256]{2,1,0:T(8,128)(2,1)}), bf16[8,176,256]{2,1,0:T(8,128)(2,1)S(1)}, u32[]{:S(2)}, u32[]{:S(2)}) async-start(bf16[8,176,256]{2,1,0:T(8,128)(2,1)} %pad_maximum_fusion), calls=%async_computation | async-start | bytes 1441792 | tf_op jit(solution)/shard_map/all_to_all | solution.py:140
  17.8 13.7 %collective-permute-start.3 = (bf16[576,128]{1,0:T(8,128)(2,1)S(1)}, bf16[576,128]{1,0:T(8,128)(2,1)S(1)}, u32[]{:S(2)}, u32[]{:S(2)}) collective-permute-start(bf16[576,128]{1,0:T(8,128)(2,1)S(1)} %collective-permute-done.2.refs_6_.refs_9_), channel_id=1, source_target_pairs={{0,2},{2,0},{4,6},{6,4},{8,10},{10,8},{12,14},{14,12},{1,3},{3,1},... | collective-permute-start | bytes 442376 | tf_op jit(solution)/shard_map/ppermute | solution.py:113
  19.8 14.6 %collective-permute-start.4 = (bf16[576,128]{1,0:T(8,128)(2,1)S(1)}, bf16[576,128]{1,0:T(8,128)(2,1)S(1)}, u32[]{:S(2)}, u32[]{:S(2)}) collective-permute-start(bf16[576,128]{1,0:T(8,128)(2,1)S(1)} %collective-permute-done.refs_10_.refs_13_), channel_id=1, source_target_pairs={{0,2},{2,0},{4,6},{6,4},{8,10},{10,8},{12,14},{14,12},{1,3},{3,1},... | collective-permute-start | bytes 442376 | tf_op jit(solution)/shard_map/ppermute | solution.py:113
  19.9 14.5 %collective-permute-start.5 = (bf16[576,128]{1,0:T(8,128)(2,1)S(1)}, bf16[576,128]{1,0:T(8,128)(2,1)S(1)}, u32[]{:S(2)}, u32[]{:S(2)}) collective-permute-start(bf16[576,128]{1,0:T(8,128)(2,1)S(1)} %collective-permute-done.refs_10_.refs_13_), channel_id=1, source_target_pairs={{0,4},{2,6},{4,0},{6,2},{8,12},{10,14},{12,8},{14,10},{1,5},{3,7},... | collective-permute-start | bytes 442376 | tf_op jit(solution)/shard_map/ppermute | solution.py:113
  21.8 12.5 %collective-permute-start.6 = (bf16[576,128]{1,0:T(8,128)(2,1)S(1)}, bf16[576,128]{1,0:T(8,128)(2,1)S(1)}, u32[]{:S(2)}, u32[]{:S(2)}) collective-permute-start(bf16[576,128]{1,0:T(8,128)(2,1)S(1)} %collective-permute-done.1.refs_4_.refs_7_), channel_id=1, source_target_pairs={{0,1},{1,0},{2,3},{3,2},{4,5},{5,4},{6,7},{7,6},{8,9},{9,8},{10,11... | collective-permute-start | bytes 442376 | tf_op jit(solution)/shard_map/ppermute | solution.py:131
  21.8 12.5 %collective-permute-start.7 = (bf16[576,128]{1,0:T(8,128)(2,1)S(1)}, bf16[576,128]{1,0:T(8,128)(2,1)S(1)}, u32[]{:S(2)}, u32[]{:S(2)}) collective-permute-start(bf16[576,128]{1,0:T(8,128)(2,1)S(1)} %collective-permute-done.2.refs_6_.refs_9_), channel_id=1, source_target_pairs={{0,1},{1,0},{2,3},{3,2},{4,5},{5,4},{6,7},{7,6},{8,9},{9,8},{10,11... | collective-permute-start | bytes 442376 | tf_op jit(solution)/shard_map/ppermute | solution.py:131
  22.4 23.3 %copy-start = (bf16[256,576]{0,1:T(8,128)(2,1)S(1)}, bf16[256,576]{0,1:T(8,128)(2,1)}, u32[]{:S(2)}) copy-start(bf16[256,576]{0,1:T(8,128)(2,1)} %param.6) | copy-start | bytes 884740
  22.5 23.3 %copy-start.1 = (s32[8]{0:T(128)S(1)}, s32[8]{0:T(128)}, u32[]{:S(2)}) copy-start(s32[8]{0:T(128)} %refs_0_.3) | copy-start | bytes 100
  37.0 11.6 %collective-permute-start.8 = (bf16[7,128,256]{2,1,0:T(8,128)(2,1)S(1)}, bf16[7,128,256]{2,1,0:T(8,128)(2,1)S(1)}, u32[]{:S(2)}, u32[]{:S(2)}) collective-permute-start(bf16[7,128,256]{2,1,0:T(8,128)(2,1)S(1)} %fusion), channel_id=1, source_target_pairs={{0,16},{16,0},{1,17},{17,1},{2,18},{18,2},{3,19},{19,3},{4,20},{20... | collective-permute-start | bytes 1376264 | tf_op jit(solution)/shard_map/ppermute | solution.py:149
  38.5 5.1 %collective-permute-start.13 = (bf16[576,128]{1,0:T(8,128)(2,1)S(1)}, bf16[576,128]{1,0:T(8,128)(2,1)S(1)}, u32[]{:S(2)}, u32[]{:S(2)}) collective-permute-start(bf16[576,128]{1,0:T(8,128)(2,1)S(1)} %collective-permute-done.4.refs_12_.refs_15_), channel_id=1, source_target_pairs={{0,4},{2,6},{4,0},{6,2},{8,12},{10,14},{12,8},{14,10},{1,5},{3,7},... | collective-permute-start | bytes 442376 | tf_op jit(solution)/shard_map/ppermute | solution.py:113
  39.0 5.2 %collective-permute-start.10 = (bf16[576,128]{1,0:T(8,128)(2,1)S(1)}, bf16[576,128]{1,0:T(8,128)(2,1)S(1)}, u32[]{:S(2)}, u32[]{:S(2)}) collective-permute-start(bf16[576,128]{1,0:T(8,128)(2,1)S(1)} %collective-permute-done.refs_10_.refs_13_), channel_id=1, source_target_pairs={{0,1},{1,0},{2,3},{3,2},{4,5},{5,4},{6,7},{7,6},{8,9},{9,8},{10,11... | collective-permute-start | bytes 442376 | tf_op jit(solution)/shard_map/ppermute | solution.py:131
  43.7 1.7 %collective-permute-start.14 = (bf16[576,128]{1,0:T(8,128)(2,1)S(1)}, bf16[576,128]{1,0:T(8,128)(2,1)S(1)}, u32[]{:S(2)}, u32[]{:S(2)}) collective-permute-start(bf16[576,128]{1,0:T(8,128)(2,1)S(1)} %collective-permute-done.13.refs_16_.refs_19_), channel_id=1, source_target_pairs={{0,1},{1,0},{2,3},{3,2},{4,5},{5,4},{6,7},{7,6},{8,9},{9,8},{10,11... | collective-permute-start | bytes 442376 | tf_op jit(solution)/shard_map/ppermute | solution.py:131
  43.7 1.7 %collective-permute-start.9 = (bf16[576,128]{1,0:T(8,128)(2,1)S(1)}, bf16[576,128]{1,0:T(8,128)(2,1)S(1)}, u32[]{:S(2)}, u32[]{:S(2)}) collective-permute-start(bf16[576,128]{1,0:T(8,128)(2,1)S(1)} %collective-permute-done.3.refs_8_.refs_11_), channel_id=1, source_target_pairs={{0,1},{1,0},{2,3},{3,2},{4,5},{5,4},{6,7},{7,6},{8,9},{9,8},{10,11... | collective-permute-start | bytes 442376 | tf_op jit(solution)/shard_map/ppermute | solution.py:131
  44.2 1.4 %collective-permute-start.11 = (bf16[576,128]{1,0:T(8,128)(2,1)S(1)}, bf16[576,128]{1,0:T(8,128)(2,1)S(1)}, u32[]{:S(2)}, u32[]{:S(2)}) collective-permute-start(bf16[576,128]{1,0:T(8,128)(2,1)S(1)} %collective-permute-done.4.refs_12_.refs_15_), channel_id=1, source_target_pairs={{0,1},{1,0},{2,3},{3,2},{4,5},{5,4},{6,7},{7,6},{8,9},{9,8},{10,11... | collective-permute-start | bytes 442376 | tf_op jit(solution)/shard_map/ppermute | solution.py:131
  44.2 1.6 %collective-permute-start.12 = (bf16[576,128]{1,0:T(8,128)(2,1)S(1)}, bf16[576,128]{1,0:T(8,128)(2,1)S(1)}, u32[]{:S(2)}, u32[]{:S(2)}) collective-permute-start(bf16[576,128]{1,0:T(8,128)(2,1)S(1)} %collective-permute-done.5.refs_14_.refs_17_), channel_id=1, source_target_pairs={{0,1},{1,0},{2,3},{3,2},{4,5},{5,4},{6,7},{7,6},{8,9},{9,8},{10,11... | collective-permute-start | bytes 442376 | tf_op jit(solution)/shard_map/ppermute | solution.py:131

commit v8 on v6

--- a/solution.py
+++ b/solution.py
@@ -18,15 +18,19 @@
 
 
 def attend_kernel(slots, pair, which, *refs):
+    me = lax.axis_index("ctx")
     order_ref, start_ref, packed_ref = refs[:3]
     if which == 0:
         weight_ref = packed_ref
         refs = refs[3:]
     else:
-        weight_ref, done_ref = refs[3:5]
-        refs = refs[5:]
+        near = slots // 2
+        near_refs, (others_ref, done_ref) = refs[3:3 + near], refs[3 + near:5 + near]
+        *refs, weight_ref = refs[5 + near:]
+        for slot, near_ref in enumerate(near_refs):
+            weight_ref[me ^ slot] = near_ref[...]
+        weight_ref[pl.ds((me // near ^ 1) * near, near)] = others_ref[...]
     own_ref, *piece_refs, out_ref = refs
-    me = lax.axis_index("ctx")
     core = lax.axis_index("tp")
     rows = own_ref.shape[1]
     half = rows // 2
@@ -112,6 +116,19 @@
     weight = kv_weight.reshape(depth, contexts, 2, pair, width)
     weight = lax.dynamic_index_in_dim(weight, group, 2, keepdims=False)
     weight = weight.transpose(1, 2, 0, 3).reshape(contexts, pair * depth, width)
+    me = lax.axis_index("ctx")
+    by_head = kv_weight.reshape(depth, contexts, 2, pair, width)
+
+    def second_pair(owner):
+        part = lax.dynamic_slice(
+            by_head, (0, owner, 1 - group, 0, 0), (depth, 1, 1, pair, width)
+        )
+        part = part.reshape(depth, pair, width).transpose(1, 0, 2)
+        return part.reshape(pair * depth, width)
+
+    kept = second_pair(me)
+    near = contexts // 2
+    beside = {slot: swap(second_pair(me ^ slot), slot) for slot in range(1, near)}
     query = queries.reshape(query_rows, contexts, 2, pair, query_width)
     query = jnp.where(group == 0, query, query[:, :, ::-1])
     straight = query[..., :NOPE].transpose(1, 2, 0, 3, 4)
@@ -128,14 +145,15 @@
     held = {0: lax.dynamic_slice_in_dim(turned_cache, core * half, half, 1)}
     for slot, source, bit in EARLY:
         held[slot] = swap(held[source], bit)
-    waited = lax.optimization_barrier((packed, held[4], held[1], held[2]))
-    packed, held[4], held[1], held[2] = waited
+    waited = lax.optimization_barrier((packed, held[4], held[1], held[2], beside[1], beside[2]))
+    packed, held[4], held[1], held[2], beside[1], beside[2] = waited
     packed = lax.all_to_all(packed, "ctx", 0, 0, tiled=True)
     for slot, source, bit in LATE:
         held[slot] = swap(held[source], bit)
     traded = {slot: trade(held[slot]) for slot in (1, 2)}
-    packed, held[3], held[5], held[6], traded[1], traded[2] = lax.optimization_barrier((packed, held[3], held[5], held[6], traded[1], traded[2]))
-    other = lax.ppermute(packed[:, :pair * depth], "groups", [(0, 1), (1, 0)])
+    packed, kept, held[3], held[5], held[6], traded[1], traded[2] = lax.optimization_barrier((packed, kept, held[3], held[5], held[6], traded[1], traded[2]))
+    others = lax.dynamic_slice_in_dim(packed, (me // near ^ 1) * near, near, 0)[:, :pair * depth]
+    others = lax.ppermute(others, "groups", [(0, 1), (1, 0)])
     pieces = [turned_cache]
     for slot in range(1, contexts):
         pieces += [held[slot], traded.get(slot, None) if slot in traded else trade(held[slot])]
@@ -150,13 +168,14 @@
             out_shape=jax.ShapeDtypeStruct((query_count, out_heads * VD), jnp.bfloat16),
             in_specs=[scalars, scalars] + [on_chip] * (len(operands) + len(pieces)),
             out_specs=on_chip,
+            scratch_shapes=[pltpu.VMEM((contexts, pair * depth, width), jnp.bfloat16)] * which,
             compiler_params=pltpu.CompilerParams(vmem_limit_bytes=16 * 2**20),
             cost_estimate=pl.CostEstimate(flops=1048576, bytes_accessed=1 << 20, transcendentals=0),
             name="attend_" + ("first", "second")[which],
         )(block_order, span_start, *operands, *pieces)
 
     attended = attend(0, pair, [packed])
-    attended = attend(1, heads, [packed, other, attended])
+    attended = attend(1, heads, [packed, kept, *beside.values(), others, attended])
     attended = attended.reshape(contexts, query_rows, heads * VD)
     attended = lax.all_to_all(attended, "ctx", 0, 0, tiled=True)
     attended = attended.reshape(contexts, query_rows, heads, VD).transpose(1, 0, 2, 3)

time: 66 us -> 62.1 us (0.941)
  waiting for transfers between devices: 21.9 us -> 15.6 us
  starting transfers between devices: 19 us -> 21.9 us
    ppermute x7 -> x10, waiting for transfers between devices: 18.3 us -> 13.8 us  [swap(): return lax.ppermute(array, 'ctx', [(i, i ^ bit) for i in range(contexts)])]
    ppermute x7 -> x10, starting transfers between devices: 11.6 us -> 14.9 us  [swap(): return lax.ppermute(array, 'ctx', [(i, i ^ bit) for i in range(contexts)])]
    reshape x1, local copies, waits for them, and re-layouts: 0.44 us -> 1.51 us  [split_by_heads(): weight = kv_weight.reshape(depth, contexts, 2, pair, width)]
    reshape x2, local copies, waits for them, and re-layouts: 1.27 us -> 0.32 us  [split_by_heads(): query = queries.reshape(query_rows, contexts, 2, pair, query_width)]
    all_to_all x1, waiting for transfers between devices: 2.34 us -> 1.48 us  [split_by_heads(): packed = lax.all_to_all(packed, 'ctx', 0, 0, tiled=True)]
    ppermute x1, waiting for transfers between devices: 0.85 us -> 0.01 us  [split_by_heads(): others = lax.ppermute(others, 'groups', [(0, 1), (1, 0)])]
    dynamic_slice x1, local copies, waits for them, and re-layouts: 1.58 us -> 0.92 us  [split_by_heads(): held = {0: lax.dynamic_slice_in_dim(turned_cache, core * half, half, 1)}]
  transfers between devices with their start and end apart: 16 -> 19, of which waited for: 9 -> 8; matrix products, arithmetic and copies ran while one was open for 6% -> 7% of each run, Pallas kernels for 4% -> 5%
where the time goes in v8:
time: 62.1 us; the launch traced here: 61.8 us
  starting transfers between devices  21.9 us (35%)
  waiting for transfers between devices  15.6 us (25%)
  blocking collectives  11.6 us (19%)
  Pallas kernels  5.69 us (9%)
  local copies, waits for them, and re-layouts  4.92 us (8%)
  other arithmetic  1.19 us (2%)
  between operations  0.86 us (1%)
    ppermute x10, starting transfers between devices, swap(): return lax.ppermute(array, 'ctx', [(i, i ^ bit) for i in range(contexts)])  14.9 us
    ppermute x10, waiting for transfers between devices, swap(): return lax.ppermute(array, 'ctx', [(i, i ^ bit) for i in range(contexts)])  13.8 us
    all_to_all x1, blocking collectives, split_by_heads(): attended = lax.all_to_all(attended, 'ctx', 0, 0, tiled=True)  11.6 us
    pallas_call x2, Pallas kernels, attend(): pl.pallas_call(functools.partial(attend_kernel, contexts, pair, which), o...  5.69 us
    all_to_all x1, starting transfers between devices, split_by_heads(): packed = lax.all_to_all(packed, 'ctx', 0, 0, tiled=True)  3.82 us
    ppermute x1, starting transfers between devices, split_by_heads(): others = lax.ppermute(others, 'groups', [(0, 1), (1, 0)])  1.58 us
    ppermute x7, starting transfers between devices, trade(): return lax.ppermute(array, 'tp', [(0, 1), (1, 0)])  1.53 us
    reshape x1, local copies, waits for them, and re-layouts, split_by_heads(): weight = kv_weight.reshape(depth, contexts, 2, pair, width)  1.51 us
  transfers between devices with their start and end apart: 19, of which 8 were waited for; matrix products, arithmetic and copies ran while one was open for 7% of the time, Pallas kernels for 5%

profile of v8, /device:TPU:0, one launch (start us, length us, event | category | flops | bytes accessed | tf_op | source)
XLA Modules:
  0.0 61.8 jit_solution(8970115862140711297)
XLA Ops:
  0.0 0.9 %dynamic-slice_bitcast_fusion = bf16[576,128]{1,0:T(8,128)(2,1)S(1)} fusion(bf16[256,576]{0,1:T(8,128)(2,1)} %param.6, s32[]{:T(128)S(6)} %select_n.44), kind=kLoop, calls=%fused_computation.2 | loop fusion | bytes 294916 | tf_op jit(solution)/shard_map/dynamic_slice | solution.py:145
  0.9 4.1 %collective-permute-start = (bf16[576,128]{1,0:T(8,128)(2,1)S(1)}, bf16[576,128]{1,0:T(8,128)(2,1)S(1)}, u32[]{:S(2)}, u32[]{:S(2)}) collective-permute-start(bf16[576,128]{1,0:T(8,128)(2,1)S(1)} %dynamic-slice_bitcast_fusion), channel_id=1, source_target_pairs={{0,8},{2,10},{4,12},{6,14},{8,0},{10,2},{12,4},{14,6},{1,9},{3,11}... | collective-permute-start | bytes 442376 | tf_op jit(solution)/shard_map/ppermute | solution.py:114
  5.0 1.5 %collective-permute-start.1 = (bf16[576,128]{1,0:T(8,128)(2,1)S(1)}, bf16[576,128]{1,0:T(8,128)(2,1)S(1)}, u32[]{:S(2)}, u32[]{:S(2)}) collective-permute-start(bf16[576,128]{1,0:T(8,128)(2,1)S(1)} %dynamic-slice_bitcast_fusion), channel_id=1, source_target_pairs={{0,2},{2,0},{4,6},{6,4},{8,10},{10,8},{12,14},{14,12},{1,3},{3,1},... | collective-permute-start | bytes 442376 | tf_op jit(solution)/shard_map/ppermute | solution.py:114
  6.5 1.6 %collective-permute-start.2 = (bf16[576,128]{1,0:T(8,128)(2,1)S(1)}, bf16[576,128]{1,0:T(8,128)(2,1)S(1)}, u32[]{:S(2)}, u32[]{:S(2)}) collective-permute-start(bf16[576,128]{1,0:T(8,128)(2,1)S(1)} %dynamic-slice_bitcast_fusion), channel_id=1, source_target_pairs={{0,4},{2,6},{4,0},{6,2},{8,12},{10,14},{12,8},{14,10},{1,5},{3,7},... | collective-permute-start | bytes 442376 | tf_op jit(solution)/shard_map/ppermute | solution.py:114
  8.1 1.5 %reshape.49 = bf16[64,8,2,2,256]{4,3,2,1,0:T(2,128)(2,1)S(1)} reshape(bf16[64,32,256]{2,1,0:T(8,128)(2,1)} %param.7) | data formatting | bytes 2097152 | tf_op jit(solution)/shard_map/reshape | solution.py:116
  9.6 0.3 constant_dynamic-slice_fusion.1
  9.9 0.6 collective-permute-start.3
  10.5 0.5 collective-permute-start.4
  11.1 0.1 reshape.51
  11.2 0.2 copy.8
  11.4 0.3 broadcast_select_fusion
  11.7 0.1 slice_bitcast_fusion
  11.8 0.1 slice_bitcast_fusion.1
  11.9 0.4 constant_dynamic-slice_fusion.5
  12.3 0.1 reshape.53
  12.5 0.1 copy.9
  12.6 0.1 reshape.52
  12.7 0.2 copy.6
  12.8 0.9 %pad_maximum_fusion = bf16[8,176,256]{2,1,0:T(8,128)(2,1)} fusion(bf16[8,16,256]{2,1,0:T(8,128)(2,1)S(1)} %reshape.53, bf16[8,32,256]{2,1,0:T(8,128)(2,1)S(1)} %reshape.52, bf16[8,128,256]{2,1,0:T(8,128)(2,1)S(1)} %bitcast.40), kind=kLoop, calls=%fused_computation | loop fusion | flops 2162688 | bytes 1441792 | tf_op jit(solution)/shard_map/concatenate | solution.py:138
  13.7 0.5 collective-permute-done.3.refs_4_
  14.3 0.7 %collective-permute-done.4.refs_5_ = bf16[128,256]{1,0:T(8,128)(2,1)S(1)} collective-permute-done((bf16[128,256]{1,0:T(8,128)(2,1)S(1)}, bf16[128,256]{1,0:T(8,128)(2,1)S(1)}, u32[]{:S(2)}, u32[]{:S(2)}) %collective-permute-start.4) | collective-permute-done | bytes 65568 | tf_op jit(solution)/shard_map/ppermute | solution.py:114
  14.9 0.0 collective-permute-done.refs_10_.refs_16_
  14.9 0.0 collective-permute-done.1.refs_4_.refs_10_
  15.0 0.0 collective-permute-done.2.refs_6_.refs_12_
  15.0 3.8 %all-to-all-start = ((bf16[8,176,256]{2,1,0:T(8,128)(2,1)}), bf16[8,176,256]{2,1,0:T(8,128)(2,1)S(1)}, u32[]{:S(2)}, u32[]{:S(2)}) async-start(bf16[8,176,256]{2,1,0:T(8,128)(2,1)} %pad_maximum_fusion), calls=%async_computation | async-start | bytes 1441792 | tf_op jit(solution)/shard_map/all_to_all | solution.py:150
  18.8 2.0 %collective-permute-start.5 = (bf16[576,128]{1,0:T(8,128)(2,1)S(1)}, bf16[576,128]{1,0:T(8,128)(2,1)S(1)}, u32[]{:S(2)}, u32[]{:S(2)}) collective-permute-start(bf16[576,128]{1,0:T(8,128)(2,1)S(1)} %collective-permute-done.2.refs_6_.refs_12_), channel_id=1, source_target_pairs={{0,2},{2,0},{4,6},{6,4},{8,10},{10,8},{12,14},{14,12},{1,3},{3,1},... | collective-permute-start | bytes 442376 | tf_op jit(solution)/shard_map/ppermute | solution.py:114
  20.8 0.0 collective-permute-start.6
  20.8 2.0 %collective-permute-start.7 = (bf16[576,128]{1,0:T(8,128)(2,1)S(1)}, bf16[576,128]{1,0:T(8,128)(2,1)S(1)}, u32[]{:S(2)}, u32[]{:S(2)}) collective-permute-start(bf16[576,128]{1,0:T(8,128)(2,1)S(1)} %collective-permute-done.refs_10_.refs_16_), channel_id=1, source_target_pairs={{0,4},{2,6},{4,0},{6,2},{8,12},{10,14},{12,8},{14,10},{1,5},{3,7},... | collective-permute-start | bytes 442376 | tf_op jit(solution)/shard_map/ppermute | solution.py:114
  22.8 0.0 collective-permute-start.8
  22.8 0.5 collective-permute-start.9
  23.4 8.9 %collective-permute-done.5.refs_8_.refs_14_ = bf16[576,128]{1,0:T(8,128)(2,1)S(1)} collective-permute-done((bf16[576,128]{1,0:T(8,128)(2,1)S(1)}, bf16[576,128]{1,0:T(8,128)(2,1)S(1)}, u32[]{:S(2)}, u32[]{:S(2)}) %collective-permute-start.5) | collective-permute-done | bytes 147488 | tf_op jit(solution)/shard_map/ppermute | solution.py:114
  32.3 0.0 collective-permute-start.13
  32.3 2.3 %collective-permute-done.6.refs_12_.refs_18_ = bf16[576,128]{1,0:T(8,128)(2,1)S(1)} collective-permute-done((bf16[576,128]{1,0:T(8,128)(2,1)S(1)}, bf16[576,128]{1,0:T(8,128)(2,1)S(1)}, u32[]{:S(2)}, u32[]{:S(2)}) %collective-permute-start.6) | collective-permute-done | bytes 147488 | tf_op jit(solution)/shard_map/ppermute | solution.py:114
  34.6 1.2 %collective-permute-start.16 = (bf16[576,128]{1,0:T(8,128)(2,1)S(1)}, bf16[576,128]{1,0:T(8,128)(2,1)S(1)}, u32[]{:S(2)}, u32[]{:S(2)}) collective-permute-start(bf16[576,128]{1,0:T(8,128)(2,1)S(1)} %collective-permute-done.6.refs_12_.refs_18_), channel_id=1, source_target_pairs={{0,4},{2,6},{4,0},{6,2},{8,12},{10,14},{12,8},{14,10},{1,5},{3,7},... | collective-permute-start | bytes 442376 | tf_op jit(solution)/shard_map/ppermute | solution.py:114
  35.7 0.0 collective-permute-done.9.refs_7_.refs_13_
  35.7 1.5 %all-to-all-done.refs_2_ = bf16[8,176,256]{2,1,0:T(8,128)(2,1)S(1)} async-done(((bf16[8,176,256]{2,1,0:T(8,128)(2,1)}), bf16[8,176,256]{2,1,0:T(8,128)(2,1)S(1)}, u32[]{:S(2)}, u32[]{:S(2)}) %all-to-all-start) | async-done | bytes 720928 | tf_op jit(solution)/shard_map/all_to_all | solution.py:150
  37.2 1.6 %collective-permute-start.11 = (bf16[4,128,256]{2,1,0:T(8,128)(2,1)S(1)}, bf16[4,128,256]{2,1,0:T(8,128)(2,1)S(1)}, u32[]{:S(2)}, u32[]{:S(2)}) collective-permute-start(bf16[4,128,256]{2,1,0:T(8,128)(2,1)S(1)} %constant_dynamic-slice_fusion), channel_id=1, source_target_pairs={{0,16},{16,0},{1,17},{17,1},{2,18},{18,2},{3,19},{19,3},{4,20},{20... | collective-permute-start | bytes 786440 | tf_op jit(solution)/shard_map/ppermute | solution.py:156
  38.8 1.2 %collective-permute-done.16.refs_16_.refs_22_ = bf16[576,128]{1,0:T(8,128)(2,1)S(1)} collective-permute-done((bf16[576,128]{1,0:T(8,128)(2,1)S(1)}, bf16[576,128]{1,0:T(8,128)(2,1)S(1)}, u32[]{:S(2)}, u32[]{:S(2)}) %collective-permute-start.16) | collective-permute-done | bytes 147488 | tf_op jit(solution)/shard_map/ppermute | solution.py:114
  40.0 0.5 collective-permute-start.12
  40.5 0.0 collective-permute-start.14
  40.5 0.5 collective-permute-start.15
  41.0 0.3 collective-permute-done.17.refs_17_.refs_23_
  41.4 1.4 %collective-permute-start.10 = (bf16[128,256]{1,0:T(8,128)(2,1)S(1)}, bf16[128,256]{1,0:T(8,128)(2,1)S(1)}, u32[]{:S(2)}, u32[]{:S(2)}) collective-permute-start(bf16[128,256]{1,0:T(8,128)(2,1)S(1)} %bitcast.43), channel_id=1, source_target_pairs={{0,6},{2,4},{4,2},{6,0},{8,14},{10,12},{12,10},{14,8},{1,7},{3,5},... | collective-permute-start | bytes 196616 | tf_op jit(solution)/shard_map/ppermute | solution.py:114
  43.5 2.8 %attend_first.1.refs_8_ = bf16[128,256]{1,0:T(8,128)(2,1)S(1)} custom-call(s32[8]{0:T(128)S(1)} %copy-done.1, s32[1]{0:T(128)S(6)} %copy.15.refs_1_, bf16[8,176,256]{2,1,0:T(8,128)(2,1)S(1)} %all-to-all-done.refs_2_, bf16[576,256]{1,0:T(8,128)(2,1)S(1)} %bitcast.36, bf16[576,128]{1,0:T(8,128)(2,1)S(1)} %collective-permute-done.1.refs_4_.refs_10_, ...), custom_call_target="tpu_custom_call" | custom-call | flops 1048576 | bytes 1048576 | tf_op jit(solution)/shard_map/attend_first/pallas_call | solution.py:166
  46.3 0.2 collective-permute-done.10.refs_6_
  46.5 2.9 %attend_second.1 = bf16[128,512]{1,0:T(8,128)(2,1)S(1)} custom-call(s32[8]{0:T(128)S(1)} %copy-done.1, s32[1]{0:T(128)S(6)} %copy.15.refs_1_, bf16[8,176,256]{2,1,0:T(8,128)(2,1)S(1)} %all-to-all-done.refs_2_, bf16[128,256]{1,0:T(8,128)(2,1)S(1)} %bitcast.39, bf16[128,256]{1,0:T(8,128)(2,1)S(1)} %collective-permute-done.3.refs_4_, ...), custom_call_target="tpu_custom_call" | custom-call | flops 1048576 | bytes 1048576 | tf_op jit(solution)/shard_map/attend_second/pallas_call | solution.py:166
  49.4 11.6 %all_to_all.10 = bf16[8,16,512]{2,1,0:T(8,128)(2,1)S(1)} all-to-all(bf16[8,16,512]{2,1,0:T(8,128)(2,1)S(1)} %bitcast.38), channel_id=1, replica_groups=mesh['groups'=2,'ctx'=8,'tp'=2] {'ctx'}, dimensions={0} | all-to-all | bytes 262144 | tf_op jit(solution)/shard_map/all_to_all | solution.py:180
  61.1 0.7 %copy.14 = bf16[8,16,4,128]{3,2,0,1:T(4,128)(2,1)} copy(bf16[8,16,4,128]{3,2,1,0:T(4,128)(2,1)S(1)} %reshape.63) | data formatting | bytes 262144 | tf_op jit(solution)/shard_map/reshape | solution.py:181
  (20 shorter events, 0.1 us)
Async XLA Ops:
  0.9 14.0 %collective-permute-start = (bf16[576,128]{1,0:T(8,128)(2,1)S(1)}, bf16[576,128]{1,0:T(8,128)(2,1)S(1)}, u32[]{:S(2)}, u32[]{:S(2)}) collective-permute-start(bf16[576,128]{1,0:T(8,128)(2,1)S(1)} %dynamic-slice_bitcast_fusion), channel_id=1, source_target_pairs={{0,8},{2,10},{4,12},{6,14},{8,0},{10,2},{12,4},{14,6},{1,9},{3,11}... | collective-permute-start | bytes 442376 | tf_op jit(solution)/shard_map/ppermute | solution.py:114
  5.0 9.9 %collective-permute-start.1 = (bf16[576,128]{1,0:T(8,128)(2,1)S(1)}, bf16[576,128]{1,0:T(8,128)(2,1)S(1)}, u32[]{:S(2)}, u32[]{:S(2)}) collective-permute-start(bf16[576,128]{1,0:T(8,128)(2,1)S(1)} %dynamic-slice_bitcast_fusion), channel_id=1, source_target_pairs={{0,2},{2,0},{4,6},{6,4},{8,10},{10,8},{12,14},{14,12},{1,3},{3,1},... | collective-permute-start | bytes 442376 | tf_op jit(solution)/shard_map/ppermute | solution.py:114
  6.5 8.4 %collective-permute-start.2 = (bf16[576,128]{1,0:T(8,128)(2,1)S(1)}, bf16[576,128]{1,0:T(8,128)(2,1)S(1)}, u32[]{:S(2)}, u32[]{:S(2)}) collective-permute-start(bf16[576,128]{1,0:T(8,128)(2,1)S(1)} %dynamic-slice_bitcast_fusion), channel_id=1, source_target_pairs={{0,4},{2,6},{4,0},{6,2},{8,12},{10,14},{12,8},{14,10},{1,5},{3,7},... | collective-permute-start | bytes 442376 | tf_op jit(solution)/shard_map/ppermute | solution.py:114
  8.1 3.0 %copy-start.2 = (bf16[16,32,192]{2,1,0:T(8,128)(2,1)S(1)}, bf16[16,32,192]{2,1,0:T(8,128)(2,1)}, u32[]{:S(2)}) copy-start(bf16[16,32,192]{2,1,0:T(8,128)(2,1)} %param.5) | copy-start | bytes 589828
  9.9 4.3 %collective-permute-start.3 = (bf16[128,256]{1,0:T(8,128)(2,1)S(1)}, bf16[128,256]{1,0:T(8,128)(2,1)S(1)}, u32[]{:S(2)}, u32[]{:S(2)}) collective-permute-start(bf16[128,256]{1,0:T(8,128)(2,1)S(1)} %bitcast.41), channel_id=1, source_target_pairs={{0,2},{2,0},{4,6},{6,4},{8,10},{10,8},{12,14},{14,12},{1,3},{3,1},... | collective-permute-start | bytes 196616 | tf_op jit(solution)/shard_map/ppermute | solution.py:114
  10.5 4.4 %collective-permute-start.4 = (bf16[128,256]{1,0:T(8,128)(2,1)S(1)}, bf16[128,256]{1,0:T(8,128)(2,1)S(1)}, u32[]{:S(2)}, u32[]{:S(2)}) collective-permute-start(bf16[128,256]{1,0:T(8,128)(2,1)S(1)} %bitcast.42), channel_id=1, source_target_pairs={{0,4},{2,6},{4,0},{6,2},{8,12},{10,14},{12,8},{14,10},{1,5},{3,7},... | collective-permute-start | bytes 196616 | tf_op jit(solution)/shard_map/ppermute | solution.py:114
  13.7 29.7 %copy-start = (bf16[256,576]{0,1:T(8,128)(2,1)S(1)}, bf16[256,576]{0,1:T(8,128)(2,1)}, u32[]{:S(2)}) copy-start(bf16[256,576]{0,1:T(8,128)(2,1)} %param.6) | copy-start | bytes 884740
  13.7 29.7 %copy-start.1 = (s32[8]{0:T(128)S(1)}, s32[8]{0:T(128)}, u32[]{:S(2)}) copy-start(s32[8]{0:T(128)} %refs_0_.3) | copy-start | bytes 100
  15.0 22.3 %all-to-all-start = ((bf16[8,176,256]{2,1,0:T(8,128)(2,1)}), bf16[8,176,256]{2,1,0:T(8,128)(2,1)S(1)}, u32[]{:S(2)}, u32[]{:S(2)}) async-start(bf16[8,176,256]{2,1,0:T(8,128)(2,1)} %pad_maximum_fusion), calls=%async_computation | async-start | bytes 1441792 | tf_op jit(solution)/shard_map/all_to_all | solution.py:150
  18.8 13.5 %collective-permute-start.5 = (bf16[576,128]{1,0:T(8,128)(2,1)S(1)}, bf16[576,128]{1,0:T(8,128)(2,1)S(1)}, u32[]{:S(2)}, u32[]{:S(2)}) collective-permute-start(bf16[576,128]{1,0:T(8,128)(2,1)S(1)} %collective-permute-done.2.refs_6_.refs_12_), channel_id=1, source_target_pairs={{0,2},{2,0},{4,6},{6,4},{8,10},{10,8},{12,14},{14,12},{1,3},{3,1},... | collective-permute-start | bytes 442376 | tf_op jit(solution)/shard_map/ppermute | solution.py:114
  20.8 13.8 %collective-permute-start.6 = (bf16[576,128]{1,0:T(8,128)(2,1)S(1)}, bf16[576,128]{1,0:T(8,128)(2,1)S(1)}, u32[]{:S(2)}, u32[]{:S(2)}) collective-permute-start(bf16[576,128]{1,0:T(8,128)(2,1)S(1)} %collective-permute-done.refs_10_.refs_16_), channel_id=1, source_target_pairs={{0,2},{2,0},{4,6},{6,4},{8,10},{10,8},{12,14},{14,12},{1,3},{3,1},... | collective-permute-start | bytes 442376 | tf_op jit(solution)/shard_map/ppermute | solution.py:114
  20.8 14.9 %collective-permute-start.7 = (bf16[576,128]{1,0:T(8,128)(2,1)S(1)}, bf16[576,128]{1,0:T(8,128)(2,1)S(1)}, u32[]{:S(2)}, u32[]{:S(2)}) collective-permute-start(bf16[576,128]{1,0:T(8,128)(2,1)S(1)} %collective-permute-done.refs_10_.refs_16_), channel_id=1, source_target_pairs={{0,4},{2,6},{4,0},{6,2},{8,12},{10,14},{12,8},{14,10},{1,5},{3,7},... | collective-permute-start | bytes 442376 | tf_op jit(solution)/shard_map/ppermute | solution.py:114
  22.8 12.9 %collective-permute-start.8 = (bf16[576,128]{1,0:T(8,128)(2,1)S(1)}, bf16[576,128]{1,0:T(8,128)(2,1)S(1)}, u32[]{:S(2)}, u32[]{:S(2)}) collective-permute-start(bf16[576,128]{1,0:T(8,128)(2,1)S(1)} %collective-permute-done.1.refs_4_.refs_10_), channel_id=1, source_target_pairs={{0,1},{1,0},{2,3},{3,2},{4,5},{5,4},{6,7},{7,6},{8,9},{9,8},{10,11... | collective-permute-start | bytes 442376 | tf_op jit(solution)/shard_map/ppermute | solution.py:141
  22.8 12.9 %collective-permute-start.9 = (bf16[576,128]{1,0:T(8,128)(2,1)S(1)}, bf16[576,128]{1,0:T(8,128)(2,1)S(1)}, u32[]{:S(2)}, u32[]{:S(2)}) collective-permute-start(bf16[576,128]{1,0:T(8,128)(2,1)S(1)} %collective-permute-done.2.refs_6_.refs_12_), channel_id=1, source_target_pairs={{0,1},{1,0},{2,3},{3,2},{4,5},{5,4},{6,7},{7,6},{8,9},{9,8},{10,11... | collective-permute-start | bytes 442376 | tf_op jit(solution)/shard_map/ppermute | solution.py:141
  32.3 8.2 %collective-permute-start.13 = (bf16[576,128]{1,0:T(8,128)(2,1)S(1)}, bf16[576,128]{1,0:T(8,128)(2,1)S(1)}, u32[]{:S(2)}, u32[]{:S(2)}) collective-permute-start(bf16[576,128]{1,0:T(8,128)(2,1)S(1)} %collective-permute-done.refs_10_.refs_16_), channel_id=1, source_target_pairs={{0,1},{1,0},{2,3},{3,2},{4,5},{5,4},{6,7},{7,6},{8,9},{9,8},{10,11... | collective-permute-start | bytes 442376 | tf_op jit(solution)/shard_map/ppermute | solution.py:141
  34.6 5.4 %collective-permute-start.16 = (bf16[576,128]{1,0:T(8,128)(2,1)S(1)}, bf16[576,128]{1,0:T(8,128)(2,1)S(1)}, u32[]{:S(2)}, u32[]{:S(2)}) collective-permute-start(bf16[576,128]{1,0:T(8,128)(2,1)S(1)} %collective-permute-done.6.refs_12_.refs_18_), channel_id=1, source_target_pairs={{0,4},{2,6},{4,0},{6,2},{8,12},{10,14},{12,8},{14,10},{1,5},{3,7},... | collective-permute-start | bytes 442376 | tf_op jit(solution)/shard_map/ppermute | solution.py:114
  37.2 9.3 %collective-permute-start.11 = (bf16[4,128,256]{2,1,0:T(8,128)(2,1)S(1)}, bf16[4,128,256]{2,1,0:T(8,128)(2,1)S(1)}, u32[]{:S(2)}, u32[]{:S(2)}) collective-permute-start(bf16[4,128,256]{2,1,0:T(8,128)(2,1)S(1)} %constant_dynamic-slice_fusion), channel_id=1, source_target_pairs={{0,16},{16,0},{1,17},{17,1},{2,18},{18,2},{3,19},{19,3},{4,20},{20... | collective-permute-start | bytes 786440 | tf_op jit(solution)/shard_map/ppermute | solution.py:156
  40.0 1.4 %collective-permute-start.17 = (bf16[576,128]{1,0:T(8,128)(2,1)S(1)}, bf16[576,128]{1,0:T(8,128)(2,1)S(1)}, u32[]{:S(2)}, u32[]{:S(2)}) collective-permute-start(bf16[576,128]{1,0:T(8,128)(2,1)S(1)} %collective-permute-done.16.refs_16_.refs_22_), channel_id=1, source_target_pairs={{0,1},{1,0},{2,3},{3,2},{4,5},{5,4},{6,7},{7,6},{8,9},{9,8},{10,11... | collective-permute-start | bytes 442376 | tf_op jit(solution)/shard_map/ppermute | solution.py:141
  40.0 3.5 %collective-permute-start.12 = (bf16[576,128]{1,0:T(8,128)(2,1)S(1)}, bf16[576,128]{1,0:T(8,128)(2,1)S(1)}, u32[]{:S(2)}, u32[]{:S(2)}) collective-permute-start(bf16[576,128]{1,0:T(8,128)(2,1)S(1)} %collective-permute-done.5.refs_8_.refs_14_), channel_id=1, source_target_pairs={{0,1},{1,0},{2,3},{3,2},{4,5},{5,4},{6,7},{7,6},{8,9},{9,8},{10,11... | collective-permute-start | bytes 442376 | tf_op jit(solution)/shard_map/ppermute | solution.py:141
  40.5 3.0 %collective-permute-start.14 = (bf16[576,128]{1,0:T(8,128)(2,1)S(1)}, bf16[576,128]{1,0:T(8,128)(2,1)S(1)}, u32[]{:S(2)}, u32[]{:S(2)}) collective-permute-start(bf16[576,128]{1,0:T(8,128)(2,1)S(1)} %collective-permute-done.6.refs_12_.refs_18_), channel_id=1, source_target_pairs={{0,1},{1,0},{2,3},{3,2},{4,5},{5,4},{6,7},{7,6},{8,9},{9,8},{10,11... | collective-permute-start | bytes 442376 | tf_op jit(solution)/shard_map/ppermute | solution.py:141
  40.5 3.0 %collective-permute-start.15 = (bf16[576,128]{1,0:T(8,128)(2,1)S(1)}, bf16[576,128]{1,0:T(8,128)(2,1)S(1)}, u32[]{:S(2)}, u32[]{:S(2)}) collective-permute-start(bf16[576,128]{1,0:T(8,128)(2,1)S(1)} %collective-permute-done.7.refs_14_.refs_20_), channel_id=1, source_target_pairs={{0,1},{1,0},{2,3},{3,2},{4,5},{5,4},{6,7},{7,6},{8,9},{9,8},{10,11... | collective-permute-start | bytes 442376 | tf_op jit(solution)/shard_map/ppermute | solution.py:141
  41.4 5.2 %collective-permute-start.10 = (bf16[128,256]{1,0:T(8,128)(2,1)S(1)}, bf16[128,256]{1,0:T(8,128)(2,1)S(1)}, u32[]{:S(2)}, u32[]{:S(2)}) collective-permute-start(bf16[128,256]{1,0:T(8,128)(2,1)S(1)} %bitcast.43), channel_id=1, source_target_pairs={{0,6},{2,4},{4,2},{6,0},{8,14},{10,12},{12,10},{14,8},{1,7},{3,5},... | collective-permute-start | bytes 196616 | tf_op jit(solution)/shard_map/ppermute | solution.py:114

commit v9 on v8

--- a/solution.py
+++ b/solution.py
@@ -113,11 +113,10 @@
     def swap(array, bit):
         return lax.ppermute(array, "ctx", [(i, i ^ bit) for i in range(contexts)])
 
-    weight = kv_weight.reshape(depth, contexts, 2, pair, width)
-    weight = lax.dynamic_index_in_dim(weight, group, 2, keepdims=False)
-    weight = weight.transpose(1, 2, 0, 3).reshape(contexts, pair * depth, width)
     me = lax.axis_index("ctx")
     by_head = kv_weight.reshape(depth, contexts, 2, pair, width)
+    weight = lax.dynamic_index_in_dim(by_head, group, 2, keepdims=False)
+    weight = weight.transpose(1, 2, 0, 3).reshape(contexts, pair * depth, width)
 
     def second_pair(owner):
         part = lax.dynamic_slice(
@@ -151,12 +150,15 @@
     for slot, source, bit in LATE:
         held[slot] = swap(held[source], bit)
     traded = {slot: trade(held[slot]) for slot in (1, 2)}
-    packed, kept, held[3], held[5], held[6], traded[1], traded[2] = lax.optimization_barrier((packed, kept, held[3], held[5], held[6], traded[1], traded[2]))
+    waited = lax.optimization_barrier((packed, kept, held[3], held[5], held[6], traded))
+    packed, kept, held[3], held[5], held[6], traded = waited
     others = lax.dynamic_slice_in_dim(packed, (me // near ^ 1) * near, near, 0)[:, :pair * depth]
     others = lax.ppermute(others, "groups", [(0, 1), (1, 0)])
     pieces = [turned_cache]
     for slot in range(1, contexts):
-        pieces += [held[slot], traded.get(slot, None) if slot in traded else trade(held[slot])]
+        if slot not in traded:
+            traded[slot] = trade(held[slot])
+        pieces += [held[slot], traded[slot]]
 
     query_count = contexts * query_rows
     on_chip = pl.BlockSpec(memory_space=pltpu.VMEM)
@@ -170,7 +172,7 @@
             out_specs=on_chip,
             scratch_shapes=[pltpu.VMEM((contexts, pair * depth, width), jnp.bfloat16)] * which,
             compiler_params=pltpu.CompilerParams(vmem_limit_bytes=16 * 2**20),
-            cost_estimate=pl.CostEstimate(flops=1048576, bytes_accessed=1 << 20, transcendentals=0),
+            cost_estimate=pl.CostEstimate(flops=1 << 20, bytes_accessed=1 << 20, transcendentals=0),
             name="attend_" + ("first", "second")[which],
         )(block_order, span_start, *operands, *pieces)
 
@@ -275,7 +277,7 @@
 
     def local(queries, latent_cache, kv_weight, block_order, span_start):
         arrays = (queries, latent_cache, kv_weight, block_order, span_start)
-        paired = queries.shape[1] % (2 * contexts) == 0 and contexts == 8
+        paired = queries.shape[1] % (2 * contexts) == 0 and contexts == 1 + len(EARLY) + len(LATE)
         if paired and cores == 2 and mesh.shape["groups"] == 2:
             return split_by_heads(contexts, cores, *arrays)
         return split_by_context(*arrays)

time: 62.1 us -> 62.1 us (level)
  no operation moved by 1% of the time
where the time goes in v9:
time: 62.1 us; the launch traced here: 61.8 us
  starting transfers between devices  21.9 us (35%)
  waiting for transfers between devices  15.6 us (25%)
  blocking collectives  11.6 us (19%)
  Pallas kernels  5.69 us (9%)
  local copies, waits for them, and re-layouts  4.92 us (8%)
  other arithmetic  1.19 us (2%)
  between operations  0.86 us (1%)
    ppermute x10, starting transfers between devices, swap(): return lax.ppermute(array, 'ctx', [(i, i ^ bit) for i in range(contexts)])  14.9 us
    ppermute x10, waiting for transfers between devices, swap(): return lax.ppermute(array, 'ctx', [(i, i ^ bit) for i in range(contexts)])  13.8 us
    all_to_all x1, blocking collectives, split_by_heads(): attended = lax.all_to_all(attended, 'ctx', 0, 0, tiled=True)  11.6 us
    pallas_call x2, Pallas kernels, attend(): pl.pallas_call(functools.partial(attend_kernel, contexts, pair, which), o...  5.69 us
    all_to_all x1, starting transfers between devices, split_by_heads(): packed = lax.all_to_all(packed, 'ctx', 0, 0, tiled=True)  3.82 us
    ppermute x1, starting transfers between devices, split_by_heads(): others = lax.ppermute(others, 'groups', [(0, 1), (1, 0)])  1.58 us
    ppermute x7, starting transfers between devices, trade(): return lax.ppermute(array, 'tp', [(0, 1), (1, 0)])  1.53 us
    reshape x1, local copies, waits for them, and re-layouts, split_by_heads(): by_head = kv_weight.reshape(depth, contexts, 2, pair, width)  1.51 us
  transfers between devices with their start and end apart: 19, of which 8 were waited for; matrix products, arithmetic and copies ran while one was open for 7% of the time, Pallas kernels for 5%

profile of v9, /device:TPU:0, one launch (start us, length us, event | category | flops | bytes accessed | tf_op | source)
XLA Modules:
  0.0 61.8 jit_solution(8970115862140711297)
XLA Ops:
  0.0 0.9 %dynamic-slice_bitcast_fusion = bf16[576,128]{1,0:T(8,128)(2,1)S(1)} fusion(bf16[256,576]{0,1:T(8,128)(2,1)} %param.6, s32[]{:T(128)S(6)} %select_n.44), kind=kLoop, calls=%fused_computation.2 | loop fusion | bytes 294916 | tf_op jit(solution)/shard_map/dynamic_slice | solution.py:144
  0.9 4.1 %collective-permute-start = (bf16[576,128]{1,0:T(8,128)(2,1)S(1)}, bf16[576,128]{1,0:T(8,128)(2,1)S(1)}, u32[]{:S(2)}, u32[]{:S(2)}) collective-permute-start(bf16[576,128]{1,0:T(8,128)(2,1)S(1)} %dynamic-slice_bitcast_fusion), channel_id=1, source_target_pairs={{0,8},{2,10},{4,12},{6,14},{8,0},{10,2},{12,4},{14,6},{1,9},{3,11}... | collective-permute-start | bytes 442376 | tf_op jit(solution)/shard_map/ppermute | solution.py:114
  5.0 1.5 %collective-permute-start.1 = (bf16[576,128]{1,0:T(8,128)(2,1)S(1)}, bf16[576,128]{1,0:T(8,128)(2,1)S(1)}, u32[]{:S(2)}, u32[]{:S(2)}) collective-permute-start(bf16[576,128]{1,0:T(8,128)(2,1)S(1)} %dynamic-slice_bitcast_fusion), channel_id=1, source_target_pairs={{0,2},{2,0},{4,6},{6,4},{8,10},{10,8},{12,14},{14,12},{1,3},{3,1},... | collective-permute-start | bytes 442376 | tf_op jit(solution)/shard_map/ppermute | solution.py:114
  6.5 1.6 %collective-permute-start.2 = (bf16[576,128]{1,0:T(8,128)(2,1)S(1)}, bf16[576,128]{1,0:T(8,128)(2,1)S(1)}, u32[]{:S(2)}, u32[]{:S(2)}) collective-permute-start(bf16[576,128]{1,0:T(8,128)(2,1)S(1)} %dynamic-slice_bitcast_fusion), channel_id=1, source_target_pairs={{0,4},{2,6},{4,0},{6,2},{8,12},{10,14},{12,8},{14,10},{1,5},{3,7},... | collective-permute-start | bytes 442376 | tf_op jit(solution)/shard_map/ppermute | solution.py:114
  8.1 1.5 %reshape.48 = bf16[64,8,2,2,256]{4,3,2,1,0:T(2,128)(2,1)S(1)} reshape(bf16[64,32,256]{2,1,0:T(8,128)(2,1)} %param.7) | data formatting | bytes 2097152 | tf_op jit(solution)/shard_map/reshape | solution.py:117
  9.6 0.3 constant_dynamic-slice_fusion.1
  9.9 0.6 collective-permute-start.3
  10.5 0.5 collective-permute-start.4
  11.1 0.1 reshape.50
  11.2 0.2 copy.8
  11.4 0.3 broadcast_select_fusion
  11.7 0.1 slice_bitcast_fusion
  11.8 0.1 slice_bitcast_fusion.1
  11.9 0.4 constant_dynamic-slice_fusion.5
  12.3 0.1 reshape.52
  12.5 0.1 copy.9
  12.6 0.1 reshape.51
  12.7 0.2 copy.6
  12.8 0.9 %pad_maximum_fusion = bf16[8,176,256]{2,1,0:T(8,128)(2,1)} fusion(bf16[8,16,256]{2,1,0:T(8,128)(2,1)S(1)} %reshape.52, bf16[8,32,256]{2,1,0:T(8,128)(2,1)S(1)} %reshape.51, bf16[8,128,256]{2,1,0:T(8,128)(2,1)S(1)} %bitcast.40), kind=kLoop, calls=%fused_computation | loop fusion | flops 2162688 | bytes 1441792 | tf_op jit(solution)/shard_map/concatenate | solution.py:137
  13.7 0.5 collective-permute-done.3.refs_4_
  14.3 0.7 %collective-permute-done.4.refs_5_ = bf16[128,256]{1,0:T(8,128)(2,1)S(1)} collective-permute-done((bf16[128,256]{1,0:T(8,128)(2,1)S(1)}, bf16[128,256]{1,0:T(8,128)(2,1)S(1)}, u32[]{:S(2)}, u32[]{:S(2)}) %collective-permute-start.4) | collective-permute-done | bytes 65568 | tf_op jit(solution)/shard_map/ppermute | solution.py:114
  14.9 0.0 collective-permute-done.refs_10_.refs_16_
  14.9 0.0 collective-permute-done.1.refs_4_.refs_10_
  15.0 0.0 collective-permute-done.2.refs_6_.refs_12_
  15.0 3.8 %all-to-all-start = ((bf16[8,176,256]{2,1,0:T(8,128)(2,1)}), bf16[8,176,256]{2,1,0:T(8,128)(2,1)S(1)}, u32[]{:S(2)}, u32[]{:S(2)}) async-start(bf16[8,176,256]{2,1,0:T(8,128)(2,1)} %pad_maximum_fusion), calls=%async_computation | async-start | bytes 1441792 | tf_op jit(solution)/shard_map/all_to_all | solution.py:149
  18.8 2.0 %collective-permute-start.5 = (bf16[576,128]{1,0:T(8,128)(2,1)S(1)}, bf16[576,128]{1,0:T(8,128)(2,1)S(1)}, u32[]{:S(2)}, u32[]{:S(2)}) collective-permute-start(bf16[576,128]{1,0:T(8,128)(2,1)S(1)} %collective-permute-done.2.refs_6_.refs_12_), channel_id=1, source_target_pairs={{0,2},{2,0},{4,6},{6,4},{8,10},{10,8},{12,14},{14,12},{1,3},{3,1},... | collective-permute-start | bytes 442376 | tf_op jit(solution)/shard_map/ppermute | solution.py:114
  20.8 0.0 collective-permute-start.6
  20.8 2.0 %collective-permute-start.7 = (bf16[576,128]{1,0:T(8,128)(2,1)S(1)}, bf16[576,128]{1,0:T(8,128)(2,1)S(1)}, u32[]{:S(2)}, u32[]{:S(2)}) collective-permute-start(bf16[576,128]{1,0:T(8,128)(2,1)S(1)} %collective-permute-done.refs_10_.refs_16_), channel_id=1, source_target_pairs={{0,4},{2,6},{4,0},{6,2},{8,12},{10,14},{12,8},{14,10},{1,5},{3,7},... | collective-permute-start | bytes 442376 | tf_op jit(solution)/shard_map/ppermute | solution.py:114
  22.8 0.0 collective-permute-start.8
  22.8 0.5 collective-permute-start.9
  23.4 8.9 %collective-permute-done.5.refs_8_.refs_14_ = bf16[576,128]{1,0:T(8,128)(2,1)S(1)} collective-permute-done((bf16[576,128]{1,0:T(8,128)(2,1)S(1)}, bf16[576,128]{1,0:T(8,128)(2,1)S(1)}, u32[]{:S(2)}, u32[]{:S(2)}) %collective-permute-start.5) | collective-permute-done | bytes 147488 | tf_op jit(solution)/shard_map/ppermute | solution.py:114
  32.3 0.0 collective-permute-start.13
  32.3 2.3 %collective-permute-done.6.refs_12_.refs_18_ = bf16[576,128]{1,0:T(8,128)(2,1)S(1)} collective-permute-done((bf16[576,128]{1,0:T(8,128)(2,1)S(1)}, bf16[576,128]{1,0:T(8,128)(2,1)S(1)}, u32[]{:S(2)}, u32[]{:S(2)}) %collective-permute-start.6) | collective-permute-done | bytes 147488 | tf_op jit(solution)/shard_map/ppermute | solution.py:114
  34.6 1.2 %collective-permute-start.16 = (bf16[576,128]{1,0:T(8,128)(2,1)S(1)}, bf16[576,128]{1,0:T(8,128)(2,1)S(1)}, u32[]{:S(2)}, u32[]{:S(2)}) collective-permute-start(bf16[576,128]{1,0:T(8,128)(2,1)S(1)} %collective-permute-done.6.refs_12_.refs_18_), channel_id=1, source_target_pairs={{0,4},{2,6},{4,0},{6,2},{8,12},{10,14},{12,8},{14,10},{1,5},{3,7},... | collective-permute-start | bytes 442376 | tf_op jit(solution)/shard_map/ppermute | solution.py:114
  35.7 0.0 collective-permute-done.9.refs_7_.refs_13_
  35.7 1.5 %all-to-all-done.refs_2_ = bf16[8,176,256]{2,1,0:T(8,128)(2,1)S(1)} async-done(((bf16[8,176,256]{2,1,0:T(8,128)(2,1)}), bf16[8,176,256]{2,1,0:T(8,128)(2,1)S(1)}, u32[]{:S(2)}, u32[]{:S(2)}) %all-to-all-start) | async-done | bytes 720928 | tf_op jit(solution)/shard_map/all_to_all | solution.py:149
  37.2 1.6 %collective-permute-start.11 = (bf16[4,128,256]{2,1,0:T(8,128)(2,1)S(1)}, bf16[4,128,256]{2,1,0:T(8,128)(2,1)S(1)}, u32[]{:S(2)}, u32[]{:S(2)}) collective-permute-start(bf16[4,128,256]{2,1,0:T(8,128)(2,1)S(1)} %constant_dynamic-slice_fusion), channel_id=1, source_target_pairs={{0,16},{16,0},{1,17},{17,1},{2,18},{18,2},{3,19},{19,3},{4,20},{20... | collective-permute-start | bytes 786440 | tf_op jit(solution)/shard_map/ppermute | solution.py:156
  38.8 1.2 %collective-permute-done.16.refs_16_.refs_22_ = bf16[576,128]{1,0:T(8,128)(2,1)S(1)} collective-permute-done((bf16[576,128]{1,0:T(8,128)(2,1)S(1)}, bf16[576,128]{1,0:T(8,128)(2,1)S(1)}, u32[]{:S(2)}, u32[]{:S(2)}) %collective-permute-start.16) | collective-permute-done | bytes 147488 | tf_op jit(solution)/shard_map/ppermute | solution.py:114
  40.0 0.5 collective-permute-start.12
  40.5 0.0 collective-permute-start.14
  40.5 0.5 collective-permute-start.15
  41.0 0.3 collective-permute-done.17.refs_17_.refs_23_
  41.4 1.4 %collective-permute-start.10 = (bf16[128,256]{1,0:T(8,128)(2,1)S(1)}, bf16[128,256]{1,0:T(8,128)(2,1)S(1)}, u32[]{:S(2)}, u32[]{:S(2)}) collective-permute-start(bf16[128,256]{1,0:T(8,128)(2,1)S(1)} %bitcast.43), channel_id=1, source_target_pairs={{0,6},{2,4},{4,2},{6,0},{8,14},{10,12},{12,10},{14,8},{1,7},{3,5},... | collective-permute-start | bytes 196616 | tf_op jit(solution)/shard_map/ppermute | solution.py:114
  43.5 2.8 %attend_first.1.refs_8_ = bf16[128,256]{1,0:T(8,128)(2,1)S(1)} custom-call(s32[8]{0:T(128)S(1)} %copy-done.1, s32[1]{0:T(128)S(6)} %copy.15.refs_1_, bf16[8,176,256]{2,1,0:T(8,128)(2,1)S(1)} %all-to-all-done.refs_2_, bf16[576,256]{1,0:T(8,128)(2,1)S(1)} %bitcast.36, bf16[576,128]{1,0:T(8,128)(2,1)S(1)} %collective-permute-done.1.refs_4_.refs_10_, ...), custom_call_target="tpu_custom_call" | custom-call | flops 1048576 | bytes 1048576 | tf_op jit(solution)/shard_map/attend_first/pallas_call | solution.py:168
  46.3 0.2 collective-permute-done.10.refs_6_
  46.5 2.9 %attend_second.1 = bf16[128,512]{1,0:T(8,128)(2,1)S(1)} custom-call(s32[8]{0:T(128)S(1)} %copy-done.1, s32[1]{0:T(128)S(6)} %copy.15.refs_1_, bf16[8,176,256]{2,1,0:T(8,128)(2,1)S(1)} %all-to-all-done.refs_2_, bf16[128,256]{1,0:T(8,128)(2,1)S(1)} %bitcast.39, bf16[128,256]{1,0:T(8,128)(2,1)S(1)} %collective-permute-done.3.refs_4_, ...), custom_call_target="tpu_custom_call" | custom-call | flops 1048576 | bytes 1048576 | tf_op jit(solution)/shard_map/attend_second/pallas_call | solution.py:168
  49.4 11.6 %all_to_all.10 = bf16[8,16,512]{2,1,0:T(8,128)(2,1)S(1)} all-to-all(bf16[8,16,512]{2,1,0:T(8,128)(2,1)S(1)} %bitcast.38), channel_id=1, replica_groups=mesh['groups'=2,'ctx'=8,'tp'=2] {'ctx'}, dimensions={0} | all-to-all | bytes 262144 | tf_op jit(solution)/shard_map/all_to_all | solution.py:182
  61.1 0.7 %copy.14 = bf16[8,16,4,128]{3,2,0,1:T(4,128)(2,1)} copy(bf16[8,16,4,128]{3,2,1,0:T(4,128)(2,1)S(1)} %reshape.62) | data formatting | bytes 262144 | tf_op jit(solution)/shard_map/reshape | solution.py:183
  (20 shorter events, 0.1 us)
Async XLA Ops:
  0.9 14.0 %collective-permute-start = (bf16[576,128]{1,0:T(8,128)(2,1)S(1)}, bf16[576,128]{1,0:T(8,128)(2,1)S(1)}, u32[]{:S(2)}, u32[]{:S(2)}) collective-permute-start(bf16[576,128]{1,0:T(8,128)(2,1)S(1)} %dynamic-slice_bitcast_fusion), channel_id=1, source_target_pairs={{0,8},{2,10},{4,12},{6,14},{8,0},{10,2},{12,4},{14,6},{1,9},{3,11}... | collective-permute-start | bytes 442376 | tf_op jit(solution)/shard_map/ppermute | solution.py:114
  5.0 9.9 %collective-permute-start.1 = (bf16[576,128]{1,0:T(8,128)(2,1)S(1)}, bf16[576,128]{1,0:T(8,128)(2,1)S(1)}, u32[]{:S(2)}, u32[]{:S(2)}) collective-permute-start(bf16[576,128]{1,0:T(8,128)(2,1)S(1)} %dynamic-slice_bitcast_fusion), channel_id=1, source_target_pairs={{0,2},{2,0},{4,6},{6,4},{8,10},{10,8},{12,14},{14,12},{1,3},{3,1},... | collective-permute-start | bytes 442376 | tf_op jit(solution)/shard_map/ppermute | solution.py:114
  6.5 8.4 %collective-permute-start.2 = (bf16[576,128]{1,0:T(8,128)(2,1)S(1)}, bf16[576,128]{1,0:T(8,128)(2,1)S(1)}, u32[]{:S(2)}, u32[]{:S(2)}) collective-permute-start(bf16[576,128]{1,0:T(8,128)(2,1)S(1)} %dynamic-slice_bitcast_fusion), channel_id=1, source_target_pairs={{0,4},{2,6},{4,0},{6,2},{8,12},{10,14},{12,8},{14,10},{1,5},{3,7},... | collective-permute-start | bytes 442376 | tf_op jit(solution)/shard_map/ppermute | solution.py:114
  8.1 3.0 %copy-start.2 = (bf16[16,32,192]{2,1,0:T(8,128)(2,1)S(1)}, bf16[16,32,192]{2,1,0:T(8,128)(2,1)}, u32[]{:S(2)}) copy-start(bf16[16,32,192]{2,1,0:T(8,128)(2,1)} %param.5) | copy-start | bytes 589828
  9.9 4.3 %collective-permute-start.3 = (bf16[128,256]{1,0:T(8,128)(2,1)S(1)}, bf16[128,256]{1,0:T(8,128)(2,1)S(1)}, u32[]{:S(2)}, u32[]{:S(2)}) collective-permute-start(bf16[128,256]{1,0:T(8,128)(2,1)S(1)} %bitcast.41), channel_id=1, source_target_pairs={{0,2},{2,0},{4,6},{6,4},{8,10},{10,8},{12,14},{14,12},{1,3},{3,1},... | collective-permute-start | bytes 196616 | tf_op jit(solution)/shard_map/ppermute | solution.py:114
  10.5 4.4 %collective-permute-start.4 = (bf16[128,256]{1,0:T(8,128)(2,1)S(1)}, bf16[128,256]{1,0:T(8,128)(2,1)S(1)}, u32[]{:S(2)}, u32[]{:S(2)}) collective-permute-start(bf16[128,256]{1,0:T(8,128)(2,1)S(1)} %bitcast.42), channel_id=1, source_target_pairs={{0,4},{2,6},{4,0},{6,2},{8,12},{10,14},{12,8},{14,10},{1,5},{3,7},... | collective-permute-start | bytes 196616 | tf_op jit(solution)/shard_map/ppermute | solution.py:114
  13.7 29.7 %copy-start = (bf16[256,576]{0,1:T(8,128)(2,1)S(1)}, bf16[256,576]{0,1:T(8,128)(2,1)}, u32[]{:S(2)}) copy-start(bf16[256,576]{0,1:T(8,128)(2,1)} %param.6) | copy-start | bytes 884740
  13.7 29.7 %copy-start.1 = (s32[8]{0:T(128)S(1)}, s32[8]{0:T(128)}, u32[]{:S(2)}) copy-start(s32[8]{0:T(128)} %refs_0_.3) | copy-start | bytes 100
  15.0 22.3 %all-to-all-start = ((bf16[8,176,256]{2,1,0:T(8,128)(2,1)}), bf16[8,176,256]{2,1,0:T(8,128)(2,1)S(1)}, u32[]{:S(2)}, u32[]{:S(2)}) async-start(bf16[8,176,256]{2,1,0:T(8,128)(2,1)} %pad_maximum_fusion), calls=%async_computation | async-start | bytes 1441792 | tf_op jit(solution)/shard_map/all_to_all | solution.py:149
  18.8 13.5 %collective-permute-start.5 = (bf16[576,128]{1,0:T(8,128)(2,1)S(1)}, bf16[576,128]{1,0:T(8,128)(2,1)S(1)}, u32[]{:S(2)}, u32[]{:S(2)}) collective-permute-start(bf16[576,128]{1,0:T(8,128)(2,1)S(1)} %collective-permute-done.2.refs_6_.refs_12_), channel_id=1, source_target_pairs={{0,2},{2,0},{4,6},{6,4},{8,10},{10,8},{12,14},{14,12},{1,3},{3,1},... | collective-permute-start | bytes 442376 | tf_op jit(solution)/shard_map/ppermute | solution.py:114
  20.8 13.8 %collective-permute-start.6 = (bf16[576,128]{1,0:T(8,128)(2,1)S(1)}, bf16[576,128]{1,0:T(8,128)(2,1)S(1)}, u32[]{:S(2)}, u32[]{:S(2)}) collective-permute-start(bf16[576,128]{1,0:T(8,128)(2,1)S(1)} %collective-permute-done.refs_10_.refs_16_), channel_id=1, source_target_pairs={{0,2},{2,0},{4,6},{6,4},{8,10},{10,8},{12,14},{14,12},{1,3},{3,1},... | collective-permute-start | bytes 442376 | tf_op jit(solution)/shard_map/ppermute | solution.py:114
  20.8 14.9 %collective-permute-start.7 = (bf16[576,128]{1,0:T(8,128)(2,1)S(1)}, bf16[576,128]{1,0:T(8,128)(2,1)S(1)}, u32[]{:S(2)}, u32[]{:S(2)}) collective-permute-start(bf16[576,128]{1,0:T(8,128)(2,1)S(1)} %collective-permute-done.refs_10_.refs_16_), channel_id=1, source_target_pairs={{0,4},{2,6},{4,0},{6,2},{8,12},{10,14},{12,8},{14,10},{1,5},{3,7},... | collective-permute-start | bytes 442376 | tf_op jit(solution)/shard_map/ppermute | solution.py:114
  22.8 12.9 %collective-permute-start.8 = (bf16[576,128]{1,0:T(8,128)(2,1)S(1)}, bf16[576,128]{1,0:T(8,128)(2,1)S(1)}, u32[]{:S(2)}, u32[]{:S(2)}) collective-permute-start(bf16[576,128]{1,0:T(8,128)(2,1)S(1)} %collective-permute-done.1.refs_4_.refs_10_), channel_id=1, source_target_pairs={{0,1},{1,0},{2,3},{3,2},{4,5},{5,4},{6,7},{7,6},{8,9},{9,8},{10,11... | collective-permute-start | bytes 442376 | tf_op jit(solution)/shard_map/ppermute | solution.py:140
  22.8 12.9 %collective-permute-start.9 = (bf16[576,128]{1,0:T(8,128)(2,1)S(1)}, bf16[576,128]{1,0:T(8,128)(2,1)S(1)}, u32[]{:S(2)}, u32[]{:S(2)}) collective-permute-start(bf16[576,128]{1,0:T(8,128)(2,1)S(1)} %collective-permute-done.2.refs_6_.refs_12_), channel_id=1, source_target_pairs={{0,1},{1,0},{2,3},{3,2},{4,5},{5,4},{6,7},{7,6},{8,9},{9,8},{10,11... | collective-permute-start | bytes 442376 | tf_op jit(solution)/shard_map/ppermute | solution.py:140
  32.3 8.2 %collective-permute-start.13 = (bf16[576,128]{1,0:T(8,128)(2,1)S(1)}, bf16[576,128]{1,0:T(8,128)(2,1)S(1)}, u32[]{:S(2)}, u32[]{:S(2)}) collective-permute-start(bf16[576,128]{1,0:T(8,128)(2,1)S(1)} %collective-permute-done.refs_10_.refs_16_), channel_id=1, source_target_pairs={{0,1},{1,0},{2,3},{3,2},{4,5},{5,4},{6,7},{7,6},{8,9},{9,8},{10,11... | collective-permute-start | bytes 442376 | tf_op jit(solution)/shard_map/ppermute | solution.py:140
  34.6 5.4 %collective-permute-start.16 = (bf16[576,128]{1,0:T(8,128)(2,1)S(1)}, bf16[576,128]{1,0:T(8,128)(2,1)S(1)}, u32[]{:S(2)}, u32[]{:S(2)}) collective-permute-start(bf16[576,128]{1,0:T(8,128)(2,1)S(1)} %collective-permute-done.6.refs_12_.refs_18_), channel_id=1, source_target_pairs={{0,4},{2,6},{4,0},{6,2},{8,12},{10,14},{12,8},{14,10},{1,5},{3,7},... | collective-permute-start | bytes 442376 | tf_op jit(solution)/shard_map/ppermute | solution.py:114
  37.2 9.3 %collective-permute-start.11 = (bf16[4,128,256]{2,1,0:T(8,128)(2,1)S(1)}, bf16[4,128,256]{2,1,0:T(8,128)(2,1)S(1)}, u32[]{:S(2)}, u32[]{:S(2)}) collective-permute-start(bf16[4,128,256]{2,1,0:T(8,128)(2,1)S(1)} %constant_dynamic-slice_fusion), channel_id=1, source_target_pairs={{0,16},{16,0},{1,17},{17,1},{2,18},{18,2},{3,19},{19,3},{4,20},{20... | collective-permute-start | bytes 786440 | tf_op jit(solution)/shard_map/ppermute | solution.py:156
  40.0 1.4 %collective-permute-start.17 = (bf16[576,128]{1,0:T(8,128)(2,1)S(1)}, bf16[576,128]{1,0:T(8,128)(2,1)S(1)}, u32[]{:S(2)}, u32[]{:S(2)}) collective-permute-start(bf16[576,128]{1,0:T(8,128)(2,1)S(1)} %collective-permute-done.16.refs_16_.refs_22_), channel_id=1, source_target_pairs={{0,1},{1,0},{2,3},{3,2},{4,5},{5,4},{6,7},{7,6},{8,9},{9,8},{10,11... | collective-permute-start | bytes 442376 | tf_op jit(solution)/shard_map/ppermute | solution.py:140
  40.0 3.5 %collective-permute-start.12 = (bf16[576,128]{1,0:T(8,128)(2,1)S(1)}, bf16[576,128]{1,0:T(8,128)(2,1)S(1)}, u32[]{:S(2)}, u32[]{:S(2)}) collective-permute-start(bf16[576,128]{1,0:T(8,128)(2,1)S(1)} %collective-permute-done.5.refs_8_.refs_14_), channel_id=1, source_target_pairs={{0,1},{1,0},{2,3},{3,2},{4,5},{5,4},{6,7},{7,6},{8,9},{9,8},{10,11... | collective-permute-start | bytes 442376 | tf_op jit(solution)/shard_map/ppermute | solution.py:140
  40.5 3.0 %collective-permute-start.14 = (bf16[576,128]{1,0:T(8,128)(2,1)S(1)}, bf16[576,128]{1,0:T(8,128)(2,1)S(1)}, u32[]{:S(2)}, u32[]{:S(2)}) collective-permute-start(bf16[576,128]{1,0:T(8,128)(2,1)S(1)} %collective-permute-done.6.refs_12_.refs_18_), channel_id=1, source_target_pairs={{0,1},{1,0},{2,3},{3,2},{4,5},{5,4},{6,7},{7,6},{8,9},{9,8},{10,11... | collective-permute-start | bytes 442376 | tf_op jit(solution)/shard_map/ppermute | solution.py:140
  40.5 3.0 %collective-permute-start.15 = (bf16[576,128]{1,0:T(8,128)(2,1)S(1)}, bf16[576,128]{1,0:T(8,128)(2,1)S(1)}, u32[]{:S(2)}, u32[]{:S(2)}) collective-permute-start(bf16[576,128]{1,0:T(8,128)(2,1)S(1)} %collective-permute-done.7.refs_14_.refs_20_), channel_id=1, source_target_pairs={{0,1},{1,0},{2,3},{3,2},{4,5},{5,4},{6,7},{7,6},{8,9},{9,8},{10,11... | collective-permute-start | bytes 442376 | tf_op jit(solution)/shard_map/ppermute | solution.py:140
  41.4 5.2 %collective-permute-start.10 = (bf16[128,256]{1,0:T(8,128)(2,1)S(1)}, bf16[128,256]{1,0:T(8,128)(2,1)S(1)}, u32[]{:S(2)}, u32[]{:S(2)}) collective-permute-start(bf16[128,256]{1,0:T(8,128)(2,1)S(1)} %bitcast.43), channel_id=1, source_target_pairs={{0,6},{2,4},{4,2},{6,0},{8,14},{10,12},{12,10},{14,8},{1,7},{3,5},... | collective-permute-start | bytes 196616 | tf_op jit(solution)/shard_map/ppermute | solution.py:114

commit v10 on v9

--- a/solution.py
+++ b/solution.py
@@ -50,7 +50,7 @@
         begin = first + 2 * query_rows
         turned = packed_ref[:, begin:begin + query_rows, head * ROPE:(head + 1) * ROPE]
         turned = turned.reshape(query_count, ROPE)
-        queries.append(jnp.concatenate([part, turned, jnp.zeros_like(turned)], axis=1))
+        queries.append(jnp.concatenate([part, turned], axis=1))
     weights = jnp.concatenate(weights, axis=1).T
     ahead = lax.broadcasted_iota(jnp.int32, (query_count, half), 1) - lax.broadcasted_iota(
         jnp.int32, (query_count, half), 0
@@ -76,7 +76,7 @@
         for member in range(pair):
             begin = member * width
             keys = jnp.concatenate(
-                [projected[begin:begin + NOPE], rope, jnp.zeros_like(rope)], axis=0
+                [projected[begin:begin + NOPE], rope], axis=0
             )
             score = jnp.dot(queries[member], keys, preferred_element_type=jnp.float32)
             scores[member].append(jnp.where(visible, score, HIDDEN))

time: 62.1 us -> 62.1 us (level)
  no operation moved by 1% of the time
where the time goes in v10:
time: 62.1 us; the launch traced here: 61.8 us
  starting transfers between devices  21.9 us (35%)
  waiting for transfers between devices  15.6 us (25%)
  blocking collectives  11.6 us (19%)
  Pallas kernels  5.69 us (9%)
  local copies, waits for them, and re-layouts  4.92 us (8%)
  other arithmetic  1.19 us (2%)
  between operations  0.86 us (1%)
    ppermute x10, starting transfers between devices, swap(): return lax.ppermute(array, 'ctx', [(i, i ^ bit) for i in range(contexts)])  14.9 us
    ppermute x10, waiting for transfers between devices, swap(): return lax.ppermute(array, 'ctx', [(i, i ^ bit) for i in range(contexts)])  13.8 us
    all_to_all x1, blocking collectives, split_by_heads(): attended = lax.all_to_all(attended, 'ctx', 0, 0, tiled=True)  11.6 us
    pallas_call x2, Pallas kernels, attend(): pl.pallas_call(functools.partial(attend_kernel, contexts, pair, which), o...  5.69 us
    all_to_all x1, starting transfers between devices, split_by_heads(): packed = lax.all_to_all(packed, 'ctx', 0, 0, tiled=True)  3.82 us
    ppermute x1, starting transfers between devices, split_by_heads(): others = lax.ppermute(others, 'groups', [(0, 1), (1, 0)])  1.58 us
    ppermute x7, starting transfers between devices, trade(): return lax.ppermute(array, 'tp', [(0, 1), (1, 0)])  1.53 us
    reshape x1, local copies, waits for them, and re-layouts, split_by_heads(): by_head = kv_weight.reshape(depth, contexts, 2, pair, width)  1.51 us
  transfers between devices with their start and end apart: 19, of which 8 were waited for; matrix products, arithmetic and copies ran while one was open for 7% of the time, Pallas kernels for 5%

profile of v10, /device:TPU:0, one launch (start us, length us, event | category | flops | bytes accessed | tf_op | source)
XLA Modules:
  0.0 61.8 jit_solution(8970115862140711297)
XLA Ops:
  0.0 0.9 %dynamic-slice_bitcast_fusion = bf16[576,128]{1,0:T(8,128)(2,1)S(1)} fusion(bf16[256,576]{0,1:T(8,128)(2,1)} %param.6, s32[]{:T(128)S(6)} %select_n.44), kind=kLoop, calls=%fused_computation.2 | loop fusion | bytes 294916 | tf_op jit(solution)/shard_map/dynamic_slice | solution.py:144
  0.9 4.1 %collective-permute-start = (bf16[576,128]{1,0:T(8,128)(2,1)S(1)}, bf16[576,128]{1,0:T(8,128)(2,1)S(1)}, u32[]{:S(2)}, u32[]{:S(2)}) collective-permute-start(bf16[576,128]{1,0:T(8,128)(2,1)S(1)} %dynamic-slice_bitcast_fusion), channel_id=1, source_target_pairs={{0,8},{2,10},{4,12},{6,14},{8,0},{10,2},{12,4},{14,6},{1,9},{3,11}... | collective-permute-start | bytes 442376 | tf_op jit(solution)/shard_map/ppermute | solution.py:114
  5.0 1.5 %collective-permute-start.1 = (bf16[576,128]{1,0:T(8,128)(2,1)S(1)}, bf16[576,128]{1,0:T(8,128)(2,1)S(1)}, u32[]{:S(2)}, u32[]{:S(2)}) collective-permute-start(bf16[576,128]{1,0:T(8,128)(2,1)S(1)} %dynamic-slice_bitcast_fusion), channel_id=1, source_target_pairs={{0,2},{2,0},{4,6},{6,4},{8,10},{10,8},{12,14},{14,12},{1,3},{3,1},... | collective-permute-start | bytes 442376 | tf_op jit(solution)/shard_map/ppermute | solution.py:114
  6.5 1.6 %collective-permute-start.2 = (bf16[576,128]{1,0:T(8,128)(2,1)S(1)}, bf16[576,128]{1,0:T(8,128)(2,1)S(1)}, u32[]{:S(2)}, u32[]{:S(2)}) collective-permute-start(bf16[576,128]{1,0:T(8,128)(2,1)S(1)} %dynamic-slice_bitcast_fusion), channel_id=1, source_target_pairs={{0,4},{2,6},{4,0},{6,2},{8,12},{10,14},{12,8},{14,10},{1,5},{3,7},... | collective-permute-start | bytes 442376 | tf_op jit(solution)/shard_map/ppermute | solution.py:114
  8.1 1.5 %reshape.48 = bf16[64,8,2,2,256]{4,3,2,1,0:T(2,128)(2,1)S(1)} reshape(bf16[64,32,256]{2,1,0:T(8,128)(2,1)} %param.7) | data formatting | bytes 2097152 | tf_op jit(solution)/shard_map/reshape | solution.py:117
  9.6 0.3 constant_dynamic-slice_fusion.1
  9.9 0.6 collective-permute-start.3
  10.5 0.5 collective-permute-start.4
  11.1 0.1 reshape.50
  11.2 0.2 copy.8
  11.4 0.3 broadcast_select_fusion
  11.7 0.1 slice_bitcast_fusion
  11.8 0.1 slice_bitcast_fusion.1
  11.9 0.4 constant_dynamic-slice_fusion.5
  12.3 0.1 reshape.52
  12.5 0.1 copy.9
  12.6 0.1 reshape.51
  12.7 0.2 copy.6
  12.8 0.9 %pad_maximum_fusion = bf16[8,176,256]{2,1,0:T(8,128)(2,1)} fusion(bf16[8,16,256]{2,1,0:T(8,128)(2,1)S(1)} %reshape.52, bf16[8,32,256]{2,1,0:T(8,128)(2,1)S(1)} %reshape.51, bf16[8,128,256]{2,1,0:T(8,128)(2,1)S(1)} %bitcast.40), kind=kLoop, calls=%fused_computation | loop fusion | flops 2162688 | bytes 1441792 | tf_op jit(solution)/shard_map/concatenate | solution.py:137
  13.7 0.5 collective-permute-done.3.refs_4_
  14.3 0.7 %collective-permute-done.4.refs_5_ = bf16[128,256]{1,0:T(8,128)(2,1)S(1)} collective-permute-done((bf16[128,256]{1,0:T(8,128)(2,1)S(1)}, bf16[128,256]{1,0:T(8,128)(2,1)S(1)}, u32[]{:S(2)}, u32[]{:S(2)}) %collective-permute-start.4) | collective-permute-done | bytes 65568 | tf_op jit(solution)/shard_map/ppermute | solution.py:114
  14.9 0.0 collective-permute-done.refs_10_.refs_16_
  14.9 0.0 collective-permute-done.1.refs_4_.refs_10_
  15.0 0.0 collective-permute-done.2.refs_6_.refs_12_
  15.0 3.8 %all-to-all-start = ((bf16[8,176,256]{2,1,0:T(8,128)(2,1)}), bf16[8,176,256]{2,1,0:T(8,128)(2,1)S(1)}, u32[]{:S(2)}, u32[]{:S(2)}) async-start(bf16[8,176,256]{2,1,0:T(8,128)(2,1)} %pad_maximum_fusion), calls=%async_computation | async-start | bytes 1441792 | tf_op jit(solution)/shard_map/all_to_all | solution.py:149
  18.8 2.0 %collective-permute-start.5 = (bf16[576,128]{1,0:T(8,128)(2,1)S(1)}, bf16[576,128]{1,0:T(8,128)(2,1)S(1)}, u32[]{:S(2)}, u32[]{:S(2)}) collective-permute-start(bf16[576,128]{1,0:T(8,128)(2,1)S(1)} %collective-permute-done.2.refs_6_.refs_12_), channel_id=1, source_target_pairs={{0,2},{2,0},{4,6},{6,4},{8,10},{10,8},{12,14},{14,12},{1,3},{3,1},... | collective-permute-start | bytes 442376 | tf_op jit(solution)/shard_map/ppermute | solution.py:114
  20.8 0.0 collective-permute-start.6
  20.8 2.0 %collective-permute-start.7 = (bf16[576,128]{1,0:T(8,128)(2,1)S(1)}, bf16[576,128]{1,0:T(8,128)(2,1)S(1)}, u32[]{:S(2)}, u32[]{:S(2)}) collective-permute-start(bf16[576,128]{1,0:T(8,128)(2,1)S(1)} %collective-permute-done.refs_10_.refs_16_), channel_id=1, source_target_pairs={{0,4},{2,6},{4,0},{6,2},{8,12},{10,14},{12,8},{14,10},{1,5},{3,7},... | collective-permute-start | bytes 442376 | tf_op jit(solution)/shard_map/ppermute | solution.py:114
  22.8 0.0 collective-permute-start.8
  22.8 0.5 collective-permute-start.9
  23.4 8.9 %collective-permute-done.5.refs_8_.refs_14_ = bf16[576,128]{1,0:T(8,128)(2,1)S(1)} collective-permute-done((bf16[576,128]{1,0:T(8,128)(2,1)S(1)}, bf16[576,128]{1,0:T(8,128)(2,1)S(1)}, u32[]{:S(2)}, u32[]{:S(2)}) %collective-permute-start.5) | collective-permute-done | bytes 147488 | tf_op jit(solution)/shard_map/ppermute | solution.py:114
  32.3 0.0 collective-permute-start.13
  32.3 2.3 %collective-permute-done.6.refs_12_.refs_18_ = bf16[576,128]{1,0:T(8,128)(2,1)S(1)} collective-permute-done((bf16[576,128]{1,0:T(8,128)(2,1)S(1)}, bf16[576,128]{1,0:T(8,128)(2,1)S(1)}, u32[]{:S(2)}, u32[]{:S(2)}) %collective-permute-start.6) | collective-permute-done | bytes 147488 | tf_op jit(solution)/shard_map/ppermute | solution.py:114
  34.6 1.2 %collective-permute-start.16 = (bf16[576,128]{1,0:T(8,128)(2,1)S(1)}, bf16[576,128]{1,0:T(8,128)(2,1)S(1)}, u32[]{:S(2)}, u32[]{:S(2)}) collective-permute-start(bf16[576,128]{1,0:T(8,128)(2,1)S(1)} %collective-permute-done.6.refs_12_.refs_18_), channel_id=1, source_target_pairs={{0,4},{2,6},{4,0},{6,2},{8,12},{10,14},{12,8},{14,10},{1,5},{3,7},... | collective-permute-start | bytes 442376 | tf_op jit(solution)/shard_map/ppermute | solution.py:114
  35.7 0.0 collective-permute-done.9.refs_7_.refs_13_
  35.7 1.5 %all-to-all-done.refs_2_ = bf16[8,176,256]{2,1,0:T(8,128)(2,1)S(1)} async-done(((bf16[8,176,256]{2,1,0:T(8,128)(2,1)}), bf16[8,176,256]{2,1,0:T(8,128)(2,1)S(1)}, u32[]{:S(2)}, u32[]{:S(2)}) %all-to-all-start) | async-done | bytes 720928 | tf_op jit(solution)/shard_map/all_to_all | solution.py:149
  37.2 1.6 %collective-permute-start.11 = (bf16[4,128,256]{2,1,0:T(8,128)(2,1)S(1)}, bf16[4,128,256]{2,1,0:T(8,128)(2,1)S(1)}, u32[]{:S(2)}, u32[]{:S(2)}) collective-permute-start(bf16[4,128,256]{2,1,0:T(8,128)(2,1)S(1)} %constant_dynamic-slice_fusion), channel_id=1, source_target_pairs={{0,16},{16,0},{1,17},{17,1},{2,18},{18,2},{3,19},{19,3},{4,20},{20... | collective-permute-start | bytes 786440 | tf_op jit(solution)/shard_map/ppermute | solution.py:156
  38.8 1.2 %collective-permute-done.16.refs_16_.refs_22_ = bf16[576,128]{1,0:T(8,128)(2,1)S(1)} collective-permute-done((bf16[576,128]{1,0:T(8,128)(2,1)S(1)}, bf16[576,128]{1,0:T(8,128)(2,1)S(1)}, u32[]{:S(2)}, u32[]{:S(2)}) %collective-permute-start.16) | collective-permute-done | bytes 147488 | tf_op jit(solution)/shard_map/ppermute | solution.py:114
  40.0 0.5 collective-permute-start.12
  40.5 0.0 collective-permute-start.14
  40.5 0.5 collective-permute-start.15
  41.0 0.3 collective-permute-done.17.refs_17_.refs_23_
  41.4 1.4 %collective-permute-start.10 = (bf16[128,256]{1,0:T(8,128)(2,1)S(1)}, bf16[128,256]{1,0:T(8,128)(2,1)S(1)}, u32[]{:S(2)}, u32[]{:S(2)}) collective-permute-start(bf16[128,256]{1,0:T(8,128)(2,1)S(1)} %bitcast.43), channel_id=1, source_target_pairs={{0,6},{2,4},{4,2},{6,0},{8,14},{10,12},{12,10},{14,8},{1,7},{3,5},... | collective-permute-start | bytes 196616 | tf_op jit(solution)/shard_map/ppermute | solution.py:114
  43.5 2.8 %attend_first.1.refs_8_ = bf16[128,256]{1,0:T(8,128)(2,1)S(1)} custom-call(s32[8]{0:T(128)S(1)} %copy-done.1, s32[1]{0:T(128)S(6)} %copy.15.refs_1_, bf16[8,176,256]{2,1,0:T(8,128)(2,1)S(1)} %all-to-all-done.refs_2_, bf16[576,256]{1,0:T(8,128)(2,1)S(1)} %bitcast.36, bf16[576,128]{1,0:T(8,128)(2,1)S(1)} %collective-permute-done.1.refs_4_.refs_10_, ...), custom_call_target="tpu_custom_call" | custom-call | flops 1048576 | bytes 1048576 | tf_op jit(solution)/shard_map/attend_first/pallas_call | solution.py:168
  46.3 0.2 collective-permute-done.10.refs_6_
  46.5 2.9 %attend_second.1 = bf16[128,512]{1,0:T(8,128)(2,1)S(1)} custom-call(s32[8]{0:T(128)S(1)} %copy-done.1, s32[1]{0:T(128)S(6)} %copy.15.refs_1_, bf16[8,176,256]{2,1,0:T(8,128)(2,1)S(1)} %all-to-all-done.refs_2_, bf16[128,256]{1,0:T(8,128)(2,1)S(1)} %bitcast.39, bf16[128,256]{1,0:T(8,128)(2,1)S(1)} %collective-permute-done.3.refs_4_, ...), custom_call_target="tpu_custom_call" | custom-call | flops 1048576 | bytes 1048576 | tf_op jit(solution)/shard_map/attend_second/pallas_call | solution.py:168
  49.4 11.6 %all_to_all.10 = bf16[8,16,512]{2,1,0:T(8,128)(2,1)S(1)} all-to-all(bf16[8,16,512]{2,1,0:T(8,128)(2,1)S(1)} %bitcast.38), channel_id=1, replica_groups=mesh['groups'=2,'ctx'=8,'tp'=2] {'ctx'}, dimensions={0} | all-to-all | bytes 262144 | tf_op jit(solution)/shard_map/all_to_all | solution.py:182
  61.1 0.7 %copy.14 = bf16[8,16,4,128]{3,2,0,1:T(4,128)(2,1)} copy(bf16[8,16,4,128]{3,2,1,0:T(4,128)(2,1)S(1)} %reshape.62) | data formatting | bytes 262144 | tf_op jit(solution)/shard_map/reshape | solution.py:183
  (20 shorter events, 0.1 us)
Async XLA Ops:
  0.9 14.0 %collective-permute-start = (bf16[576,128]{1,0:T(8,128)(2,1)S(1)}, bf16[576,128]{1,0:T(8,128)(2,1)S(1)}, u32[]{:S(2)}, u32[]{:S(2)}) collective-permute-start(bf16[576,128]{1,0:T(8,128)(2,1)S(1)} %dynamic-slice_bitcast_fusion), channel_id=1, source_target_pairs={{0,8},{2,10},{4,12},{6,14},{8,0},{10,2},{12,4},{14,6},{1,9},{3,11}... | collective-permute-start | bytes 442376 | tf_op jit(solution)/shard_map/ppermute | solution.py:114
  5.0 9.9 %collective-permute-start.1 = (bf16[576,128]{1,0:T(8,128)(2,1)S(1)}, bf16[576,128]{1,0:T(8,128)(2,1)S(1)}, u32[]{:S(2)}, u32[]{:S(2)}) collective-permute-start(bf16[576,128]{1,0:T(8,128)(2,1)S(1)} %dynamic-slice_bitcast_fusion), channel_id=1, source_target_pairs={{0,2},{2,0},{4,6},{6,4},{8,10},{10,8},{12,14},{14,12},{1,3},{3,1},... | collective-permute-start | bytes 442376 | tf_op jit(solution)/shard_map/ppermute | solution.py:114
  6.5 8.4 %collective-permute-start.2 = (bf16[576,128]{1,0:T(8,128)(2,1)S(1)}, bf16[576,128]{1,0:T(8,128)(2,1)S(1)}, u32[]{:S(2)}, u32[]{:S(2)}) collective-permute-start(bf16[576,128]{1,0:T(8,128)(2,1)S(1)} %dynamic-slice_bitcast_fusion), channel_id=1, source_target_pairs={{0,4},{2,6},{4,0},{6,2},{8,12},{10,14},{12,8},{14,10},{1,5},{3,7},... | collective-permute-start | bytes 442376 | tf_op jit(solution)/shard_map/ppermute | solution.py:114
  8.1 3.0 %copy-start.2 = (bf16[16,32,192]{2,1,0:T(8,128)(2,1)S(1)}, bf16[16,32,192]{2,1,0:T(8,128)(2,1)}, u32[]{:S(2)}) copy-start(bf16[16,32,192]{2,1,0:T(8,128)(2,1)} %param.5) | copy-start | bytes 589828
  9.9 4.3 %collective-permute-start.3 = (bf16[128,256]{1,0:T(8,128)(2,1)S(1)}, bf16[128,256]{1,0:T(8,128)(2,1)S(1)}, u32[]{:S(2)}, u32[]{:S(2)}) collective-permute-start(bf16[128,256]{1,0:T(8,128)(2,1)S(1)} %bitcast.41), channel_id=1, source_target_pairs={{0,2},{2,0},{4,6},{6,4},{8,10},{10,8},{12,14},{14,12},{1,3},{3,1},... | collective-permute-start | bytes 196616 | tf_op jit(solution)/shard_map/ppermute | solution.py:114
  10.5 4.4 %collective-permute-start.4 = (bf16[128,256]{1,0:T(8,128)(2,1)S(1)}, bf16[128,256]{1,0:T(8,128)(2,1)S(1)}, u32[]{:S(2)}, u32[]{:S(2)}) collective-permute-start(bf16[128,256]{1,0:T(8,128)(2,1)S(1)} %bitcast.42), channel_id=1, source_target_pairs={{0,4},{2,6},{4,0},{6,2},{8,12},{10,14},{12,8},{14,10},{1,5},{3,7},... | collective-permute-start | bytes 196616 | tf_op jit(solution)/shard_map/ppermute | solution.py:114
  13.7 29.7 %copy-start = (bf16[256,576]{0,1:T(8,128)(2,1)S(1)}, bf16[256,576]{0,1:T(8,128)(2,1)}, u32[]{:S(2)}) copy-start(bf16[256,576]{0,1:T(8,128)(2,1)} %param.6) | copy-start | bytes 884740
  13.7 29.7 %copy-start.1 = (s32[8]{0:T(128)S(1)}, s32[8]{0:T(128)}, u32[]{:S(2)}) copy-start(s32[8]{0:T(128)} %refs_0_.3) | copy-start | bytes 100
  15.0 22.3 %all-to-all-start = ((bf16[8,176,256]{2,1,0:T(8,128)(2,1)}), bf16[8,176,256]{2,1,0:T(8,128)(2,1)S(1)}, u32[]{:S(2)}, u32[]{:S(2)}) async-start(bf16[8,176,256]{2,1,0:T(8,128)(2,1)} %pad_maximum_fusion), calls=%async_computation | async-start | bytes 1441792 | tf_op jit(solution)/shard_map/all_to_all | solution.py:149
  18.8 13.5 %collective-permute-start.5 = (bf16[576,128]{1,0:T(8,128)(2,1)S(1)}, bf16[576,128]{1,0:T(8,128)(2,1)S(1)}, u32[]{:S(2)}, u32[]{:S(2)}) collective-permute-start(bf16[576,128]{1,0:T(8,128)(2,1)S(1)} %collective-permute-done.2.refs_6_.refs_12_), channel_id=1, source_target_pairs={{0,2},{2,0},{4,6},{6,4},{8,10},{10,8},{12,14},{14,12},{1,3},{3,1},... | collective-permute-start | bytes 442376 | tf_op jit(solution)/shard_map/ppermute | solution.py:114
  20.8 13.8 %collective-permute-start.6 = (bf16[576,128]{1,0:T(8,128)(2,1)S(1)}, bf16[576,128]{1,0:T(8,128)(2,1)S(1)}, u32[]{:S(2)}, u32[]{:S(2)}) collective-permute-start(bf16[576,128]{1,0:T(8,128)(2,1)S(1)} %collective-permute-done.refs_10_.refs_16_), channel_id=1, source_target_pairs={{0,2},{2,0},{4,6},{6,4},{8,10},{10,8},{12,14},{14,12},{1,3},{3,1},... | collective-permute-start | bytes 442376 | tf_op jit(solution)/shard_map/ppermute | solution.py:114
  20.8 14.9 %collective-permute-start.7 = (bf16[576,128]{1,0:T(8,128)(2,1)S(1)}, bf16[576,128]{1,0:T(8,128)(2,1)S(1)}, u32[]{:S(2)}, u32[]{:S(2)}) collective-permute-start(bf16[576,128]{1,0:T(8,128)(2,1)S(1)} %collective-permute-done.refs_10_.refs_16_), channel_id=1, source_target_pairs={{0,4},{2,6},{4,0},{6,2},{8,12},{10,14},{12,8},{14,10},{1,5},{3,7},... | collective-permute-start | bytes 442376 | tf_op jit(solution)/shard_map/ppermute | solution.py:114
  22.8 12.9 %collective-permute-start.8 = (bf16[576,128]{1,0:T(8,128)(2,1)S(1)}, bf16[576,128]{1,0:T(8,128)(2,1)S(1)}, u32[]{:S(2)}, u32[]{:S(2)}) collective-permute-start(bf16[576,128]{1,0:T(8,128)(2,1)S(1)} %collective-permute-done.1.refs_4_.refs_10_), channel_id=1, source_target_pairs={{0,1},{1,0},{2,3},{3,2},{4,5},{5,4},{6,7},{7,6},{8,9},{9,8},{10,11... | collective-permute-start | bytes 442376 | tf_op jit(solution)/shard_map/ppermute | solution.py:140
  22.8 12.9 %collective-permute-start.9 = (bf16[576,128]{1,0:T(8,128)(2,1)S(1)}, bf16[576,128]{1,0:T(8,128)(2,1)S(1)}, u32[]{:S(2)}, u32[]{:S(2)}) collective-permute-start(bf16[576,128]{1,0:T(8,128)(2,1)S(1)} %collective-permute-done.2.refs_6_.refs_12_), channel_id=1, source_target_pairs={{0,1},{1,0},{2,3},{3,2},{4,5},{5,4},{6,7},{7,6},{8,9},{9,8},{10,11... | collective-permute-start | bytes 442376 | tf_op jit(solution)/shard_map/ppermute | solution.py:140
  32.3 8.2 %collective-permute-start.13 = (bf16[576,128]{1,0:T(8,128)(2,1)S(1)}, bf16[576,128]{1,0:T(8,128)(2,1)S(1)}, u32[]{:S(2)}, u32[]{:S(2)}) collective-permute-start(bf16[576,128]{1,0:T(8,128)(2,1)S(1)} %collective-permute-done.refs_10_.refs_16_), channel_id=1, source_target_pairs={{0,1},{1,0},{2,3},{3,2},{4,5},{5,4},{6,7},{7,6},{8,9},{9,8},{10,11... | collective-permute-start | bytes 442376 | tf_op jit(solution)/shard_map/ppermute | solution.py:140
  34.6 5.4 %collective-permute-start.16 = (bf16[576,128]{1,0:T(8,128)(2,1)S(1)}, bf16[576,128]{1,0:T(8,128)(2,1)S(1)}, u32[]{:S(2)}, u32[]{:S(2)}) collective-permute-start(bf16[576,128]{1,0:T(8,128)(2,1)S(1)} %collective-permute-done.6.refs_12_.refs_18_), channel_id=1, source_target_pairs={{0,4},{2,6},{4,0},{6,2},{8,12},{10,14},{12,8},{14,10},{1,5},{3,7},... | collective-permute-start | bytes 442376 | tf_op jit(solution)/shard_map/ppermute | solution.py:114
  37.2 9.3 %collective-permute-start.11 = (bf16[4,128,256]{2,1,0:T(8,128)(2,1)S(1)}, bf16[4,128,256]{2,1,0:T(8,128)(2,1)S(1)}, u32[]{:S(2)}, u32[]{:S(2)}) collective-permute-start(bf16[4,128,256]{2,1,0:T(8,128)(2,1)S(1)} %constant_dynamic-slice_fusion), channel_id=1, source_target_pairs={{0,16},{16,0},{1,17},{17,1},{2,18},{18,2},{3,19},{19,3},{4,20},{20... | collective-permute-start | bytes 786440 | tf_op jit(solution)/shard_map/ppermute | solution.py:156
  40.0 1.4 %collective-permute-start.17 = (bf16[576,128]{1,0:T(8,128)(2,1)S(1)}, bf16[576,128]{1,0:T(8,128)(2,1)S(1)}, u32[]{:S(2)}, u32[]{:S(2)}) collective-permute-start(bf16[576,128]{1,0:T(8,128)(2,1)S(1)} %collective-permute-done.16.refs_16_.refs_22_), channel_id=1, source_target_pairs={{0,1},{1,0},{2,3},{3,2},{4,5},{5,4},{6,7},{7,6},{8,9},{9,8},{10,11... | collective-permute-start | bytes 442376 | tf_op jit(solution)/shard_map/ppermute | solution.py:140
  40.0 3.5 %collective-permute-start.12 = (bf16[576,128]{1,0:T(8,128)(2,1)S(1)}, bf16[576,128]{1,0:T(8,128)(2,1)S(1)}, u32[]{:S(2)}, u32[]{:S(2)}) collective-permute-start(bf16[576,128]{1,0:T(8,128)(2,1)S(1)} %collective-permute-done.5.refs_8_.refs_14_), channel_id=1, source_target_pairs={{0,1},{1,0},{2,3},{3,2},{4,5},{5,4},{6,7},{7,6},{8,9},{9,8},{10,11... | collective-permute-start | bytes 442376 | tf_op jit(solution)/shard_map/ppermute | solution.py:140
  40.5 3.0 %collective-permute-start.14 = (bf16[576,128]{1,0:T(8,128)(2,1)S(1)}, bf16[576,128]{1,0:T(8,128)(2,1)S(1)}, u32[]{:S(2)}, u32[]{:S(2)}) collective-permute-start(bf16[576,128]{1,0:T(8,128)(2,1)S(1)} %collective-permute-done.6.refs_12_.refs_18_), channel_id=1, source_target_pairs={{0,1},{1,0},{2,3},{3,2},{4,5},{5,4},{6,7},{7,6},{8,9},{9,8},{10,11... | collective-permute-start | bytes 442376 | tf_op jit(solution)/shard_map/ppermute | solution.py:140
  40.5 3.0 %collective-permute-start.15 = (bf16[576,128]{1,0:T(8,128)(2,1)S(1)}, bf16[576,128]{1,0:T(8,128)(2,1)S(1)}, u32[]{:S(2)}, u32[]{:S(2)}) collective-permute-start(bf16[576,128]{1,0:T(8,128)(2,1)S(1)} %collective-permute-done.7.refs_14_.refs_20_), channel_id=1, source_target_pairs={{0,1},{1,0},{2,3},{3,2},{4,5},{5,4},{6,7},{7,6},{8,9},{9,8},{10,11... | collective-permute-start | bytes 442376 | tf_op jit(solution)/shard_map/ppermute | solution.py:140
  41.4 5.2 %collective-permute-start.10 = (bf16[128,256]{1,0:T(8,128)(2,1)S(1)}, bf16[128,256]{1,0:T(8,128)(2,1)S(1)}, u32[]{:S(2)}, u32[]{:S(2)}) collective-permute-start(bf16[128,256]{1,0:T(8,128)(2,1)S(1)} %bitcast.43), channel_id=1, source_target_pairs={{0,6},{2,4},{4,2},{6,0},{8,14},{10,12},{12,10},{14,8},{1,7},{3,5},... | collective-permute-start | bytes 196616 | tf_op jit(solution)/shard_map/ppermute | solution.py:114

commit v11 on v10

--- a/solution.py
+++ b/solution.py
@@ -149,7 +149,7 @@
     packed = lax.all_to_all(packed, "ctx", 0, 0, tiled=True)
     for slot, source, bit in LATE:
         held[slot] = swap(held[source], bit)
-    traded = {slot: trade(held[slot]) for slot in (1, 2)}
+    traded = {slot: trade(held[slot]) for slot in (1, 2, 3)}
     waited = lax.optimization_barrier((packed, kept, held[3], held[5], held[6], traded))
     packed, kept, held[3], held[5], held[6], traded = waited
     others = lax.dynamic_slice_in_dim(packed, (me // near ^ 1) * near, near, 0)[:, :pair * depth]

time: 62.1 us -> 61.5 us (level)
  transfers between devices with their start and end apart: 19 -> 19, of which waited for: 8 -> 7; matrix products, arithmetic and copies ran while one was open for 7% -> 7% of each run, Pallas kernels for 5% -> 5%
where the time goes in v11:
time: 61.5 us; the launch traced here: 61.3 us
  starting transfers between devices  21.4 us (35%)
  waiting for transfers between devices  15.6 us (25%)
  blocking collectives  11.6 us (19%)
  Pallas kernels  5.69 us (9%)
  local copies, waits for them, and re-layouts  4.92 us (8%)
  other arithmetic  1.19 us (2%)
  between operations  0.88 us (1%)
    ppermute x10, starting transfers between devices, swap(): return lax.ppermute(array, 'ctx', [(i, i ^ bit) for i in range(contexts)])  15 us
    ppermute x10, waiting for transfers between devices, swap(): return lax.ppermute(array, 'ctx', [(i, i ^ bit) for i in range(contexts)])  14.1 us
    all_to_all x1, blocking collectives, split_by_heads(): attended = lax.all_to_all(attended, 'ctx', 0, 0, tiled=True)  11.6 us
    pallas_call x2, Pallas kernels, attend(): pl.pallas_call(functools.partial(attend_kernel, contexts, pair, which), o...  5.69 us
    all_to_all x1, starting transfers between devices, split_by_heads(): packed = lax.all_to_all(packed, 'ctx', 0, 0, tiled=True)  3.82 us
    ppermute x1, starting transfers between devices, split_by_heads(): others = lax.ppermute(others, 'groups', [(0, 1), (1, 0)])  1.58 us
    reshape x1, local copies, waits for them, and re-layouts, split_by_heads(): by_head = kv_weight.reshape(depth, contexts, 2, pair, width)  1.51 us
    all_to_all x1, waiting for transfers between devices, split_by_heads(): packed = lax.all_to_all(packed, 'ctx', 0, 0, tiled=True)  1.47 us
  transfers between devices with their start and end apart: 19, of which 7 were waited for; matrix products, arithmetic and copies ran while one was open for 7% of the time, Pallas kernels for 5%

profile of v11, /device:TPU:0, one launch (start us, length us, event | category | flops | bytes accessed | tf_op | source)
XLA Modules:
  0.0 61.3 jit_solution(10238415651597414903)
XLA Ops:
  0.0 0.9 %dynamic-slice_bitcast_fusion = bf16[576,128]{1,0:T(8,128)(2,1)S(1)} fusion(bf16[256,576]{0,1:T(8,128)(2,1)} %param.6, s32[]{:T(128)S(6)} %select_n.44), kind=kLoop, calls=%fused_computation.2 | loop fusion | bytes 294916 | tf_op jit(solution)/shard_map/dynamic_slice | solution.py:144
  0.9 4.1 %collective-permute-start = (bf16[576,128]{1,0:T(8,128)(2,1)S(1)}, bf16[576,128]{1,0:T(8,128)(2,1)S(1)}, u32[]{:S(2)}, u32[]{:S(2)}) collective-permute-start(bf16[576,128]{1,0:T(8,128)(2,1)S(1)} %dynamic-slice_bitcast_fusion), channel_id=1, source_target_pairs={{0,8},{2,10},{4,12},{6,14},{8,0},{10,2},{12,4},{14,6},{1,9},{3,11}... | collective-permute-start | bytes 442376 | tf_op jit(solution)/shard_map/ppermute | solution.py:114
  5.0 1.5 %collective-permute-start.1 = (bf16[576,128]{1,0:T(8,128)(2,1)S(1)}, bf16[576,128]{1,0:T(8,128)(2,1)S(1)}, u32[]{:S(2)}, u32[]{:S(2)}) collective-permute-start(bf16[576,128]{1,0:T(8,128)(2,1)S(1)} %dynamic-slice_bitcast_fusion), channel_id=1, source_target_pairs={{0,2},{2,0},{4,6},{6,4},{8,10},{10,8},{12,14},{14,12},{1,3},{3,1},... | collective-permute-start | bytes 442376 | tf_op jit(solution)/shard_map/ppermute | solution.py:114
  6.5 1.6 %collective-permute-start.2 = (bf16[576,128]{1,0:T(8,128)(2,1)S(1)}, bf16[576,128]{1,0:T(8,128)(2,1)S(1)}, u32[]{:S(2)}, u32[]{:S(2)}) collective-permute-start(bf16[576,128]{1,0:T(8,128)(2,1)S(1)} %dynamic-slice_bitcast_fusion), channel_id=1, source_target_pairs={{0,4},{2,6},{4,0},{6,2},{8,12},{10,14},{12,8},{14,10},{1,5},{3,7},... | collective-permute-start | bytes 442376 | tf_op jit(solution)/shard_map/ppermute | solution.py:114
  8.1 1.5 %reshape.48 = bf16[64,8,2,2,256]{4,3,2,1,0:T(2,128)(2,1)S(1)} reshape(bf16[64,32,256]{2,1,0:T(8,128)(2,1)} %param.7) | data formatting | bytes 2097152 | tf_op jit(solution)/shard_map/reshape | solution.py:117
  9.6 0.3 constant_dynamic-slice_fusion.1
  9.9 0.6 collective-permute-start.3
  10.5 0.5 collective-permute-start.4
  11.1 0.1 reshape.50
  11.2 0.2 copy.8
  11.4 0.3 broadcast_select_fusion
  11.7 0.1 slice_bitcast_fusion
  11.8 0.1 slice_bitcast_fusion.1
  11.9 0.4 constant_dynamic-slice_fusion.5
  12.3 0.1 reshape.52
  12.5 0.1 copy.9
  12.6 0.1 reshape.51
  12.7 0.2 copy.6
  12.8 0.9 %pad_maximum_fusion = bf16[8,176,256]{2,1,0:T(8,128)(2,1)} fusion(bf16[8,16,256]{2,1,0:T(8,128)(2,1)S(1)} %reshape.52, bf16[8,32,256]{2,1,0:T(8,128)(2,1)S(1)} %reshape.51, bf16[8,128,256]{2,1,0:T(8,128)(2,1)S(1)} %bitcast.40), kind=kLoop, calls=%fused_computation | loop fusion | flops 2162688 | bytes 1441792 | tf_op jit(solution)/shard_map/concatenate | solution.py:137
  13.7 0.5 collective-permute-done.3.refs_4_
  14.3 0.7 %collective-permute-done.4.refs_5_ = bf16[128,256]{1,0:T(8,128)(2,1)S(1)} collective-permute-done((bf16[128,256]{1,0:T(8,128)(2,1)S(1)}, bf16[128,256]{1,0:T(8,128)(2,1)S(1)}, u32[]{:S(2)}, u32[]{:S(2)}) %collective-permute-start.4) | collective-permute-done | bytes 65568 | tf_op jit(solution)/shard_map/ppermute | solution.py:114
  14.9 0.0 collective-permute-done.refs_10_.refs_16_
  14.9 0.0 collective-permute-done.1.refs_4_.refs_10_
  15.0 0.0 collective-permute-done.2.refs_6_.refs_12_
  15.0 3.8 %all-to-all-start = ((bf16[8,176,256]{2,1,0:T(8,128)(2,1)}), bf16[8,176,256]{2,1,0:T(8,128)(2,1)S(1)}, u32[]{:S(2)}, u32[]{:S(2)}) async-start(bf16[8,176,256]{2,1,0:T(8,128)(2,1)} %pad_maximum_fusion), calls=%async_computation | async-start | bytes 1441792 | tf_op jit(solution)/shard_map/all_to_all | solution.py:149
  18.8 2.0 %collective-permute-start.5 = (bf16[576,128]{1,0:T(8,128)(2,1)S(1)}, bf16[576,128]{1,0:T(8,128)(2,1)S(1)}, u32[]{:S(2)}, u32[]{:S(2)}) collective-permute-start(bf16[576,128]{1,0:T(8,128)(2,1)S(1)} %collective-permute-done.2.refs_6_.refs_12_), channel_id=1, source_target_pairs={{0,2},{2,0},{4,6},{6,4},{8,10},{10,8},{12,14},{14,12},{1,3},{3,1},... | collective-permute-start | bytes 442376 | tf_op jit(solution)/shard_map/ppermute | solution.py:114
  20.8 0.0 collective-permute-start.6
  20.8 2.0 %collective-permute-start.7 = (bf16[576,128]{1,0:T(8,128)(2,1)S(1)}, bf16[576,128]{1,0:T(8,128)(2,1)S(1)}, u32[]{:S(2)}, u32[]{:S(2)}) collective-permute-start(bf16[576,128]{1,0:T(8,128)(2,1)S(1)} %collective-permute-done.refs_10_.refs_16_), channel_id=1, source_target_pairs={{0,4},{2,6},{4,0},{6,2},{8,12},{10,14},{12,8},{14,10},{1,5},{3,7},... | collective-permute-start | bytes 442376 | tf_op jit(solution)/shard_map/ppermute | solution.py:114
  22.8 0.0 collective-permute-start.9
  22.8 0.5 collective-permute-start.8
  23.3 8.9 %collective-permute-done.5.refs_8_.refs_14_ = bf16[576,128]{1,0:T(8,128)(2,1)S(1)} collective-permute-done((bf16[576,128]{1,0:T(8,128)(2,1)S(1)}, bf16[576,128]{1,0:T(8,128)(2,1)S(1)}, u32[]{:S(2)}, u32[]{:S(2)}) %collective-permute-start.5) | collective-permute-done | bytes 147488 | tf_op jit(solution)/shard_map/ppermute | solution.py:114
  32.3 0.0 collective-permute-start.10
  32.3 2.3 %collective-permute-done.6.refs_12_.refs_18_ = bf16[576,128]{1,0:T(8,128)(2,1)S(1)} collective-permute-done((bf16[576,128]{1,0:T(8,128)(2,1)S(1)}, bf16[576,128]{1,0:T(8,128)(2,1)S(1)}, u32[]{:S(2)}, u32[]{:S(2)}) %collective-permute-start.6) | collective-permute-done | bytes 147488 | tf_op jit(solution)/shard_map/ppermute | solution.py:114
  34.6 1.2 %collective-permute-start.16 = (bf16[576,128]{1,0:T(8,128)(2,1)S(1)}, bf16[576,128]{1,0:T(8,128)(2,1)S(1)}, u32[]{:S(2)}, u32[]{:S(2)}) collective-permute-start(bf16[576,128]{1,0:T(8,128)(2,1)S(1)} %collective-permute-done.6.refs_12_.refs_18_), channel_id=1, source_target_pairs={{0,4},{2,6},{4,0},{6,2},{8,12},{10,14},{12,8},{14,10},{1,5},{3,7},... | collective-permute-start | bytes 442376 | tf_op jit(solution)/shard_map/ppermute | solution.py:114
  35.7 0.0 collective-permute-done.9.refs_7_.refs_13_
  35.7 0.0 collective-permute-done.10.refs_9_.refs_15_
  35.8 1.5 %all-to-all-done.refs_2_ = bf16[8,176,256]{2,1,0:T(8,128)(2,1)S(1)} async-done(((bf16[8,176,256]{2,1,0:T(8,128)(2,1)}), bf16[8,176,256]{2,1,0:T(8,128)(2,1)S(1)}, u32[]{:S(2)}, u32[]{:S(2)}) %all-to-all-start) | async-done | bytes 720928 | tf_op jit(solution)/shard_map/all_to_all | solution.py:149
  37.2 1.6 %collective-permute-start.12 = (bf16[4,128,256]{2,1,0:T(8,128)(2,1)S(1)}, bf16[4,128,256]{2,1,0:T(8,128)(2,1)S(1)}, u32[]{:S(2)}, u32[]{:S(2)}) collective-permute-start(bf16[4,128,256]{2,1,0:T(8,128)(2,1)S(1)} %constant_dynamic-slice_fusion), channel_id=1, source_target_pairs={{0,16},{16,0},{1,17},{17,1},{2,18},{18,2},{3,19},{19,3},{4,20},{20... | collective-permute-start | bytes 786440 | tf_op jit(solution)/shard_map/ppermute | solution.py:156
  38.8 0.0 collective-permute-start.13
  38.8 1.2 %collective-permute-done.16.refs_16_.refs_22_ = bf16[576,128]{1,0:T(8,128)(2,1)S(1)} collective-permute-done((bf16[576,128]{1,0:T(8,128)(2,1)S(1)}, bf16[576,128]{1,0:T(8,128)(2,1)S(1)}, u32[]{:S(2)}, u32[]{:S(2)}) %collective-permute-start.16) | collective-permute-done | bytes 147488 | tf_op jit(solution)/shard_map/ppermute | solution.py:114
  40.0 0.5 collective-permute-start.14
  40.5 0.0 collective-permute-start.15
  40.6 1.4 %collective-permute-start.11 = (bf16[128,256]{1,0:T(8,128)(2,1)S(1)}, bf16[128,256]{1,0:T(8,128)(2,1)S(1)}, u32[]{:S(2)}, u32[]{:S(2)}) collective-permute-start(bf16[128,256]{1,0:T(8,128)(2,1)S(1)} %bitcast.43), channel_id=1, source_target_pairs={{0,6},{2,4},{4,2},{6,0},{8,14},{10,12},{12,10},{14,8},{1,7},{3,5},... | collective-permute-start | bytes 196616 | tf_op jit(solution)/shard_map/ppermute | solution.py:114
  42.7 2.8 %attend_first.1.refs_8_ = bf16[128,256]{1,0:T(8,128)(2,1)S(1)} custom-call(s32[8]{0:T(128)S(1)} %copy-done.1, s32[1]{0:T(128)S(6)} %copy.15.refs_1_, bf16[8,176,256]{2,1,0:T(8,128)(2,1)S(1)} %all-to-all-done.refs_2_, bf16[576,256]{1,0:T(8,128)(2,1)S(1)} %bitcast.36, bf16[576,128]{1,0:T(8,128)(2,1)S(1)} %collective-permute-done.1.refs_4_.refs_10_, ...), custom_call_target="tpu_custom_call" | custom-call | flops 1048576 | bytes 1048576 | tf_op jit(solution)/shard_map/attend_first/pallas_call | solution.py:168
  45.5 0.5 collective-permute-done.11.refs_6_
  46.0 2.9 %attend_second.1 = bf16[128,512]{1,0:T(8,128)(2,1)S(1)} custom-call(s32[8]{0:T(128)S(1)} %copy-done.1, s32[1]{0:T(128)S(6)} %copy.15.refs_1_, bf16[8,176,256]{2,1,0:T(8,128)(2,1)S(1)} %all-to-all-done.refs_2_, bf16[128,256]{1,0:T(8,128)(2,1)S(1)} %bitcast.39, bf16[128,256]{1,0:T(8,128)(2,1)S(1)} %collective-permute-done.3.refs_4_, ...), custom_call_target="tpu_custom_call" | custom-call | flops 1048576 | bytes 1048576 | tf_op jit(solution)/shard_map/attend_second/pallas_call | solution.py:168
  48.9 11.6 %all_to_all.10 = bf16[8,16,512]{2,1,0:T(8,128)(2,1)S(1)} all-to-all(bf16[8,16,512]{2,1,0:T(8,128)(2,1)S(1)} %bitcast.38), channel_id=1, replica_groups=mesh['groups'=2,'ctx'=8,'tp'=2] {'ctx'}, dimensions={0} | all-to-all | bytes 262144 | tf_op jit(solution)/shard_map/all_to_all | solution.py:182
  60.6 0.7 %copy.14 = bf16[8,16,4,128]{3,2,0,1:T(4,128)(2,1)} copy(bf16[8,16,4,128]{3,2,1,0:T(4,128)(2,1)S(1)} %reshape.62) | data formatting | bytes 262144 | tf_op jit(solution)/shard_map/reshape | solution.py:183
  (20 shorter events, 0.1 us)
Async XLA Ops:
  0.9 14.0 %collective-permute-start = (bf16[576,128]{1,0:T(8,128)(2,1)S(1)}, bf16[576,128]{1,0:T(8,128)(2,1)S(1)}, u32[]{:S(2)}, u32[]{:S(2)}) collective-permute-start(bf16[576,128]{1,0:T(8,128)(2,1)S(1)} %dynamic-slice_bitcast_fusion), channel_id=1, source_target_pairs={{0,8},{2,10},{4,12},{6,14},{8,0},{10,2},{12,4},{14,6},{1,9},{3,11}... | collective-permute-start | bytes 442376 | tf_op jit(solution)/shard_map/ppermute | solution.py:114
  5.0 9.9 %collective-permute-start.1 = (bf16[576,128]{1,0:T(8,128)(2,1)S(1)}, bf16[576,128]{1,0:T(8,128)(2,1)S(1)}, u32[]{:S(2)}, u32[]{:S(2)}) collective-permute-start(bf16[576,128]{1,0:T(8,128)(2,1)S(1)} %dynamic-slice_bitcast_fusion), channel_id=1, source_target_pairs={{0,2},{2,0},{4,6},{6,4},{8,10},{10,8},{12,14},{14,12},{1,3},{3,1},... | collective-permute-start | bytes 442376 | tf_op jit(solution)/shard_map/ppermute | solution.py:114
  6.5 8.4 %collective-permute-start.2 = (bf16[576,128]{1,0:T(8,128)(2,1)S(1)}, bf16[576,128]{1,0:T(8,128)(2,1)S(1)}, u32[]{:S(2)}, u32[]{:S(2)}) collective-permute-start(bf16[576,128]{1,0:T(8,128)(2,1)S(1)} %dynamic-slice_bitcast_fusion), channel_id=1, source_target_pairs={{0,4},{2,6},{4,0},{6,2},{8,12},{10,14},{12,8},{14,10},{1,5},{3,7},... | collective-permute-start | bytes 442376 | tf_op jit(solution)/shard_map/ppermute | solution.py:114
  8.1 3.0 %copy-start.2 = (bf16[16,32,192]{2,1,0:T(8,128)(2,1)S(1)}, bf16[16,32,192]{2,1,0:T(8,128)(2,1)}, u32[]{:S(2)}) copy-start(bf16[16,32,192]{2,1,0:T(8,128)(2,1)} %param.5) | copy-start | bytes 589828
  9.9 4.3 %collective-permute-start.3 = (bf16[128,256]{1,0:T(8,128)(2,1)S(1)}, bf16[128,256]{1,0:T(8,128)(2,1)S(1)}, u32[]{:S(2)}, u32[]{:S(2)}) collective-permute-start(bf16[128,256]{1,0:T(8,128)(2,1)S(1)} %bitcast.41), channel_id=1, source_target_pairs={{0,2},{2,0},{4,6},{6,4},{8,10},{10,8},{12,14},{14,12},{1,3},{3,1},... | collective-permute-start | bytes 196616 | tf_op jit(solution)/shard_map/ppermute | solution.py:114
  10.5 4.4 %collective-permute-start.4 = (bf16[128,256]{1,0:T(8,128)(2,1)S(1)}, bf16[128,256]{1,0:T(8,128)(2,1)S(1)}, u32[]{:S(2)}, u32[]{:S(2)}) collective-permute-start(bf16[128,256]{1,0:T(8,128)(2,1)S(1)} %bitcast.42), channel_id=1, source_target_pairs={{0,4},{2,6},{4,0},{6,2},{8,12},{10,14},{12,8},{14,10},{1,5},{3,7},... | collective-permute-start | bytes 196616 | tf_op jit(solution)/shard_map/ppermute | solution.py:114
  13.7 29.0 %copy-start = (bf16[256,576]{0,1:T(8,128)(2,1)S(1)}, bf16[256,576]{0,1:T(8,128)(2,1)}, u32[]{:S(2)}) copy-start(bf16[256,576]{0,1:T(8,128)(2,1)} %param.6) | copy-start | bytes 884740
  13.7 29.0 %copy-start.1 = (s32[8]{0:T(128)S(1)}, s32[8]{0:T(128)}, u32[]{:S(2)}) copy-start(s32[8]{0:T(128)} %refs_0_.3) | copy-start | bytes 100
  15.0 22.3 %all-to-all-start = ((bf16[8,176,256]{2,1,0:T(8,128)(2,1)}), bf16[8,176,256]{2,1,0:T(8,128)(2,1)S(1)}, u32[]{:S(2)}, u32[]{:S(2)}) async-start(bf16[8,176,256]{2,1,0:T(8,128)(2,1)} %pad_maximum_fusion), calls=%async_computation | async-start | bytes 1441792 | tf_op jit(solution)/shard_map/all_to_all | solution.py:149
  18.8 13.5 %collective-permute-start.5 = (bf16[576,128]{1,0:T(8,128)(2,1)S(1)}, bf16[576,128]{1,0:T(8,128)(2,1)S(1)}, u32[]{:S(2)}, u32[]{:S(2)}) collective-permute-start(bf16[576,128]{1,0:T(8,128)(2,1)S(1)} %collective-permute-done.2.refs_6_.refs_12_), channel_id=1, source_target_pairs={{0,2},{2,0},{4,6},{6,4},{8,10},{10,8},{12,14},{14,12},{1,3},{3,1},... | collective-permute-start | bytes 442376 | tf_op jit(solution)/shard_map/ppermute | solution.py:114
  20.8 13.8 %collective-permute-start.6 = (bf16[576,128]{1,0:T(8,128)(2,1)S(1)}, bf16[576,128]{1,0:T(8,128)(2,1)S(1)}, u32[]{:S(2)}, u32[]{:S(2)}) collective-permute-start(bf16[576,128]{1,0:T(8,128)(2,1)S(1)} %collective-permute-done.refs_10_.refs_16_), channel_id=1, source_target_pairs={{0,2},{2,0},{4,6},{6,4},{8,10},{10,8},{12,14},{14,12},{1,3},{3,1},... | collective-permute-start | bytes 442376 | tf_op jit(solution)/shard_map/ppermute | solution.py:114
  20.8 14.9 %collective-permute-start.7 = (bf16[576,128]{1,0:T(8,128)(2,1)S(1)}, bf16[576,128]{1,0:T(8,128)(2,1)S(1)}, u32[]{:S(2)}, u32[]{:S(2)}) collective-permute-start(bf16[576,128]{1,0:T(8,128)(2,1)S(1)} %collective-permute-done.refs_10_.refs_16_), channel_id=1, source_target_pairs={{0,4},{2,6},{4,0},{6,2},{8,12},{10,14},{12,8},{14,10},{1,5},{3,7},... | collective-permute-start | bytes 442376 | tf_op jit(solution)/shard_map/ppermute | solution.py:114
  22.8 12.9 %collective-permute-start.9 = (bf16[576,128]{1,0:T(8,128)(2,1)S(1)}, bf16[576,128]{1,0:T(8,128)(2,1)S(1)}, u32[]{:S(2)}, u32[]{:S(2)}) collective-permute-start(bf16[576,128]{1,0:T(8,128)(2,1)S(1)} %collective-permute-done.2.refs_6_.refs_12_), channel_id=1, source_target_pairs={{0,1},{1,0},{2,3},{3,2},{4,5},{5,4},{6,7},{7,6},{8,9},{9,8},{10,11... | collective-permute-start | bytes 442376 | tf_op jit(solution)/shard_map/ppermute | solution.py:140
  22.8 12.9 %collective-permute-start.8 = (bf16[576,128]{1,0:T(8,128)(2,1)S(1)}, bf16[576,128]{1,0:T(8,128)(2,1)S(1)}, u32[]{:S(2)}, u32[]{:S(2)}) collective-permute-start(bf16[576,128]{1,0:T(8,128)(2,1)S(1)} %collective-permute-done.1.refs_4_.refs_10_), channel_id=1, source_target_pairs={{0,1},{1,0},{2,3},{3,2},{4,5},{5,4},{6,7},{7,6},{8,9},{9,8},{10,11... | collective-permute-start | bytes 442376 | tf_op jit(solution)/shard_map/ppermute | solution.py:140
  32.3 3.5 %collective-permute-start.10 = (bf16[576,128]{1,0:T(8,128)(2,1)S(1)}, bf16[576,128]{1,0:T(8,128)(2,1)S(1)}, u32[]{:S(2)}, u32[]{:S(2)}) collective-permute-start(bf16[576,128]{1,0:T(8,128)(2,1)S(1)} %collective-permute-done.5.refs_8_.refs_14_), channel_id=1, source_target_pairs={{0,1},{1,0},{2,3},{3,2},{4,5},{5,4},{6,7},{7,6},{8,9},{9,8},{10,11... | collective-permute-start | bytes 442376 | tf_op jit(solution)/shard_map/ppermute | solution.py:140
  34.6 5.5 %collective-permute-start.16 = (bf16[576,128]{1,0:T(8,128)(2,1)S(1)}, bf16[576,128]{1,0:T(8,128)(2,1)S(1)}, u32[]{:S(2)}, u32[]{:S(2)}) collective-permute-start(bf16[576,128]{1,0:T(8,128)(2,1)S(1)} %collective-permute-done.6.refs_12_.refs_18_), channel_id=1, source_target_pairs={{0,4},{2,6},{4,0},{6,2},{8,12},{10,14},{12,8},{14,10},{1,5},{3,7},... | collective-permute-start | bytes 442376 | tf_op jit(solution)/shard_map/ppermute | solution.py:114
  37.2 8.8 %collective-permute-start.12 = (bf16[4,128,256]{2,1,0:T(8,128)(2,1)S(1)}, bf16[4,128,256]{2,1,0:T(8,128)(2,1)S(1)}, u32[]{:S(2)}, u32[]{:S(2)}) collective-permute-start(bf16[4,128,256]{2,1,0:T(8,128)(2,1)S(1)} %constant_dynamic-slice_fusion), channel_id=1, source_target_pairs={{0,16},{16,0},{1,17},{17,1},{2,18},{18,2},{3,19},{19,3},{4,20},{20... | collective-permute-start | bytes 786440 | tf_op jit(solution)/shard_map/ppermute | solution.py:156
  38.8 1.7 %collective-permute-start.13 = (bf16[576,128]{1,0:T(8,128)(2,1)S(1)}, bf16[576,128]{1,0:T(8,128)(2,1)S(1)}, u32[]{:S(2)}, u32[]{:S(2)}) collective-permute-start(bf16[576,128]{1,0:T(8,128)(2,1)S(1)} %collective-permute-done.refs_10_.refs_16_), channel_id=1, source_target_pairs={{0,1},{1,0},{2,3},{3,2},{4,5},{5,4},{6,7},{7,6},{8,9},{9,8},{10,11... | collective-permute-start | bytes 442376 | tf_op jit(solution)/shard_map/ppermute | solution.py:140
  40.0 2.6 %collective-permute-start.17 = (bf16[576,128]{1,0:T(8,128)(2,1)S(1)}, bf16[576,128]{1,0:T(8,128)(2,1)S(1)}, u32[]{:S(2)}, u32[]{:S(2)}) collective-permute-start(bf16[576,128]{1,0:T(8,128)(2,1)S(1)} %collective-permute-done.16.refs_16_.refs_22_), channel_id=1, source_target_pairs={{0,1},{1,0},{2,3},{3,2},{4,5},{5,4},{6,7},{7,6},{8,9},{9,8},{10,11... | collective-permute-start | bytes 442376 | tf_op jit(solution)/shard_map/ppermute | solution.py:140
  40.0 2.6 %collective-permute-start.14 = (bf16[576,128]{1,0:T(8,128)(2,1)S(1)}, bf16[576,128]{1,0:T(8,128)(2,1)S(1)}, u32[]{:S(2)}, u32[]{:S(2)}) collective-permute-start(bf16[576,128]{1,0:T(8,128)(2,1)S(1)} %collective-permute-done.6.refs_12_.refs_18_), channel_id=1, source_target_pairs={{0,1},{1,0},{2,3},{3,2},{4,5},{5,4},{6,7},{7,6},{8,9},{9,8},{10,11... | collective-permute-start | bytes 442376 | tf_op jit(solution)/shard_map/ppermute | solution.py:140
  40.5 2.2 %collective-permute-start.15 = (bf16[576,128]{1,0:T(8,128)(2,1)S(1)}, bf16[576,128]{1,0:T(8,128)(2,1)S(1)}, u32[]{:S(2)}, u32[]{:S(2)}) collective-permute-start(bf16[576,128]{1,0:T(8,128)(2,1)S(1)} %collective-permute-done.7.refs_14_.refs_20_), channel_id=1, source_target_pairs={{0,1},{1,0},{2,3},{3,2},{4,5},{5,4},{6,7},{7,6},{8,9},{9,8},{10,11... | collective-permute-start | bytes 442376 | tf_op jit(solution)/shard_map/ppermute | solution.py:140
  40.6 5.5 %collective-permute-start.11 = (bf16[128,256]{1,0:T(8,128)(2,1)S(1)}, bf16[128,256]{1,0:T(8,128)(2,1)S(1)}, u32[]{:S(2)}, u32[]{:S(2)}) collective-permute-start(bf16[128,256]{1,0:T(8,128)(2,1)S(1)} %bitcast.43), channel_id=1, source_target_pairs={{0,6},{2,4},{4,2},{6,0},{8,14},{10,12},{12,10},{14,8},{1,7},{3,5},... | collective-permute-start | bytes 196616 | tf_op jit(solution)/shard_map/ppermute | solution.py:114

commit v12 on v11

--- a/solution.py
+++ b/solution.py
@@ -14,7 +14,7 @@
 VD = 128
 HIDDEN = -1e30
 EARLY = ((4, 0, 4), (1, 0, 1), (2, 0, 2))
-LATE = ((3, 2, 1), (5, 4, 1), (6, 4, 2), (7, 5, 2))
+LATE = ((3, 2, 1), (5, 4, 1), (6, 4, 2), (7, 6, 1))
 
 
 def attend_kernel(slots, pair, which, *refs):

time: 61.5 us -> 62.3 us (1.013)
  starting transfers between devices: 21.4 us -> 23.9 us
  waiting for transfers between devices: 15.6 us -> 13.4 us
    ppermute x10, waiting for transfers between devices: 14.1 us -> 11.3 us  [swap(): return lax.ppermute(array, 'ctx', [(i, i ^ bit) for i in range(contexts)])]
    ppermute x10, starting transfers between devices: 15 us -> 16.9 us  [swap(): return lax.ppermute(array, 'ctx', [(i, i ^ bit) for i in range(contexts)])]
  transfers between devices with their start and end apart: 19 -> 19, of which waited for: 7 -> 6; matrix products, arithmetic and copies ran while one was open for 7% -> 7% of each run, Pallas kernels for 5% -> 5%
where the time goes in v12:
time: 62.3 us; the launch traced here: 62.1 us
  starting transfers between devices  23.9 us (38%)
  waiting for transfers between devices  13.4 us (22%)
  blocking collectives  12.1 us (19%)
  Pallas kernels  5.71 us (9%)
  local copies, waits for them, and re-layouts  4.92 us (8%)
  other arithmetic  1.19 us (2%)
  between operations  0.89 us (1%)
    ppermute x10, starting transfers between devices, swap(): return lax.ppermute(array, 'ctx', [(i, i ^ bit) for i in range(contexts)])  16.9 us
    all_to_all x1, blocking collectives, split_by_heads(): attended = lax.all_to_all(attended, 'ctx', 0, 0, tiled=True)  12.1 us
    ppermute x10, waiting for transfers between devices, swap(): return lax.ppermute(array, 'ctx', [(i, i ^ bit) for i in range(contexts)])  11.3 us
    pallas_call x2, Pallas kernels, attend(): pl.pallas_call(functools.partial(attend_kernel, contexts, pair, which), o...  5.71 us
    all_to_all x1, starting transfers between devices, split_by_heads(): packed = lax.all_to_all(packed, 'ctx', 0, 0, tiled=True)  3.82 us
    all_to_all x1, waiting for transfers between devices, split_by_heads(): packed = lax.all_to_all(packed, 'ctx', 0, 0, tiled=True)  1.82 us
    ppermute x1, starting transfers between devices, split_by_heads(): others = lax.ppermute(others, 'groups', [(0, 1), (1, 0)])  1.58 us
    ppermute x7, starting transfers between devices, trade(): return lax.ppermute(array, 'tp', [(0, 1), (1, 0)])  1.53 us
  transfers between devices with their start and end apart: 19, of which 6 were waited for; matrix products, arithmetic and copies ran while one was open for 7% of the time, Pallas kernels for 5%

profile of v12, /device:TPU:0, one launch (start us, length us, event | category | flops | bytes accessed | tf_op | source)
XLA Modules:
  0.0 62.1 jit_solution(11656863592539684833)
XLA Ops:
  0.0 0.9 %dynamic-slice_bitcast_fusion = bf16[576,128]{1,0:T(8,128)(2,1)S(1)} fusion(bf16[256,576]{0,1:T(8,128)(2,1)} %param.6, s32[]{:T(128)S(6)} %select_n.44), kind=kLoop, calls=%fused_computation.2 | loop fusion | bytes 294916 | tf_op jit(solution)/shard_map/dynamic_slice | solution.py:144
  0.9 4.1 %collective-permute-start = (bf16[576,128]{1,0:T(8,128)(2,1)S(1)}, bf16[576,128]{1,0:T(8,128)(2,1)S(1)}, u32[]{:S(2)}, u32[]{:S(2)}) collective-permute-start(bf16[576,128]{1,0:T(8,128)(2,1)S(1)} %dynamic-slice_bitcast_fusion), channel_id=1, source_target_pairs={{0,8},{2,10},{4,12},{6,14},{8,0},{10,2},{12,4},{14,6},{1,9},{3,11}... | collective-permute-start | bytes 442376 | tf_op jit(solution)/shard_map/ppermute | solution.py:114
  5.0 1.5 %collective-permute-start.1 = (bf16[576,128]{1,0:T(8,128)(2,1)S(1)}, bf16[576,128]{1,0:T(8,128)(2,1)S(1)}, u32[]{:S(2)}, u32[]{:S(2)}) collective-permute-start(bf16[576,128]{1,0:T(8,128)(2,1)S(1)} %dynamic-slice_bitcast_fusion), channel_id=1, source_target_pairs={{0,2},{2,0},{4,6},{6,4},{8,10},{10,8},{12,14},{14,12},{1,3},{3,1},... | collective-permute-start | bytes 442376 | tf_op jit(solution)/shard_map/ppermute | solution.py:114
  6.5 1.6 %collective-permute-start.2 = (bf16[576,128]{1,0:T(8,128)(2,1)S(1)}, bf16[576,128]{1,0:T(8,128)(2,1)S(1)}, u32[]{:S(2)}, u32[]{:S(2)}) collective-permute-start(bf16[576,128]{1,0:T(8,128)(2,1)S(1)} %dynamic-slice_bitcast_fusion), channel_id=1, source_target_pairs={{0,4},{2,6},{4,0},{6,2},{8,12},{10,14},{12,8},{14,10},{1,5},{3,7},... | collective-permute-start | bytes 442376 | tf_op jit(solution)/shard_map/ppermute | solution.py:114
  8.1 1.5 %reshape.48 = bf16[64,8,2,2,256]{4,3,2,1,0:T(2,128)(2,1)S(1)} reshape(bf16[64,32,256]{2,1,0:T(8,128)(2,1)} %param.7) | data formatting | bytes 2097152 | tf_op jit(solution)/shard_map/reshape | solution.py:117
  9.6 0.3 constant_dynamic-slice_fusion.1
  9.9 0.6 collective-permute-start.3
  10.5 0.5 collective-permute-start.4
  11.1 0.1 reshape.50
  11.2 0.2 copy.8
  11.4 0.3 broadcast_select_fusion
  11.7 0.1 slice_bitcast_fusion
  11.8 0.1 slice_bitcast_fusion.1
  11.9 0.4 constant_dynamic-slice_fusion.5
  12.3 0.1 reshape.52
  12.5 0.1 copy.9
  12.6 0.1 reshape.51
  12.7 0.2 copy.6
  12.8 0.9 %pad_maximum_fusion = bf16[8,176,256]{2,1,0:T(8,128)(2,1)} fusion(bf16[8,16,256]{2,1,0:T(8,128)(2,1)S(1)} %reshape.52, bf16[8,32,256]{2,1,0:T(8,128)(2,1)S(1)} %reshape.51, bf16[8,128,256]{2,1,0:T(8,128)(2,1)S(1)} %bitcast.40), kind=kLoop, calls=%fused_computation | loop fusion | flops 2162688 | bytes 1441792 | tf_op jit(solution)/shard_map/concatenate | solution.py:137
  13.7 0.5 collective-permute-done.3.refs_4_
  14.3 0.7 %collective-permute-done.4.refs_5_ = bf16[128,256]{1,0:T(8,128)(2,1)S(1)} collective-permute-done((bf16[128,256]{1,0:T(8,128)(2,1)S(1)}, bf16[128,256]{1,0:T(8,128)(2,1)S(1)}, u32[]{:S(2)}, u32[]{:S(2)}) %collective-permute-start.4) | collective-permute-done | bytes 65568 | tf_op jit(solution)/shard_map/ppermute | solution.py:114
  15.0 3.8 %all-to-all-start = ((bf16[8,176,256]{2,1,0:T(8,128)(2,1)}), bf16[8,176,256]{2,1,0:T(8,128)(2,1)S(1)}, u32[]{:S(2)}, u32[]{:S(2)}) async-start(bf16[8,176,256]{2,1,0:T(8,128)(2,1)} %pad_maximum_fusion), calls=%async_computation | async-start | bytes 1441792 | tf_op jit(solution)/shard_map/all_to_all | solution.py:149
  18.8 2.0 %collective-permute-start.5 = (bf16[576,128]{1,0:T(8,128)(2,1)S(1)}, bf16[576,128]{1,0:T(8,128)(2,1)S(1)}, u32[]{:S(2)}, u32[]{:S(2)}) collective-permute-start(bf16[576,128]{1,0:T(8,128)(2,1)S(1)} %collective-permute-done.2.refs_6_.refs_12_), channel_id=1, source_target_pairs={{0,2},{2,0},{4,6},{6,4},{8,10},{10,8},{12,14},{14,12},{1,3},{3,1},... | collective-permute-start | bytes 442376 | tf_op jit(solution)/shard_map/ppermute | solution.py:114
  20.8 0.0 collective-permute-start.6
  20.8 2.0 %collective-permute-start.7 = (bf16[576,128]{1,0:T(8,128)(2,1)S(1)}, bf16[576,128]{1,0:T(8,128)(2,1)S(1)}, u32[]{:S(2)}, u32[]{:S(2)}) collective-permute-start(bf16[576,128]{1,0:T(8,128)(2,1)S(1)} %collective-permute-done.refs_10_.refs_16_), channel_id=1, source_target_pairs={{0,4},{2,6},{4,0},{6,2},{8,12},{10,14},{12,8},{14,10},{1,5},{3,7},... | collective-permute-start | bytes 442376 | tf_op jit(solution)/shard_map/ppermute | solution.py:114
  22.8 0.0 collective-permute-start.9
  22.8 0.5 collective-permute-start.8
  23.3 8.9 %collective-permute-done.5.refs_8_.refs_14_ = bf16[576,128]{1,0:T(8,128)(2,1)S(1)} collective-permute-done((bf16[576,128]{1,0:T(8,128)(2,1)S(1)}, bf16[576,128]{1,0:T(8,128)(2,1)S(1)}, u32[]{:S(2)}, u32[]{:S(2)}) %collective-permute-start.5) | collective-permute-done | bytes 147488 | tf_op jit(solution)/shard_map/ppermute | solution.py:114
  32.3 0.0 collective-permute-start.10
  32.3 1.1 %collective-permute-done.7.refs_14_.refs_20_ = bf16[576,128]{1,0:T(8,128)(2,1)S(1)} collective-permute-done((bf16[576,128]{1,0:T(8,128)(2,1)S(1)}, bf16[576,128]{1,0:T(8,128)(2,1)S(1)}, u32[]{:S(2)}, u32[]{:S(2)}) %collective-permute-start.7) | collective-permute-done | bytes 147488 | tf_op jit(solution)/shard_map/ppermute | solution.py:114
  33.4 1.9 %collective-permute-start.16 = (bf16[576,128]{1,0:T(8,128)(2,1)S(1)}, bf16[576,128]{1,0:T(8,128)(2,1)S(1)}, u32[]{:S(2)}, u32[]{:S(2)}) collective-permute-start(bf16[576,128]{1,0:T(8,128)(2,1)S(1)} %collective-permute-done.7.refs_14_.refs_20_), channel_id=1, source_target_pairs={{0,2},{2,0},{4,6},{6,4},{8,10},{10,8},{12,14},{14,12},{1,3},{3,1},... | collective-permute-start | bytes 442376 | tf_op jit(solution)/shard_map/ppermute | solution.py:114
  35.3 0.0 collective-permute-done.6.refs_12_.refs_18_
  35.3 0.0 collective-permute-done.10.refs_9_.refs_15_
  35.3 1.8 %all-to-all-done.refs_2_ = bf16[8,176,256]{2,1,0:T(8,128)(2,1)S(1)} async-done(((bf16[8,176,256]{2,1,0:T(8,128)(2,1)}), bf16[8,176,256]{2,1,0:T(8,128)(2,1)S(1)}, u32[]{:S(2)}, u32[]{:S(2)}) %all-to-all-start) | async-done | bytes 720928 | tf_op jit(solution)/shard_map/all_to_all | solution.py:149
  37.2 1.6 %collective-permute-start.12 = (bf16[4,128,256]{2,1,0:T(8,128)(2,1)S(1)}, bf16[4,128,256]{2,1,0:T(8,128)(2,1)S(1)}, u32[]{:S(2)}, u32[]{:S(2)}) collective-permute-start(bf16[4,128,256]{2,1,0:T(8,128)(2,1)S(1)} %constant_dynamic-slice_fusion), channel_id=1, source_target_pairs={{0,16},{16,0},{1,17},{17,1},{2,18},{18,2},{3,19},{19,3},{4,20},{20... | collective-permute-start | bytes 786440 | tf_op jit(solution)/shard_map/ppermute | solution.py:156
  38.8 0.0 collective-permute-start.13
  38.8 0.0 collective-permute-done.16.refs_16_.refs_22_
  38.8 0.5 collective-permute-start.17
  39.3 0.0 collective-permute-start.14
  39.3 0.5 collective-permute-start.15
  39.8 0.3 collective-permute-done.13.refs_11_.refs_17_
  40.1 2.7 %collective-permute-start.11 = (bf16[128,256]{1,0:T(8,128)(2,1)S(1)}, bf16[128,256]{1,0:T(8,128)(2,1)S(1)}, u32[]{:S(2)}, u32[]{:S(2)}) collective-permute-start(bf16[128,256]{1,0:T(8,128)(2,1)S(1)} %bitcast.43), channel_id=1, source_target_pairs={{0,6},{2,4},{4,2},{6,0},{8,14},{10,12},{12,10},{14,8},{1,7},{3,5},... | collective-permute-start | bytes 196616 | tf_op jit(solution)/shard_map/ppermute | solution.py:114
  43.5 0.0 collective-permute-done.14.refs_13_.refs_19_
  43.5 0.0 collective-permute-done.15.refs_15_.refs_21_
  43.5 2.8 %attend_first.1.refs_8_ = bf16[128,256]{1,0:T(8,128)(2,1)S(1)} custom-call(s32[8]{0:T(128)S(1)} %copy-done.1, s32[1]{0:T(128)S(6)} %copy.15.refs_1_, bf16[8,176,256]{2,1,0:T(8,128)(2,1)S(1)} %all-to-all-done.refs_2_, bf16[576,256]{1,0:T(8,128)(2,1)S(1)} %bitcast.36, bf16[576,128]{1,0:T(8,128)(2,1)S(1)} %collective-permute-done.1.refs_4_.refs_10_, ...), custom_call_target="tpu_custom_call" | custom-call | flops 1048576 | bytes 1048576 | tf_op jit(solution)/shard_map/attend_first/pallas_call | solution.py:168
  46.4 2.9 %attend_second.1 = bf16[128,512]{1,0:T(8,128)(2,1)S(1)} custom-call(s32[8]{0:T(128)S(1)} %copy-done.1, s32[1]{0:T(128)S(6)} %copy.15.refs_1_, bf16[8,176,256]{2,1,0:T(8,128)(2,1)S(1)} %all-to-all-done.refs_2_, bf16[128,256]{1,0:T(8,128)(2,1)S(1)} %bitcast.39, bf16[128,256]{1,0:T(8,128)(2,1)S(1)} %collective-permute-done.3.refs_4_, ...), custom_call_target="tpu_custom_call" | custom-call | flops 1048576 | bytes 1048576 | tf_op jit(solution)/shard_map/attend_second/pallas_call | solution.py:168
  49.3 12.1 %all_to_all.10 = bf16[8,16,512]{2,1,0:T(8,128)(2,1)S(1)} all-to-all(bf16[8,16,512]{2,1,0:T(8,128)(2,1)S(1)} %bitcast.38), channel_id=1, replica_groups=mesh['groups'=2,'ctx'=8,'tp'=2] {'ctx'}, dimensions={0} | all-to-all | bytes 262144 | tf_op jit(solution)/shard_map/all_to_all | solution.py:182
  61.4 0.7 %copy.14 = bf16[8,16,4,128]{3,2,0,1:T(4,128)(2,1)} copy(bf16[8,16,4,128]{3,2,1,0:T(4,128)(2,1)S(1)} %reshape.62) | data formatting | bytes 262144 | tf_op jit(solution)/shard_map/reshape | solution.py:183
  (20 shorter events, 0.1 us)
Async XLA Ops:
  0.9 14.0 %collective-permute-start = (bf16[576,128]{1,0:T(8,128)(2,1)S(1)}, bf16[576,128]{1,0:T(8,128)(2,1)S(1)}, u32[]{:S(2)}, u32[]{:S(2)}) collective-permute-start(bf16[576,128]{1,0:T(8,128)(2,1)S(1)} %dynamic-slice_bitcast_fusion), channel_id=1, source_target_pairs={{0,8},{2,10},{4,12},{6,14},{8,0},{10,2},{12,4},{14,6},{1,9},{3,11}... | collective-permute-start | bytes 442376 | tf_op jit(solution)/shard_map/ppermute | solution.py:114
  5.0 9.9 %collective-permute-start.1 = (bf16[576,128]{1,0:T(8,128)(2,1)S(1)}, bf16[576,128]{1,0:T(8,128)(2,1)S(1)}, u32[]{:S(2)}, u32[]{:S(2)}) collective-permute-start(bf16[576,128]{1,0:T(8,128)(2,1)S(1)} %dynamic-slice_bitcast_fusion), channel_id=1, source_target_pairs={{0,2},{2,0},{4,6},{6,4},{8,10},{10,8},{12,14},{14,12},{1,3},{3,1},... | collective-permute-start | bytes 442376 | tf_op jit(solution)/shard_map/ppermute | solution.py:114
  6.5 8.4 %collective-permute-start.2 = (bf16[576,128]{1,0:T(8,128)(2,1)S(1)}, bf16[576,128]{1,0:T(8,128)(2,1)S(1)}, u32[]{:S(2)}, u32[]{:S(2)}) collective-permute-start(bf16[576,128]{1,0:T(8,128)(2,1)S(1)} %dynamic-slice_bitcast_fusion), channel_id=1, source_target_pairs={{0,4},{2,6},{4,0},{6,2},{8,12},{10,14},{12,8},{14,10},{1,5},{3,7},... | collective-permute-start | bytes 442376 | tf_op jit(solution)/shard_map/ppermute | solution.py:114
  8.1 3.0 %copy-start.2 = (bf16[16,32,192]{2,1,0:T(8,128)(2,1)S(1)}, bf16[16,32,192]{2,1,0:T(8,128)(2,1)}, u32[]{:S(2)}) copy-start(bf16[16,32,192]{2,1,0:T(8,128)(2,1)} %param.5) | copy-start | bytes 589828
  9.9 4.3 %collective-permute-start.3 = (bf16[128,256]{1,0:T(8,128)(2,1)S(1)}, bf16[128,256]{1,0:T(8,128)(2,1)S(1)}, u32[]{:S(2)}, u32[]{:S(2)}) collective-permute-start(bf16[128,256]{1,0:T(8,128)(2,1)S(1)} %bitcast.41), channel_id=1, source_target_pairs={{0,2},{2,0},{4,6},{6,4},{8,10},{10,8},{12,14},{14,12},{1,3},{3,1},... | collective-permute-start | bytes 196616 | tf_op jit(solution)/shard_map/ppermute | solution.py:114
  10.5 4.4 %collective-permute-start.4 = (bf16[128,256]{1,0:T(8,128)(2,1)S(1)}, bf16[128,256]{1,0:T(8,128)(2,1)S(1)}, u32[]{:S(2)}, u32[]{:S(2)}) collective-permute-start(bf16[128,256]{1,0:T(8,128)(2,1)S(1)} %bitcast.42), channel_id=1, source_target_pairs={{0,4},{2,6},{4,0},{6,2},{8,12},{10,14},{12,8},{14,10},{1,5},{3,7},... | collective-permute-start | bytes 196616 | tf_op jit(solution)/shard_map/ppermute | solution.py:114
  13.7 29.8 %copy-start = (bf16[256,576]{0,1:T(8,128)(2,1)S(1)}, bf16[256,576]{0,1:T(8,128)(2,1)}, u32[]{:S(2)}) copy-start(bf16[256,576]{0,1:T(8,128)(2,1)} %param.6) | copy-start | bytes 884740
  13.7 29.8 %copy-start.1 = (s32[8]{0:T(128)S(1)}, s32[8]{0:T(128)}, u32[]{:S(2)}) copy-start(s32[8]{0:T(128)} %refs_0_.3) | copy-start | bytes 100
  15.0 22.2 %all-to-all-start = ((bf16[8,176,256]{2,1,0:T(8,128)(2,1)}), bf16[8,176,256]{2,1,0:T(8,128)(2,1)S(1)}, u32[]{:S(2)}, u32[]{:S(2)}) async-start(bf16[8,176,256]{2,1,0:T(8,128)(2,1)} %pad_maximum_fusion), calls=%async_computation | async-start | bytes 1441792 | tf_op jit(solution)/shard_map/all_to_all | solution.py:149
  18.8 13.5 %collective-permute-start.5 = (bf16[576,128]{1,0:T(8,128)(2,1)S(1)}, bf16[576,128]{1,0:T(8,128)(2,1)S(1)}, u32[]{:S(2)}, u32[]{:S(2)}) collective-permute-start(bf16[576,128]{1,0:T(8,128)(2,1)S(1)} %collective-permute-done.2.refs_6_.refs_12_), channel_id=1, source_target_pairs={{0,2},{2,0},{4,6},{6,4},{8,10},{10,8},{12,14},{14,12},{1,3},{3,1},... | collective-permute-start | bytes 442376 | tf_op jit(solution)/shard_map/ppermute | solution.py:114
  20.8 14.5 %collective-permute-start.6 = (bf16[576,128]{1,0:T(8,128)(2,1)S(1)}, bf16[576,128]{1,0:T(8,128)(2,1)S(1)}, u32[]{:S(2)}, u32[]{:S(2)}) collective-permute-start(bf16[576,128]{1,0:T(8,128)(2,1)S(1)} %collective-permute-done.refs_10_.refs_16_), channel_id=1, source_target_pairs={{0,2},{2,0},{4,6},{6,4},{8,10},{10,8},{12,14},{14,12},{1,3},{3,1},... | collective-permute-start | bytes 442376 | tf_op jit(solution)/shard_map/ppermute | solution.py:114
  20.8 12.6 %collective-permute-start.7 = (bf16[576,128]{1,0:T(8,128)(2,1)S(1)}, bf16[576,128]{1,0:T(8,128)(2,1)S(1)}, u32[]{:S(2)}, u32[]{:S(2)}) collective-permute-start(bf16[576,128]{1,0:T(8,128)(2,1)S(1)} %collective-permute-done.refs_10_.refs_16_), channel_id=1, source_target_pairs={{0,4},{2,6},{4,0},{6,2},{8,12},{10,14},{12,8},{14,10},{1,5},{3,7},... | collective-permute-start | bytes 442376 | tf_op jit(solution)/shard_map/ppermute | solution.py:114
  22.8 12.5 %collective-permute-start.9 = (bf16[576,128]{1,0:T(8,128)(2,1)S(1)}, bf16[576,128]{1,0:T(8,128)(2,1)S(1)}, u32[]{:S(2)}, u32[]{:S(2)}) collective-permute-start(bf16[576,128]{1,0:T(8,128)(2,1)S(1)} %collective-permute-done.2.refs_6_.refs_12_), channel_id=1, source_target_pairs={{0,1},{1,0},{2,3},{3,2},{4,5},{5,4},{6,7},{7,6},{8,9},{9,8},{10,11... | collective-permute-start | bytes 442376 | tf_op jit(solution)/shard_map/ppermute | solution.py:140
  22.8 12.5 %collective-permute-start.8 = (bf16[576,128]{1,0:T(8,128)(2,1)S(1)}, bf16[576,128]{1,0:T(8,128)(2,1)S(1)}, u32[]{:S(2)}, u32[]{:S(2)}) collective-permute-start(bf16[576,128]{1,0:T(8,128)(2,1)S(1)} %collective-permute-done.1.refs_4_.refs_10_), channel_id=1, source_target_pairs={{0,1},{1,0},{2,3},{3,2},{4,5},{5,4},{6,7},{7,6},{8,9},{9,8},{10,11... | collective-permute-start | bytes 442376 | tf_op jit(solution)/shard_map/ppermute | solution.py:140
  32.3 3.1 %collective-permute-start.10 = (bf16[576,128]{1,0:T(8,128)(2,1)S(1)}, bf16[576,128]{1,0:T(8,128)(2,1)S(1)}, u32[]{:S(2)}, u32[]{:S(2)}) collective-permute-start(bf16[576,128]{1,0:T(8,128)(2,1)S(1)} %collective-permute-done.5.refs_8_.refs_14_), channel_id=1, source_target_pairs={{0,1},{1,0},{2,3},{3,2},{4,5},{5,4},{6,7},{7,6},{8,9},{9,8},{10,11... | collective-permute-start | bytes 442376 | tf_op jit(solution)/shard_map/ppermute | solution.py:140
  33.4 5.4 %collective-permute-start.16 = (bf16[576,128]{1,0:T(8,128)(2,1)S(1)}, bf16[576,128]{1,0:T(8,128)(2,1)S(1)}, u32[]{:S(2)}, u32[]{:S(2)}) collective-permute-start(bf16[576,128]{1,0:T(8,128)(2,1)S(1)} %collective-permute-done.7.refs_14_.refs_20_), channel_id=1, source_target_pairs={{0,2},{2,0},{4,6},{6,4},{8,10},{10,8},{12,14},{14,12},{1,3},{3,1},... | collective-permute-start | bytes 442376 | tf_op jit(solution)/shard_map/ppermute | solution.py:114
  37.2 9.2 %collective-permute-start.12 = (bf16[4,128,256]{2,1,0:T(8,128)(2,1)S(1)}, bf16[4,128,256]{2,1,0:T(8,128)(2,1)S(1)}, u32[]{:S(2)}, u32[]{:S(2)}) collective-permute-start(bf16[4,128,256]{2,1,0:T(8,128)(2,1)S(1)} %constant_dynamic-slice_fusion), channel_id=1, source_target_pairs={{0,16},{16,0},{1,17},{17,1},{2,18},{18,2},{3,19},{19,3},{4,20},{20... | collective-permute-start | bytes 786440 | tf_op jit(solution)/shard_map/ppermute | solution.py:156
  38.8 1.4 %collective-permute-start.13 = (bf16[576,128]{1,0:T(8,128)(2,1)S(1)}, bf16[576,128]{1,0:T(8,128)(2,1)S(1)}, u32[]{:S(2)}, u32[]{:S(2)}) collective-permute-start(bf16[576,128]{1,0:T(8,128)(2,1)S(1)} %collective-permute-done.refs_10_.refs_16_), channel_id=1, source_target_pairs={{0,1},{1,0},{2,3},{3,2},{4,5},{5,4},{6,7},{7,6},{8,9},{9,8},{10,11... | collective-permute-start | bytes 442376 | tf_op jit(solution)/shard_map/ppermute | solution.py:140
  38.8 4.7 %collective-permute-start.17 = (bf16[576,128]{1,0:T(8,128)(2,1)S(1)}, bf16[576,128]{1,0:T(8,128)(2,1)S(1)}, u32[]{:S(2)}, u32[]{:S(2)}) collective-permute-start(bf16[576,128]{1,0:T(8,128)(2,1)S(1)} %collective-permute-done.16.refs_16_.refs_22_), channel_id=1, source_target_pairs={{0,1},{1,0},{2,3},{3,2},{4,5},{5,4},{6,7},{7,6},{8,9},{9,8},{10,11... | collective-permute-start | bytes 442376 | tf_op jit(solution)/shard_map/ppermute | solution.py:140
  39.3 4.2 %collective-permute-start.14 = (bf16[576,128]{1,0:T(8,128)(2,1)S(1)}, bf16[576,128]{1,0:T(8,128)(2,1)S(1)}, u32[]{:S(2)}, u32[]{:S(2)}) collective-permute-start(bf16[576,128]{1,0:T(8,128)(2,1)S(1)} %collective-permute-done.6.refs_12_.refs_18_), channel_id=1, source_target_pairs={{0,1},{1,0},{2,3},{3,2},{4,5},{5,4},{6,7},{7,6},{8,9},{9,8},{10,11... | collective-permute-start | bytes 442376 | tf_op jit(solution)/shard_map/ppermute | solution.py:140
  39.3 4.2 %collective-permute-start.15 = (bf16[576,128]{1,0:T(8,128)(2,1)S(1)}, bf16[576,128]{1,0:T(8,128)(2,1)S(1)}, u32[]{:S(2)}, u32[]{:S(2)}) collective-permute-start(bf16[576,128]{1,0:T(8,128)(2,1)S(1)} %collective-permute-done.7.refs_14_.refs_20_), channel_id=1, source_target_pairs={{0,1},{1,0},{2,3},{3,2},{4,5},{5,4},{6,7},{7,6},{8,9},{9,8},{10,11... | collective-permute-start | bytes 442376 | tf_op jit(solution)/shard_map/ppermute | solution.py:140
  40.1 6.2 %collective-permute-start.11 = (bf16[128,256]{1,0:T(8,128)(2,1)S(1)}, bf16[128,256]{1,0:T(8,128)(2,1)S(1)}, u32[]{:S(2)}, u32[]{:S(2)}) collective-permute-start(bf16[128,256]{1,0:T(8,128)(2,1)S(1)} %bitcast.43), channel_id=1, source_target_pairs={{0,6},{2,4},{4,2},{6,0},{8,14},{10,12},{12,10},{14,8},{1,7},{3,5},... | collective-permute-start | bytes 196616 | tf_op jit(solution)/shard_map/ppermute | solution.py:114
